TPU v7x, 32 devices: a whole 2x2x4 slice. The times are simulated.
32 devices in a mesh: groups: 2 (over y), mx: 4 (over z), my: 4 (over x, core).
Axes of the slice: x: 2, y: 2, z: 4, core: 2. Of those that a mesh axis runs over, the one named last changes fastest.
Arguments:
- tokens: bfloat16 [2048, 8192], P(('groups', 'mx'), 'my'), parts along dimension 0, may hold values from -6 to 6
- w_gate: bfloat16 [8192, 26624], P('my', 'mx'), may hold values from -0.0625 to 0.0625
- w_up: bfloat16 [8192, 26624], P('my', 'mx'), may hold values from -0.0625 to 0.0625
- adapter_in: bfloat16 [8, 8192, 32], P(None, 'my'), may hold values from -0.0625 to 0.0625
- adapter_out: bfloat16 [8, 2, 16, 26624], P(None, None, None, 'mx'), may hold values from -0.75 to 0.75
- magnitude: float32 [8, 2, 26624], P(None, None, 'mx'), may hold values from 0.5 to 2
- partial_norms: float32 [4, 8, 2, 26624], P('my', None, None, 'mx'), may hold values from 0.06 to 2.8125, as said below
- block_tenant: int32 [16], P('groups'), parts along dimension 0, may hold values from 0 to 7
- block_rows: int32 [16], P('groups'), parts along dimension 0, may hold values from 1 to 128, 768 in all
Outputs:
- hidden: bfloat16 [2048, 26624], P('groups', ('mx', 'my')), parts along dimension 0
There are 2 independent parts, one for each index of `groups`. A program takes and returns all parts, laid end to end along the dimension named above; an argument that names none is the same for every part. Nothing has to cross between parts.
Inputs may be any that keep to these rules, and one draw needn't show every extreme that they name: `partial_norms`: positive.
All inputs are finite; a program needn't handle non-finite values.
Results may differ from a plain program's by a relative error of at most 0.0038.
Values may be sent and summed in bfloat16 or wider, within the bound.
No kernel may reach another device: no remote copies, remote signals or barrier semaphores. Data moves between devices by JAX's collectives and lax.ppermute only.
A program may use at most 384 MiB of HBM per device.

v0:
```python
import math

import jax
import jax.numpy as jnp
from jax import lax
from jax.sharding import PartitionSpec as P

RANK = 16
BLOCK_ROWS = 128


def adapter_low(rows_piece, aligned_row_total, adapter_in, block_tenant):
    row_count = rows_piece.shape[0]
    seg_rows = math.gcd(math.gcd(row_count, BLOCK_ROWS), aligned_row_total)
    seg_count = row_count // seg_rows
    seg_block = jnp.arange(seg_count, dtype=jnp.int32) * seg_rows // BLOCK_ROWS
    tenant_tables = adapter_in[block_tenant[seg_block]]
    grouped = rows_piece.reshape(seg_count, seg_rows, rows_piece.shape[1])
    low_terms = jnp.einsum(
        "skd,sdr->skr", grouped, tenant_tables, preferred_element_type=jnp.float32
    )
    return low_terms.reshape(row_count, tenant_tables.shape[2])


def finish(
    summed,
    reduced_rank_factor,
    norm_total,
    mag_cols,
    adapter_cols,
    first_row,
    block_tenant,
    block_rows,
):
    row_count = summed.shape[0]
    col_count = summed.shape[2]
    seg_rows = math.gcd(row_count, BLOCK_ROWS)
    seg_count = row_count // seg_rows
    seg_block = (first_row + jnp.arange(seg_count, dtype=jnp.int32) * seg_rows) // BLOCK_ROWS
    tenants = block_tenant[seg_block]
    col_scale = mag_cols * lax.rsqrt(norm_total)
    seg_scale = col_scale[tenants]
    seg_tables = adapter_cols[tenants]
    low_pair = reduced_rank_factor.reshape(seg_count, seg_rows, 2, RANK)
    adapted = jnp.einsum(
        "skpr,sprc->skpc", low_pair, seg_tables, preferred_element_type=jnp.float32
    )
    pre_act = (summed.reshape(seg_count, seg_rows, 2, col_count) + adapted) * seg_scale[:, None]
    hidden = jax.nn.silu(pre_act[:, :, 0]) * pre_act[:, :, 1]
    offsets = (first_row + jnp.arange(row_count, dtype=jnp.int32)).reshape(
        seg_count, seg_rows
    ) % BLOCK_ROWS
    live_mask = offsets < block_rows[seg_block][:, None]
    hidden = jnp.where(live_mask[:, :, None], hidden, jnp.zeros_like(hidden))
    return hidden.reshape(row_count, col_count).astype(jnp.bfloat16)


def on_device(
    tokens,
    w_gate,
    w_up,
    adapter_in,
    adapter_out,
    magnitude,
    partial_norms,
    block_tenant,
    block_rows,
):
    local_rows = tokens.shape[0]
    col_local = w_gate.shape[1]
    my_count = lax.axis_size("my")
    device_position = lax.axis_index("my")
    rows_piece = lax.all_gather(tokens, "mx", axis=0, tiled=True)
    gate_part = jnp.dot(rows_piece, w_gate, preferred_element_type=jnp.float32)
    up_part = jnp.dot(rows_piece, w_up, preferred_element_type=jnp.float32)
    main_part = jnp.stack((gate_part, up_part), axis=1)
    low_terms = adapter_low(rows_piece, local_rows, adapter_in, block_tenant)
    reduced_rank_factor = lax.psum(low_terms, "my").astype(jnp.bfloat16)
    summed = lax.psum_scatter(main_part, "my", scatter_dimension=2, tiled=True)
    norm_total = lax.psum_scatter(partial_norms[0], "my", scatter_dimension=2, tiled=True)
    narrow = col_local // my_count
    mag_cols = lax.dynamic_slice_in_dim(magnitude, device_position * narrow, narrow, 2)
    adapter_cols = lax.dynamic_slice_in_dim(adapter_out, device_position * narrow, narrow, 3)
    return finish(
        summed, reduced_rank_factor, norm_total, mag_cols, adapter_cols, 0, block_tenant, block_rows
    )


def solution(mesh):
    return jax.shard_map(
        on_device,
        mesh=mesh,
        in_specs=(
            P(("groups", "mx"), "my"),
            P("my", "mx"),
            P("my", "mx"),
            P(None, "my", None),
            P(None, None, None, "mx"),
            P(None, None, "mx"),
            P("my", None, None, "mx"),
            P("groups"),
            P("groups"),
        ),
        out_specs=P("groups", ("mx", "my")),
        check_vma=False,
    )
```

profile of v0, /device:TPU:8, one launch (start us, length us, event | category | flops | bytes accessed | tf_op | source)
XLA Modules:
  0.0 613.4 jit_solution(2463018174120555449)
XLA Ops:
  7.4 0.7 all-gather.2.cloned.1.call-update
  8.1 14.3 %copy.17 = f32[8,2,6656]{1,0,2:T(8,128)} copy(f32[8,2,6656]{2,1,0:T(2,128)} %bitcast.69) | data formatting | bytes 851968
  22.5 17.7 %reshape.187 = f32[6656,16]{1,0:T(8,128)} reshape(f32[6656,8,2]{2,1,0:T(8,128)} %bitcast.64) | data formatting | bytes 851968
  40.2 48.9 %all-gather.2.cloned.1.call-done = bf16[1024,2048]{1,0:T(8,128)(2,1)} async-done(((bf16[256,2048]{1,0:T(8,128)(2,1)}), bf16[1024,2048]{1,0:T(8,128)(2,1)}) %all-gather.2.cloned.1.call-update) | async-done | bytes 4194320 | tf_op jit(solution)/shard_map/all_gather | solution.py:73
  89.2 40.8 %convolution_bitcast_fusion = f32[1024,1,6656]{2,0,1:T(8,128)} fusion(bf16[1024,2048]{1,0:T(8,128)(2,1)} %all-gather.2.cloned.1.call-done, bf16[2048,6656]{1,0:T(8,128)(2,1)} %param.11), kind=kOutput, calls=%fused_computation.6 | convolution fusion | flops 27917287424 | bytes 58720256 | tf_op jit(solution)/shard_map/dot_general | solution.py:75
  129.9 36.7 %convolution_bitcast_fusion.1 = f32[1024,1,6656]{2,0,1:T(8,128)} fusion(bf16[1024,2048]{1,0:T(8,128)(2,1)S(1)} %copy-done.3, bf16[2048,6656]{1,0:T(8,128)(2,1)} %param.10), kind=kOutput, calls=%fused_computation.7 | convolution fusion | flops 27917287424 | bytes 58720256 | tf_op jit(solution)/shard_map/dot_general | solution.py:74
  166.6 37.1 %pad_maximum_fusion = f32[1024,2,6656]{2,0,1:T(8,128)} fusion(f32[1024,1,6656]{2,0,1:T(8,128)} %convolution_bitcast_fusion, f32[1024,1,6656]{2,0,1:T(8,128)} %convolution_bitcast_fusion.1), kind=kLoop, calls=%fused_computation.5 | loop fusion | flops 13631488 | bytes 109051904 | tf_op jit(solution)/shard_map/stack | solution.py:76
  203.9 0.6 copy-done.1
  204.5 0.6 gather_fusion.1
  205.1 0.6 gather_fusion
  205.8 1.0 constant_dynamic-slice_fusion
  206.8 2.7 gather_fusion.2
  209.5 2.9 gather_fusion.3
  212.5 5.7 reshape.188
  218.2 6.5 %copy.18 = f32[8,2,1664]{2,1,0:T(2,128)} copy(f32[8,2,1664]{1,0,2:T(8,128)} %bitcast.65) | data formatting | bytes 212992
  224.7 1.1 rsqrt_multiply_fusion
  225.7 1.3 gather_fusion.4
  227.0 5.3 convolution_bitcast_fusion.2
  232.4 13.7 %all-reduce.1 = bf16[1024,32]{0,1:T(8,128)(2,1)} all-reduce(f32[1024,32]{0,1:T(8,128)S(1)} %bitcast.68), channel_id=1, replica_groups=mesh['groups'=2,'mx'=4,'my'=4] {'my'}, use_global_device_ids=true, to_apply=%region_1.2 | all-reduce | flops 32768 | bytes 196608 | tf_op jit(solution)/shard_map/psum | solution.py:78
  246.1 0.9 copy.20
  247.0 328.4 %reduce-scatter.5.cloned.1.call-done = f32[1024,2,1664]{2,0,1:T(8,128)} async-done(((f32[1024,2,6656]{2,0,1:T(8,128)}), f32[1024,2,1664]{2,0,1:T(8,128)}) %reduce-scatter.5.cloned.1.call-update) | async-done | bytes 13631504 | tf_op jit(solution)/shard_map/reduce_scatter | solution.py:79
  575.4 11.9 %fusion = f32[8,128,2,1664]{3,1,2,0:T(8,128)} fusion(f32[8,128,2,1664]{3,1,0,2:T(8,128)} %bitcast.66, f32[8,2,1664]{2,1,0:T(2,128)} %gather_fusion.4, bf16[8,2,16,1664]{3,2,1,0:T(8,128)(2,1)} %gather_fusion.2, bf16[8,128,2,16]{1,0,3,2:T(8,128)(2,1)S(1)} %bitcast.70), kind=kOutput, calls=%fused_computation.9 | convolution fusion | flops 115867648 | bytes 28286976 | tf_op jit(solution)/shard_map/skpr,sprc->skpc/dot_general | solution.py:45
  587.3 11.1 %fusion.11 = (f32[8,128,1,1664]{3,1,2,0:T(8,128)}, f32[8,128,1,1664]{3,1,2,0:T(8,128)}) fusion(f32[8,128,2,1664]{3,1,2,0:T(8,128)} %fusion), kind=kLoop, calls=%fused_computation.39 | loop fusion | bytes 27262976 | tf_op jit(solution)/shard_map/slice | solution.py:49
  598.4 7.5 %fusion.2 = bf16[1024,1664]{1,0:T(8,128)(2,1)} fusion(f32[8,128,1,1664]{3,1,2,0:T(8,128)} %get-tuple-element.6, f32[8,128,1,1664]{3,1,2,0:T(8,128)} %get-tuple-element.5, pred[1024]{0:T(1024)(128)(4,1)S(1)} %fusion.8), kind=kLoop, calls=%fused_computation.12 | loop fusion | flops 11927552 | bytes 17040384 | tf_op jit(solution)/shard_map/convert_element_type | solution.py:55
  (19 shorter events, 0.3 us)
Async XLA Ops:
  7.4 198.4 %copy-start = (bf16[8,2,16,6656]{3,2,1,0:T(8,128)(2,1)S(1)}, bf16[8,2,16,6656]{3,2,1,0:T(8,128)(2,1)}, u32[]{:S(2)}) copy-start(bf16[8,2,16,6656]{3,2,1,0:T(8,128)(2,1)} %param.13) | copy-start | bytes 10223620
  7.4 81.8 %all-gather.2.cloned.1.call-start = ((), (), s32[]{:S(2)}) async-start(), calls=%async_computation.2 | async-start | bytes 5242880 | tf_op jit(solution)/shard_map/all_gather | solution.py:73
  8.1 204.4 %reduce-scatter.7.cloned.1.call-start = ((), (), s32[]{:S(2)}) async-start(), calls=%async_computation.4 | async-start | bytes 4259840
  40.2 535.2 %reduce-scatter.5.cloned.1.call-start = ((), (), s32[]{:S(2)}) async-start(), calls=%async_computation.3 | async-start | bytes 68157440 | tf_op jit(solution)/shard_map/reduce_scatter | solution.py:79
  89.2 40.8 %copy-start.3 = (bf16[1024,2048]{1,0:T(8,128)(2,1)S(1)}, bf16[1024,2048]{1,0:T(8,128)(2,1)}, u32[]{:S(2)}) copy-start(bf16[1024,2048]{1,0:T(8,128)(2,1)} %all-gather.2.cloned.1.call-done) | copy-start | bytes 12582916
  203.8 0.7 copy-start.1
  203.8 1.3 copy-start.2
Sparse Core Ops, SparseCore 0:
  9.8 79.2 all-gather.1
Sparse Core Ops, SparseCore 1:
  40.3 40.7 reduce-scatter.6
  203.9 371.4 reduce-scatter.4
where the time goes:
time: 616 us; the launch traced here: 613 us
  waiting for transfers between devices  378 us (61%)
  matrix products  94.7 us (15%)
  local copies, waits for them, and re-layouts  66.1 us (11%)
  other arithmetic  45.9 us (7%)
  between operations  14.9 us (2%)
  blocking collectives  13.7 us (2%)
    reduce_scatter x1, waiting for transfers between devices, on_device(): summed = lax.psum_scatter(main_part, 'my', scatter_dimension=2, tiled=True)  328 us
    all_gather x1, waiting for transfers between devices, on_device(): rows_piece = lax.all_gather(tokens, 'mx', axis=0, tiled=True)  48.9 us
    unnamed x13, local copies, waits for them, and re-layouts  45.7 us
    dot_general x1, matrix products, on_device(): up_part = jnp.dot(rows_piece, w_up, preferred_element_type=jnp.float32)  40.8 us
    another operation x1, other arithmetic, on_device(): main_part = jnp.stack((gate_part, up_part), axis=1)  37.1 us
    dot_general x1, matrix products, on_device(): gate_part = jnp.dot(rows_piece, w_gate, preferred_element_type=jnp.float32)  36.7 us
    psum x1, blocking collectives, on_device(): reduced_rank_factor = lax.psum(low_terms, 'my').astype(jnp.bfloat16)  13.7 us
  transfers between devices with their start and end apart: 3, of which 2 were waited for; matrix products, arithmetic and copies ran while one was open for 29% of the time, Pallas kernels for 0%

commit v1 on v0

--- a/solution.py
+++ b/solution.py
@@ -1,12 +1,376 @@
+import functools
 import math
 
 import jax
 import jax.numpy as jnp
 from jax import lax
+from jax.experimental import pallas as pl
+from jax.experimental.pallas import tpu as pltpu
 from jax.sharding import PartitionSpec as P
 
 RANK = 16
 BLOCK_ROWS = 128
+LIVE_ROWS = 768
+VMEM_LIMIT = 56 * 1024 * 1024
+
+SLOTS = (
+    (0, 0), (0, 1),
+    (-1, 0), (1, 0), (-1, 1), (1, 1),
+    (-2, 0), (2, 0), (-2, 1), (2, 1),
+    (-3, 0), (3, 0), (-3, 1), (3, 1),
+)
+CHUNKS = ((0, 128, 4), (128, 256, 8), (384, 384, 14))
+
+
+def slot_table(ids, rows, tenants, mx_count):
+    place = ids[0]
+    start = jnp.int32(0)
+    table = []
+    for distance, half in SLOTS:
+        source = place + distance
+        valid = (source >= 0) & (source < mx_count)
+        block = jnp.clip(source, 0, mx_count - 1) * 2 + half
+        count = jnp.where(valid, rows[block], 0)
+        table.append((start, count, tenants[block], jnp.where(valid, block, -1)))
+        start = start + count
+    return table
+
+
+def row_tenants(table, first, shape):
+    row = lax.broadcasted_iota(jnp.int32, shape, 0) + first
+    tenant = jnp.full(shape, -1, jnp.int32)
+    for start, count, owner, _ in table:
+        tenant = jnp.where((row >= start) & (row < start + count), owner, tenant)
+    return tenant
+
+
+def pack_kernel(mx_count, first, rows_out, slots, ids, rows, tenants, *refs):
+    token_refs = refs[:slots]
+    down_ref = refs[slots]
+    x_ref, low_ref, acc = refs[-3:]
+    table = slot_table(ids, rows, tenants, mx_count)
+    acc[...] = jnp.zeros_like(acc)
+    for slot in range(slots):
+        start, count, _, _ = table[slot]
+
+        @pl.when((count > 0) & (start < first + rows_out) & (start + count > first))
+        def _():
+            target = lax.broadcasted_iota(jnp.int32, (rows_out, BLOCK_ROWS), 0) + first
+            position = lax.broadcasted_iota(jnp.int32, (rows_out, BLOCK_ROWS), 1)
+            chosen = (position < count) & (target == position + start)
+            acc[...] += jnp.dot(
+                chosen.astype(jnp.bfloat16), token_refs[slot][...], preferred_element_type=jnp.float32
+            )
+
+    x = acc[...].astype(jnp.bfloat16)
+    x_ref[...] = x
+    for tile in range(rows_out // BLOCK_ROWS):
+        low = jnp.dot(
+            x[tile * BLOCK_ROWS:(tile + 1) * BLOCK_ROWS], down_ref[...], preferred_element_type=jnp.float32
+        )
+        tenant = row_tenants(table, first + tile * BLOCK_ROWS, low.shape)
+        lane = lax.broadcasted_iota(jnp.int32, low.shape, 1)
+        low = jnp.where(lane // (2 * RANK) == tenant, low, 0.0)
+        low = low[:, :128] + low[:, 128:]
+        low = low + pltpu.roll(low, 64, 1)
+        low = low + pltpu.roll(low, 32, 1)
+        group = lax.broadcasted_iota(jnp.int32, (32, 128), 1) // 32
+        packed = jnp.where(group == 0, low[0:32], 0.0)
+        for part in range(1, 4):
+            packed = jnp.where(group == part, low[part * 32:(part + 1) * 32], packed)
+        low_ref[tile * 32:(tile + 1) * 32, :] = packed
+
+
+def pack_rows(mx_count, first, rows_out, scalars, blocks, down, after):
+    width = blocks[0].shape[1]
+    slots = len(blocks)
+    in_specs = [pl.BlockSpec((BLOCK_ROWS, width), lambda i, *_: (0, 0))] * slots
+    in_specs.append(pl.BlockSpec(down.shape, lambda i, *_: (0, 0)))
+    in_specs += [pl.BlockSpec(memory_space=pl.ANY)] * len(after)
+    return pl.pallas_call(
+        functools.partial(pack_kernel, mx_count, first, rows_out, slots),
+        out_shape=(
+            jax.ShapeDtypeStruct((rows_out, width), jnp.bfloat16),
+            jax.ShapeDtypeStruct((rows_out // 4, 128), jnp.float32),
+        ),
+        grid_spec=pltpu.PrefetchScalarGridSpec(
+            num_scalar_prefetch=3,
+            grid=(1,),
+            in_specs=in_specs,
+            out_specs=(
+                pl.BlockSpec((rows_out, width), lambda i, *_: (0, 0)),
+                pl.BlockSpec((rows_out // 4, 128), lambda i, *_: (0, 0)),
+            ),
+            scratch_shapes=[pltpu.VMEM((rows_out, width), jnp.float32)],
+        ),
+        compiler_params=pltpu.CompilerParams(vmem_limit_bytes=VMEM_LIMIT),
+        cost_estimate=pl.CostEstimate(
+            flops=2 * rows_out * width * (256 + 512),
+            bytes_accessed=slots * BLOCK_ROWS * width * 2 + rows_out * width * 2,
+            transcendentals=0,
+        ),
+        name="pack_rows",
+    )(*scalars, *blocks, down, *after)
+
+
+def dot_kernel(steps, has_term, ids, x_ref, w_ref, *refs):
+    out_ref, acc = refs[-2:]
+    step = pl.program_id(0)
+    part = jnp.dot(x_ref[...], w_ref[...], preferred_element_type=jnp.float32)
+
+    @pl.when(step == 0)
+    def _():
+        acc[...] = part + refs[0][...].astype(jnp.float32) if has_term else part
+
+    @pl.when((step > 0) & (step < steps - 1))
+    def _():
+        acc[...] += part
+
+    @pl.when(step == steps - 1)
+    def _():
+        out_ref[...] = (acc[...] + part).astype(out_ref.dtype)
+
+
+def dot_quarter(x, w, flip, narrow, ids, out_dtype, term=None, after=()):
+    rows, depth = x.shape
+    step_depth = 512
+    steps = depth // step_depth
+    in_specs = [
+        pl.BlockSpec((rows, step_depth), lambda k, ids: (0, k)),
+        pl.BlockSpec((step_depth, narrow), lambda k, ids: (k, ids[1] ^ flip)),
+    ]
+    terms = []
+    if term is not None:
+        terms.append(term)
+        in_specs.append(pl.BlockSpec((rows, narrow), lambda k, ids: (0, 0)))
+    in_specs += [pl.BlockSpec(memory_space=pl.ANY)] * len(after)
+    return pl.pallas_call(
+        functools.partial(dot_kernel, steps, term is not None),
+        out_shape=jax.ShapeDtypeStruct((rows, narrow), out_dtype),
+        grid_spec=pltpu.PrefetchScalarGridSpec(
+            num_scalar_prefetch=1,
+            grid=(steps,),
+            in_specs=in_specs,
+            out_specs=pl.BlockSpec((rows, narrow), lambda k, ids: (0, 0)),
+            scratch_shapes=[pltpu.VMEM((rows, narrow), jnp.float32)],
+        ),
+        compiler_params=pltpu.CompilerParams(vmem_limit_bytes=VMEM_LIMIT),
+        cost_estimate=pl.CostEstimate(
+            flops=2 * rows * depth * narrow,
+            bytes_accessed=depth * narrow * 2 + rows * depth * 2 + rows * narrow * 4,
+            transcendentals=0,
+        ),
+        name="dot_quarter",
+    )(ids, x, w, *terms, *after)
+
+
+def finish_kernel(mx_count, first, ids, rows, tenants, *refs):
+    sums, far, (low_a, low_b, up_ref, scale_ref) = refs[0:2], refs[2:4], refs[4:8]
+    out_ref = refs[-1]
+    base = first + pl.program_id(0) * BLOCK_ROWS
+    table = slot_table(ids, rows, tenants, mx_count)
+    low = low_a[...] + low_b[...]
+    group = lax.broadcasted_iota(jnp.int32, (32, 128), 1) // 32
+    spread = jnp.concatenate([jnp.where(group == part, low, 0.0) for part in range(4)], axis=0)
+    spread = spread.astype(jnp.bfloat16)
+    tenant = row_tenants(table, base, (BLOCK_ROWS, 128))
+    lane = lax.broadcasted_iota(jnp.int32, (BLOCK_ROWS, 128), 1)
+    source = lax.broadcasted_iota(jnp.int32, (128, 128), 0) % (2 * RANK)
+    goal = lax.broadcasted_iota(jnp.int32, (128, 128), 1) % RANK
+    expanded = []
+    for side in range(2):
+        table_side = (source == goal + side * RANK).astype(jnp.bfloat16)
+        full = jnp.dot(spread, table_side, preferred_element_type=jnp.float32)
+        expanded.append(jnp.where(lane // RANK == tenant, full, 0.0).astype(jnp.bfloat16))
+    pick = ((lane % 8 == tenant) & (lane < 24)).astype(jnp.bfloat16)
+    columns = out_ref.shape[1]
+    for left in range(0, columns, 256):
+        right = min(left + 256, columns)
+        pre = []
+        for side in range(2):
+            scale = scale_ref[side, :, left:right]
+            high = scale.astype(jnp.bfloat16)
+            rest = scale - high.astype(jnp.float32)
+            middle = rest.astype(jnp.bfloat16)
+            final = (rest - middle.astype(jnp.float32)).astype(jnp.bfloat16)
+            stacked = jnp.concatenate(
+                [high.astype(jnp.float32), middle.astype(jnp.float32), final.astype(jnp.float32),
+                 jnp.zeros((104, right - left), jnp.float32)], axis=0
+            ).astype(jnp.bfloat16)
+            row_scale = jnp.dot(pick, stacked, preferred_element_type=jnp.float32)
+            maps = up_ref[:, side, :, left:right].reshape(8 * RANK, right - left)
+            adapted = jnp.dot(expanded[side], maps, preferred_element_type=jnp.float32)
+            total = sums[side][:, left:right] + far[side][:, left:right].astype(jnp.float32) + adapted
+            pre.append(total * row_scale)
+        hidden = pre[0] * (1.0 / (1.0 + jnp.exp(-pre[0]))) * pre[1]
+        out_ref[:, left:right] = hidden.astype(jnp.bfloat16)
+
+
+def finish_rows(mx_count, first, scalars, sums, far, lows, adapter_out, scale, after):
+    row_count, narrow = sums[0].shape
+    tenants = adapter_out.shape[0]
+    wide = pl.BlockSpec((BLOCK_ROWS, narrow), lambda i, *_: (i, 0))
+    low_spec = pl.BlockSpec((32, 128), lambda i, *_: (i, 0))
+    in_specs = [wide] * 4 + [low_spec] * 2
+    in_specs.append(
+        pl.BlockSpec((tenants, 2, RANK, narrow), lambda i, ids, *_: (0, 0, 0, ids[1]))
+    )
+    in_specs.append(pl.BlockSpec((2, tenants, narrow), lambda i, *_: (0, 0, 0)))
+    in_specs += [pl.BlockSpec(memory_space=pl.ANY)] * len(after)
+    return pl.pallas_call(
+        functools.partial(finish_kernel, mx_count, first),
+        out_shape=jax.ShapeDtypeStruct((row_count, narrow), jnp.bfloat16),
+        grid_spec=pltpu.PrefetchScalarGridSpec(
+            num_scalar_prefetch=3,
+            grid=(row_count // BLOCK_ROWS,),
+            in_specs=in_specs,
+            out_specs=wide,
+        ),
+        compiler_params=pltpu.CompilerParams(vmem_limit_bytes=VMEM_LIMIT),
+        cost_estimate=pl.CostEstimate(
+            flops=2 * row_count * narrow * 2 * 256 + 20 * row_count * narrow,
+            bytes_accessed=row_count * narrow * 14,
+            transcendentals=row_count * narrow,
+        ),
+        name="finish_rows",
+    )(*scalars, *sums, *far, *lows, adapter_out, scale, *after)
+
+
+def unpack_kernel(mx_count, chunks, ids, rows, tenants, *refs):
+    out_ref = refs[-1]
+    block = pl.program_id(0)
+    start = jnp.int32(0)
+    for first, _, _, owner in slot_table(ids, rows, tenants, mx_count):
+        start = jnp.where(owner == block, first, start)
+    count = rows[block]
+    total = None
+    for (first, row_count, _), hidden in zip(chunks, refs):
+        shape = (BLOCK_ROWS, row_count)
+        position = lax.broadcasted_iota(jnp.int32, shape, 0)
+        column = lax.broadcasted_iota(jnp.int32, shape, 1) + first
+        chosen = (position < count) & (column == position + start)
+        part = jnp.dot(chosen.astype(jnp.bfloat16), hidden[...], preferred_element_type=jnp.float32)
+        total = part if total is None else total + part
+    out_ref[...] = total.astype(jnp.bfloat16)
+
+
+def unpack_rows(mx_count, chunks, scalars, hidden, blocks):
+    narrow = hidden[0].shape[1]
+    return pl.pallas_call(
+        functools.partial(unpack_kernel, mx_count, chunks),
+        out_shape=jax.ShapeDtypeStruct((blocks * BLOCK_ROWS, narrow), jnp.bfloat16),
+        grid_spec=pltpu.PrefetchScalarGridSpec(
+            num_scalar_prefetch=3,
+            grid=(blocks,),
+            in_specs=[pl.BlockSpec(part.shape, lambda i, *_: (0, 0)) for part in hidden],
+            out_specs=pl.BlockSpec((BLOCK_ROWS, narrow), lambda i, *_: (i, 0)),
+        ),
+        compiler_params=pltpu.CompilerParams(vmem_limit_bytes=VMEM_LIMIT),
+        cost_estimate=pl.CostEstimate(
+            flops=2 * blocks * BLOCK_ROWS * LIVE_ROWS * narrow,
+            bytes_accessed=(blocks * BLOCK_ROWS + LIVE_ROWS) * narrow * 2,
+            transcendentals=0,
+        ),
+        name="unpack_rows",
+    )(*scalars, *hidden)
+
+
+def quarter(array, index, narrow):
+    return lax.dynamic_slice_in_dim(array, index * narrow, narrow, array.ndim - 1)
+
+
+def pipelined(
+    tokens, w_gate, w_up, adapter_in, adapter_out, magnitude, partial_norms, block_tenant, block_rows
+):
+    mx_count = lax.axis_size("mx")
+    my_count = lax.axis_size("my")
+    narrow = w_gate.shape[1] // my_count
+    mine = lax.axis_index("my")
+    ids = jnp.stack([lax.axis_index("mx"), mine]).astype(jnp.int32)
+    scalars = (ids, block_rows, block_tenant)
+    weights = (w_gate, w_up)
+    near = [(i, i ^ 1) for i in range(my_count)]
+    across = [(i, i ^ 2) for i in range(my_count)]
+
+    blocks = {(0, half): tokens[half * BLOCK_ROWS:(half + 1) * BLOCK_ROWS] for half in range(2)}
+    for hop in range(1, mx_count):
+        for half in range(2):
+            up = [(i, i + 1) for i in range(hop - 1, mx_count - 1)]
+            down = [(i + 1, i) for i in range(0, mx_count - hop)]
+            blocks[-hop, half] = lax.ppermute(blocks[1 - hop, half], "mx", up)
+            blocks[hop, half] = lax.ppermute(blocks[hop - 1, half], "mx", down)
+    ordered = [blocks[slot] for slot in SLOTS]
+
+    norms = partial_norms[0]
+    pair = jnp.stack([quarter(norms, mine, narrow), quarter(norms, mine ^ 2, narrow)])
+    other = jnp.stack([quarter(norms, mine ^ 1, narrow), quarter(norms, mine ^ 3, narrow)])
+    pair = pair + lax.ppermute(other, "my", near)
+    norm_total = pair[0] + lax.ppermute(pair[1], "my", across)
+    scale = quarter(magnitude, mine, narrow) * lax.rsqrt(norm_total)
+    scale = jnp.transpose(scale, (1, 0, 2))
+
+    down = jnp.transpose(adapter_in, (1, 0, 2)).reshape(adapter_in.shape[1], -1)
+
+    last = []
+
+    def chain(result):
+        last[:] = [result]
+        return result
+
+    packed, far, lows, near_got, sums, hidden = {}, {}, {}, {}, {}, {}
+
+    def pack(c):
+        first, row_count, slots = CHUNKS[c]
+        packed[c], low = pack_rows(mx_count, first, row_count, scalars, ordered[:slots], down, tuple(last))
+        chain(packed[c])
+        low = low + lax.ppermute(low, "my", near)
+        lows[c] = (low, lax.ppermute(low, "my", across))
+
+    def send_far(c):
+        got = []
+        for w in weights:
+            part = chain(dot_quarter(packed[c], w, 3, narrow, ids, jnp.bfloat16, after=tuple(last)))
+            got.append(lax.ppermute(part, "my", near))
+        far[c] = []
+        for w, term in zip(weights, got):
+            part = chain(dot_quarter(packed[c], w, 2, narrow, ids, jnp.bfloat16, term, after=tuple(last)))
+            far[c].append(lax.ppermute(part, "my", across))
+
+    def send_near(c):
+        near_got[c] = []
+        for w in weights:
+            part = chain(dot_quarter(packed[c], w, 1, narrow, ids, jnp.bfloat16, after=tuple(last)))
+            near_got[c].append(lax.ppermute(part, "my", near))
+
+    def keep(c):
+        sums[c] = [
+            chain(dot_quarter(packed[c], w, 0, narrow, ids, jnp.float32, term, after=tuple(last)))
+            for w, term in zip(weights, near_got[c])
+        ]
+
+    def finish(c):
+        hidden[c] = chain(
+            finish_rows(
+                mx_count, CHUNKS[c][0], scalars, sums[c], far[c], lows[c], adapter_out, scale, tuple(last)
+            )
+        )
+
+    pack(0)
+    send_far(0)
+    send_near(0)
+    pack(1)
+    send_far(1)
+    keep(0)
+    send_near(1)
+    pack(2)
+    send_far(2)
+    send_near(2)
+    keep(1)
+    keep(2)
+    finish(0)
+    finish(1)
+    finish(2)
+    return unpack_rows(mx_count, CHUNKS, scalars, [hidden[c] for c in range(len(CHUNKS))], block_rows.shape[0])
 
 
 def adapter_low(rows_piece, aligned_row_total, adapter_in, block_tenant):
@@ -22,15 +386,8 @@
     return low_terms.reshape(row_count, tenant_tables.shape[2])
 
 
-def finish(
-    summed,
-    reduced_rank_factor,
-    norm_total,
-    mag_cols,
-    adapter_cols,
-    first_row,
-    block_tenant,
-    block_rows,
+def finish_plain(
+    summed, reduced_rank_factor, norm_total, mag_cols, adapter_cols, first_row, block_tenant, block_rows
 ):
     row_count = summed.shape[0]
     col_count = summed.shape[2]
@@ -55,16 +412,8 @@
     return hidden.reshape(row_count, col_count).astype(jnp.bfloat16)
 
 
-def on_device(
-    tokens,
-    w_gate,
-    w_up,
-    adapter_in,
-    adapter_out,
-    magnitude,
-    partial_norms,
-    block_tenant,
-    block_rows,
+def plain(
+    tokens, w_gate, w_up, adapter_in, adapter_out, magnitude, partial_norms, block_tenant, block_rows
 ):
     local_rows = tokens.shape[0]
     col_local = w_gate.shape[1]
@@ -81,9 +430,21 @@
     narrow = col_local // my_count
     mag_cols = lax.dynamic_slice_in_dim(magnitude, device_position * narrow, narrow, 2)
     adapter_cols = lax.dynamic_slice_in_dim(adapter_out, device_position * narrow, narrow, 3)
-    return finish(
+    return finish_plain(
         summed, reduced_rank_factor, norm_total, mag_cols, adapter_cols, 0, block_tenant, block_rows
     )
+
+
+def on_device(tokens, w_gate, *rest):
+    my_count = lax.axis_size("my")
+    fits = (
+        my_count == 4
+        and lax.axis_size("mx") == 4
+        and tokens.shape[0] == 2 * BLOCK_ROWS
+        and tokens.shape[1] % 512 == 0
+        and w_gate.shape[1] % (my_count * 128) == 0
+    )
+    return (pipelined if fits else plain)(tokens, w_gate, *rest)
 
 
 def solution(mesh):

time: 616 us -> 387 us (0.63)
  waiting for transfers between devices: 378 us -> 85.6 us
  Pallas kernels: 0 us -> 233 us
  matrix products: 94.7 us -> 0 us
  local copies, waits for them, and re-layouts: 66.1 us -> 14.1 us
  starting transfers between devices: 0.09 us -> 42.5 us
  other arithmetic: 45.9 us -> 4.24 us
  between operations: 14.9 us -> 0.74 us
  blocking collectives: 13.7 us -> 0 us
    reduce_scatter x1 -> x0, waiting for transfers between devices: 328 us -> none  [on_device(): summed = lax.psum_scatter(main_part, 'my', scatter_dimension=2, tiled=True)]
    pallas_call x0 -> x31, Pallas kernels: none -> 233 us  [the longest x24 188 us: dot_quarter(): pl.pallas_call(functools.partial(dot_kernel, steps, term is not None), ou...]
    dot_general x4 -> x0, matrix products: 94.7 us -> none  [the longest x1 40.8 us: on_device(): up_part = jnp.dot(rows_piece, w_up, preferred_element_type=jnp.float32)]
    ppermute x0 -> x38, waiting for transfers between devices: none -> 85.6 us  [the longest x6 61.2 us: send_far(): far[c].append(lax.ppermute(part, 'my', across))]
    all_gather x1 -> x0, waiting for transfers between devices: 48.9 us -> none  [on_device(): rows_piece = lax.all_gather(tokens, 'mx', axis=0, tiled=True)]
    ppermute x0 -> x38, starting transfers between devices: none -> 42.5 us  [the longest x6 15.4 us: pipelined(): blocks[-hop, half] = lax.ppermute(blocks[1 - hop, half], 'mx', up)]
    another operation x1 -> x2, other arithmetic: 37.1 us -> 0.63 us  [the longest x1 0.61 us: pipelined(): ids = jnp.stack([lax.axis_index('mx'), mine]).astype(jnp.int32)]
    unnamed x13 -> x100, local copies, waits for them, and re-layouts: 45.7 us -> 10.5 us
  transfers between devices with their start and end apart: 3 -> 38, of which waited for: 2 -> 11; matrix products, arithmetic and copies ran while one was open for 29% -> 1% of each run, Pallas kernels for 0% -> 44%
where the time goes in v1:
time: 387 us; the launch traced here: 380 us
  Pallas kernels  233 us (60%)
  waiting for transfers between devices  85.6 us (22%)
  starting transfers between devices  42.5 us (11%)
  local copies, waits for them, and re-layouts  14.1 us (4%)
  other arithmetic  4.24 us (1%)
    pallas_call x24, Pallas kernels, dot_quarter(): pl.pallas_call(functools.partial(dot_kernel, steps, term is not None), ou...  188 us
    ppermute x6, waiting for transfers between devices, send_far(): far[c].append(lax.ppermute(part, 'my', across))  61.2 us
    pallas_call x3, Pallas kernels, pack_rows(): pl.pallas_call(functools.partial(pack_kernel, mx_count, first, rows_out,...  18.8 us
    pallas_call x3, Pallas kernels, finish_rows(): pl.pallas_call(functools.partial(finish_kernel, mx_count, first), out_sha...  17 us
    ppermute x6, starting transfers between devices, pipelined(): blocks[-hop, half] = lax.ppermute(blocks[1 - hop, half], 'mx', up)  15.4 us
    ppermute x6, starting transfers between devices, pipelined(): blocks[hop, half] = lax.ppermute(blocks[hop - 1, half], 'mx', down)  13 us
    unnamed x100, local copies, waits for them, and re-layouts  10.5 us
    pallas_call x1, Pallas kernels, unpack_rows(): pl.pallas_call(functools.partial(unpack_kernel, mx_count, chunks), out_sh...  8.87 us
  transfers between devices with their start and end apart: 38, of which 11 were waited for; matrix products, arithmetic and copies ran while one was open for 1% of the time, Pallas kernels for 44%

profile of v1, /device:TPU:8, one launch (start us, length us, event | category | flops | bytes accessed | tf_op | source)
XLA Modules:
  0.0 379.8 jit_solution(12137716747197485228)
XLA Ops:
  10.0 7.7 %collective-permute-done.refs_2_ = bf16[128,2048]{1,0:T(8,128)(2,1)S(1)} collective-permute-done((bf16[128,2048]{1,0:T(8,128)(2,1)S(1)}, bf16[128,2048]{1,0:T(8,128)(2,1)S(1)}, u32[]{:S(2)}, u32[]{:S(2)}) %collective-permute-start) | collective-permute-done | bytes 524320 | tf_op jit(solution)/shard_map/ppermute | solution.py:300
  50.0 6.3 %dot_quarter.26.refs_1_ = bf16[128,1664]{1,0:T(8,128)(2,1)} custom-call(s32[2]{0:T(128)} %pad_add_fusion.ids, bf16[128,2048]{1,0:T(8,128)(2,1)} %get-tuple-element.11.x_ref.refs_0_, bf16[2048,6656]{1,0:T(8,128)(2,1)} %w_ref.46, bf16[128,1664]{1,0:T(8,128)(2,1)} %copy-done.37, bf16[128,1664]{1,0:T(8,128)(2,1)} %dot_quarter.25.refs_1_), custom_call_target="tpu_custom_call" | custom-call | flops 872415232 | bytes 8192000 | tf_op jit(solution)/shard_map/dot_quarter/pallas_call | solution.py:147
  83.5 7.2 %dot_quarter.30.refs_0_ = bf16[256,1664]{1,0:T(8,128)(2,1)} custom-call(s32[2]{0:T(128)} %pad_add_fusion.ids, bf16[256,2048]{1,0:T(8,128)(2,1)} %get-tuple-element.12.x_ref.refs_0_, bf16[2048,6656]{1,0:T(8,128)(2,1)} %w_ref.46, bf16[256,2048]{1,0:T(8,128)(2,1)} %get-tuple-element.12.x_ref.refs_0_), custom_call_target="tpu_custom_call" | custom-call | flops 1744830464 | bytes 9568256 | tf_op jit(solution)/shard_map/dot_quarter/pallas_call | solution.py:147
  90.8 7.3 %dot_quarter.31.refs_1_ = bf16[256,1664]{1,0:T(8,128)(2,1)} custom-call(s32[2]{0:T(128)} %pad_add_fusion.ids, bf16[256,2048]{1,0:T(8,128)(2,1)} %get-tuple-element.12.x_ref.refs_0_, bf16[2048,6656]{1,0:T(8,128)(2,1)} %w_ref.47, bf16[256,1664]{1,0:T(8,128)(2,1)} %dot_quarter.30.refs_0_), custom_call_target="tpu_custom_call" | custom-call | flops 1744830464 | bytes 9568256 | tf_op jit(solution)/shard_map/dot_quarter/pallas_call | solution.py:147
  106.1 7.6 %dot_quarter.32.refs_1_ = bf16[256,1664]{1,0:T(8,128)(2,1)} custom-call(s32[2]{0:T(128)} %pad_add_fusion.ids, bf16[256,2048]{1,0:T(8,128)(2,1)} %get-tuple-element.12.x_ref.refs_0_, bf16[2048,6656]{1,0:T(8,128)(2,1)} %w_ref.46, bf16[256,1664]{1,0:T(8,128)(2,1)} %collective-permute-done.10.refs_0_, bf16[256,1664]{1,0:T(8,128)(2,1)} %dot_quarter.31.refs_1_), custom_call_target="tpu_custom_call" | custom-call | flops 1744830464 | bytes 9568256 | tf_op jit(solution)/shard_map/dot_quarter/pallas_call | solution.py:147
  123.3 7.5 %dot_quarter.33.refs_1_ = bf16[256,1664]{1,0:T(8,128)(2,1)} custom-call(s32[2]{0:T(128)} %pad_add_fusion.ids, bf16[256,2048]{1,0:T(8,128)(2,1)} %get-tuple-element.12.x_ref.refs_0_, bf16[2048,6656]{1,0:T(8,128)(2,1)} %w_ref.47, bf16[256,1664]{1,0:T(8,128)(2,1)} %copy-done.31, bf16[256,1664]{1,0:T(8,128)(2,1)} %dot_quarter.32.refs_1_), custom_call_target="tpu_custom_call" | custom-call | flops 1744830464 | bytes 9568256 | tf_op jit(solution)/shard_map/dot_quarter/pallas_call | solution.py:147
  130.7 6.5 %dot_quarter.34.refs_1_.refs_0_ = f32[128,1664]{1,0:T(8,128)} custom-call(s32[2]{0:T(128)} %pad_add_fusion.ids, bf16[128,2048]{1,0:T(8,128)(2,1)} %get-tuple-element.11.x_ref.refs_0_, bf16[2048,6656]{1,0:T(8,128)(2,1)} %w_ref.46, bf16[128,1664]{1,0:T(8,128)(2,1)} %collective-permute-done.4.refs_0_, bf16[256,1664]{1,0:T(8,128)(2,1)} %dot_quarter.33.refs_1_), custom_call_target="tpu_custom_call" | custom-call | flops 872415232 | bytes 8192000 | tf_op jit(solution)/shard_map/dot_quarter/pallas_call | solution.py:147
  137.2 6.5 %dot_quarter.35.refs_0_.refs_1_ = f32[128,1664]{1,0:T(8,128)} custom-call(s32[2]{0:T(128)} %pad_add_fusion.ids, bf16[128,2048]{1,0:T(8,128)(2,1)} %get-tuple-element.11.x_ref.refs_0_, bf16[2048,6656]{1,0:T(8,128)(2,1)} %w_ref.47, bf16[128,1664]{1,0:T(8,128)(2,1)} %collective-permute-done.11.refs_0_, f32[128,1664]{1,0:T(8,128)} %dot_quarter.34.refs_1_.refs_0_), custom_call_target="tpu_custom_call" | custom-call | flops 872415232 | bytes 8192000 | tf_op jit(solution)/shard_map/dot_quarter/pallas_call | solution.py:147
  143.7 7.2 %dot_quarter.36.refs_0_ = bf16[256,1664]{1,0:T(8,128)(2,1)} custom-call(s32[2]{0:T(128)} %pad_add_fusion.ids, bf16[256,2048]{1,0:T(8,128)(2,1)} %get-tuple-element.12.x_ref.refs_0_, bf16[2048,6656]{1,0:T(8,128)(2,1)} %w_ref.46, f32[128,1664]{1,0:T(8,128)} %dot_quarter.35.refs_0_.refs_1_), custom_call_target="tpu_custom_call" | custom-call | flops 1744830464 | bytes 9568256 | tf_op jit(solution)/shard_map/dot_quarter/pallas_call | solution.py:147
  150.9 7.2 %dot_quarter.37.refs_15_ = bf16[256,1664]{1,0:T(8,128)(2,1)} custom-call(s32[2]{0:T(128)} %pad_add_fusion.ids, bf16[256,2048]{1,0:T(8,128)(2,1)} %get-tuple-element.12.x_ref.refs_0_, bf16[2048,6656]{1,0:T(8,128)(2,1)} %w_ref.47, bf16[256,1664]{1,0:T(8,128)(2,1)} %dot_quarter.36.refs_0_), custom_call_target="tpu_custom_call" | custom-call | flops 1744830464 | bytes 9568256 | tf_op jit(solution)/shard_map/dot_quarter/pallas_call | solution.py:147
  160.1 8.3 %pack_rows.5 = (bf16[384,2048]{1,0:T(8,128)(2,1)}, f32[96,128]{1,0:T(8,128)}) custom-call(s32[2]{0:T(128)} %pad_add_fusion.ids, s32[8]{0:T(128)} %rows.13, s32[8]{0:T(128)} %tenants.13, bf16[128,2048]{1,0:T(8,128)(2,1)} %copy-done.2, bf16[128,2048]{1,0:T(8,128)(2,1)} %get-tuple-element.17.refs_1_, bf16[128,2048]{1,0:T(8,128)(2,1)} %copy-done.5, ...), custom_call_target="tpu_custom_call" | custom-call | flops 1207959552 | bytes 8912896 | tf_op jit(solution)/shard_map/pack_rows/pallas_call | solution.py:90
  168.4 16.9 %dot_quarter.38.refs_0_ = bf16[384,1664]{1,0:T(8,128)(2,1)} custom-call(s32[2]{0:T(128)} %pad_add_fusion.ids, bf16[384,2048]{1,0:T(8,128)(2,1)} %get-tuple-element.14.x_ref.refs_0_, bf16[2048,6656]{1,0:T(8,128)(2,1)} %w_ref.46, bf16[384,2048]{1,0:T(8,128)(2,1)} %get-tuple-element.14.x_ref.refs_0_), custom_call_target="tpu_custom_call" | custom-call | flops 2617245696 | bytes 10944512 | tf_op jit(solution)/shard_map/dot_quarter/pallas_call | solution.py:147
  185.3 8.4 %dot_quarter.39.refs_1_ = bf16[384,1664]{1,0:T(8,128)(2,1)} custom-call(s32[2]{0:T(128)} %pad_add_fusion.ids, bf16[384,2048]{1,0:T(8,128)(2,1)} %get-tuple-element.14.x_ref.refs_0_, bf16[2048,6656]{1,0:T(8,128)(2,1)} %w_ref.47, bf16[384,1664]{1,0:T(8,128)(2,1)} %dot_quarter.38.refs_0_), custom_call_target="tpu_custom_call" | custom-call | flops 2617245696 | bytes 10944512 | tf_op jit(solution)/shard_map/dot_quarter/pallas_call | solution.py:147
  198.6 8.7 %dot_quarter.40.refs_1_ = bf16[384,1664]{1,0:T(8,128)(2,1)} custom-call(s32[2]{0:T(128)} %pad_add_fusion.ids, bf16[384,2048]{1,0:T(8,128)(2,1)} %get-tuple-element.14.x_ref.refs_0_, bf16[2048,6656]{1,0:T(8,128)(2,1)} %w_ref.46, bf16[384,1664]{1,0:T(8,128)(2,1)} %copy-done.26, bf16[384,1664]{1,0:T(8,128)(2,1)} %dot_quarter.39.refs_1_), custom_call_target="tpu_custom_call" | custom-call | flops 2617245696 | bytes 10944512 | tf_op jit(solution)/shard_map/dot_quarter/pallas_call | solution.py:147
  208.4 8.7 %dot_quarter.41.refs_0_ = bf16[384,1664]{1,0:T(8,128)(2,1)} custom-call(s32[2]{0:T(128)} %pad_add_fusion.ids, bf16[384,2048]{1,0:T(8,128)(2,1)} %get-tuple-element.14.x_ref.refs_0_, bf16[2048,6656]{1,0:T(8,128)(2,1)} %w_ref.47, bf16[384,1664]{1,0:T(8,128)(2,1)} %copy-done.25, bf16[384,1664]{1,0:T(8,128)(2,1)} %dot_quarter.40.refs_1_), custom_call_target="tpu_custom_call" | custom-call | flops 2617245696 | bytes 10944512 | tf_op jit(solution)/shard_map/dot_quarter/pallas_call | solution.py:147
  217.1 8.4 %dot_quarter.42.refs_0_ = bf16[384,1664]{1,0:T(8,128)(2,1)} custom-call(s32[2]{0:T(128)} %pad_add_fusion.ids, bf16[384,2048]{1,0:T(8,128)(2,1)} %get-tuple-element.14.x_ref.refs_0_, bf16[2048,6656]{1,0:T(8,128)(2,1)} %w_ref.46, bf16[384,1664]{1,0:T(8,128)(2,1)} %dot_quarter.41.refs_0_), custom_call_target="tpu_custom_call" | custom-call | flops 2617245696 | bytes 10944512 | tf_op jit(solution)/shard_map/dot_quarter/pallas_call | solution.py:147
  235.5 8.2 %dot_quarter.43.refs_1_ = bf16[384,1664]{1,0:T(8,128)(2,1)} custom-call(s32[2]{0:T(128)} %pad_add_fusion.ids, bf16[384,2048]{1,0:T(8,128)(2,1)} %get-tuple-element.14.x_ref.refs_0_, bf16[2048,6656]{1,0:T(8,128)(2,1)} %w_ref.47, bf16[384,1664]{1,0:T(8,128)(2,1)} %dot_quarter.42.refs_0_), custom_call_target="tpu_custom_call" | custom-call | flops 2617245696 | bytes 10944512 | tf_op jit(solution)/shard_map/dot_quarter/pallas_call | solution.py:147
  254.6 7.8 %dot_quarter.44.refs_1_.refs_0_ = f32[256,1664]{1,0:T(8,128)} custom-call(s32[2]{0:T(128)} %pad_add_fusion.ids, bf16[256,2048]{1,0:T(8,128)(2,1)} %get-tuple-element.12.x_ref.refs_0_, bf16[2048,6656]{1,0:T(8,128)(2,1)} %w_ref.46, bf16[256,1664]{1,0:T(8,128)(2,1)} %copy-done.30, bf16[384,1664]{1,0:T(8,128)(2,1)} %dot_quarter.43.refs_1_), custom_call_target="tpu_custom_call" | custom-call | flops 1744830464 | bytes 9568256 | tf_op jit(solution)/shard_map/dot_quarter/pallas_call | solution.py:147
  262.4 7.9 %dot_quarter.45.refs_1_ = f32[256,1664]{1,0:T(8,128)} custom-call(s32[2]{0:T(128)} %pad_add_fusion.ids, bf16[256,2048]{1,0:T(8,128)(2,1)} %get-tuple-element.12.x_ref.refs_0_, bf16[2048,6656]{1,0:T(8,128)(2,1)} %w_ref.47, bf16[256,1664]{1,0:T(8,128)(2,1)} %collective-permute-done.28.refs_0_, f32[256,1664]{1,0:T(8,128)} %dot_quarter.44.refs_1_.refs_0_), custom_call_target="tpu_custom_call" | custom-call | flops 1744830464 | bytes 9568256 | tf_op jit(solution)/shard_map/dot_quarter/pallas_call | solution.py:147
  271.0 9.4 %dot_quarter.46.refs_1_.refs_0_ = f32[384,1664]{1,0:T(8,128)} custom-call(s32[2]{0:T(128)} %pad_add_fusion.ids, bf16[384,2048]{1,0:T(8,128)(2,1)} %get-tuple-element.14.x_ref.refs_0_, bf16[2048,6656]{1,0:T(8,128)(2,1)} %w_ref.46, bf16[384,1664]{1,0:T(8,128)(2,1)} %collective-permute-done.27.refs_0_, f32[256,1664]{1,0:T(8,128)} %dot_quarter.45.refs_1_), custom_call_target="tpu_custom_call" | custom-call | flops 2617245696 | bytes 10944512 | tf_op jit(solution)/shard_map/dot_quarter/pallas_call | solution.py:147
  280.3 9.3 %dot_quarter.47.refs_8_.refs_1_ = f32[384,1664]{1,0:T(8,128)} custom-call(s32[2]{0:T(128)} %pad_add_fusion.ids, bf16[384,2048]{1,0:T(8,128)(2,1)} %get-tuple-element.14.x_ref.refs_0_, bf16[2048,6656]{1,0:T(8,128)(2,1)} %w_ref.47, bf16[384,1664]{1,0:T(8,128)(2,1)} %collective-permute-done.26.refs_0_, f32[384,1664]{1,0:T(8,128)} %dot_quarter.46.refs_1_.refs_0_), custom_call_target="tpu_custom_call" | custom-call | flops 2617245696 | bytes 10944512 | tf_op jit(solution)/shard_map/dot_quarter/pallas_call | solution.py:147
  289.6 61.2 %collective-permute-done.12.refs_2_ = bf16[128,1664]{1,0:T(8,128)(2,1)S(1)} collective-permute-done((bf16[128,1664]{1,0:T(8,128)(2,1)S(1)}, bf16[128,1664]{1,0:T(8,128)(2,1)S(1)}, u32[]{:S(2)}, u32[]{:S(2)}) %collective-permute-start.12) | collective-permute-done | bytes 426016 | tf_op jit(solution)/shard_map/ppermute | solution.py:337
  363.4 7.3 %finish_rows.5.refs_2_ = bf16[384,1664]{1,0:T(8,128)(2,1)} custom-call(s32[2]{0:T(128)} %pad_add_fusion.ids, s32[8]{0:T(128)} %rows.13, s32[8]{0:T(128)} %tenants.13, f32[384,1664]{1,0:T(8,128)} %dot_quarter.46.refs_1_.refs_0_, f32[384,1664]{1,0:T(8,128)} %dot_quarter.47.refs_8_.refs_1_, bf16[384,1664]{1,0:T(8,128)(2,1)} %copy-done.28, ...), custom_call_target="tpu_custom_call" | custom-call | flops 667090944 | bytes 8945664 | tf_op jit(solution)/shard_map/finish_rows/pallas_call | solution.py:220
  370.7 8.9 %unpack_rows.1 = bf16[1024,1664]{1,0:T(8,128)(2,1)} custom-call(s32[2]{0:T(128)} %pad_add_fusion.ids, s32[8]{0:T(128)} %rows.13, s32[8]{0:T(128)} %tenants.13, bf16[128,1664]{1,0:T(8,128)(2,1)} %finish_rows.3.refs_8_.refs_0_, bf16[256,1664]{1,0:T(8,128)(2,1)} %finish_rows.4.refs_8_.refs_1_, bf16[384,1664]{1,0:T(8,128)(2,1)} %finish_rows.5.refs_2_), custom_call_target="tpu_custom_call" | custom-call | flops 2617245696 | bytes 5963776 | tf_op jit(solution)/shard_map/unpack_rows/pallas_call | solution.py:259
  (195 shorter events, 128.7 us)
Async XLA Ops:
  2.2 15.5 %collective-permute-start = (bf16[128,2048]{1,0:T(8,128)(2,1)S(1)}, bf16[128,2048]{1,0:T(8,128)(2,1)S(1)}, u32[]{:S(2)}, u32[]{:S(2)}) collective-permute-start(bf16[128,2048]{1,0:T(8,128)(2,1)S(1)} %get-tuple-element.18.refs_0_), channel_id=1, source_target_pairs={{0,4},{4,8},{8,12},{1,5},{5,9},{9,13},{2,6},{6,10},{10,14},{3,7},{... | collective-permute-start | bytes 1572872 | tf_op jit(solution)/shard_map/ppermute | solution.py:300
  32.5 15.5 %collective-permute-start.3 = (bf16[128,1664]{1,0:T(8,128)(2,1)}, bf16[128,1664]{1,0:T(8,128)(2,1)S(1)}, u32[]{:S(2)}, u32[]{:S(2)}) collective-permute-start(bf16[128,1664]{1,0:T(8,128)(2,1)} %dot_quarter.24.refs_0_), channel_id=1, source_target_pairs={{0,1},{1,0},{2,3},{3,2},{4,5},{5,4},{6,7},{7,6},{8,9},{9,8},{10,11... | collective-permute-start | bytes 1277960 | tf_op jit(solution)/shard_map/ppermute | solution.py:333
  38.8 17.4 %collective-permute-start.2 = (bf16[128,1664]{1,0:T(8,128)(2,1)}, bf16[128,1664]{1,0:T(8,128)(2,1)S(1)}, u32[]{:S(2)}, u32[]{:S(2)}) collective-permute-start(bf16[128,1664]{1,0:T(8,128)(2,1)} %dot_quarter.25.refs_1_), channel_id=1, source_target_pairs={{0,1},{1,0},{2,3},{3,2},{4,5},{5,4},{6,7},{7,6},{8,9},{9,8},{10,11... | collective-permute-start | bytes 1277960 | tf_op jit(solution)/shard_map/ppermute | solution.py:333
  39.2 36.4 %collective-permute-start.5 = (bf16[128,2048]{1,0:T(8,128)(2,1)S(1)}, bf16[128,2048]{1,0:T(8,128)(2,1)S(1)}, u32[]{:S(2)}, u32[]{:S(2)}) collective-permute-start(bf16[128,2048]{1,0:T(8,128)(2,1)S(1)} %copy-done.1), channel_id=1, source_target_pairs={{0,4},{4,8},{8,12},{1,5},{5,9},{9,13},{2,6},{6,10},{10,14},{3,7},{... | collective-permute-start | bytes 1572872 | tf_op jit(solution)/shard_map/ppermute | solution.py:300
  42.1 33.5 %collective-permute-start.6 = (bf16[128,2048]{1,0:T(8,128)(2,1)S(1)}, bf16[128,2048]{1,0:T(8,128)(2,1)S(1)}, u32[]{:S(2)}, u32[]{:S(2)}) collective-permute-start(bf16[128,2048]{1,0:T(8,128)(2,1)S(1)} %copy-done.1), channel_id=1, source_target_pairs={{4,0},{8,4},{12,8},{5,1},{9,5},{13,9},{6,2},{10,6},{14,10},{7,3},{... | collective-permute-start | bytes 1572872 | tf_op jit(solution)/shard_map/ppermute | solution.py:301
  45.1 30.6 %collective-permute-start.7 = (bf16[128,2048]{1,0:T(8,128)(2,1)S(1)}, bf16[128,2048]{1,0:T(8,128)(2,1)S(1)}, u32[]{:S(2)}, u32[]{:S(2)}) collective-permute-start(bf16[128,2048]{1,0:T(8,128)(2,1)S(1)} %copy-done.6), channel_id=1, source_target_pairs={{4,8},{8,12},{5,9},{9,13},{6,10},{10,14},{7,11},{11,15},{20,24},{2... | collective-permute-start | bytes 1572872 | tf_op jit(solution)/shard_map/ppermute | solution.py:300
  48.0 27.6 %collective-permute-start.8 = (bf16[128,2048]{1,0:T(8,128)(2,1)S(1)}, bf16[128,2048]{1,0:T(8,128)(2,1)S(1)}, u32[]{:S(2)}, u32[]{:S(2)}) collective-permute-start(bf16[128,2048]{1,0:T(8,128)(2,1)S(1)} %copy-done.8), channel_id=1, source_target_pairs={{4,0},{8,4},{5,1},{9,5},{6,2},{10,6},{7,3},{11,7},{20,16},{24,20},... | collective-permute-start | bytes 1572872 | tf_op jit(solution)/shard_map/ppermute | solution.py:301
  98.2 23.8 %collective-permute-start.9 = (bf16[256,1664]{1,0:T(8,128)(2,1)}, bf16[256,1664]{1,0:T(8,128)(2,1)S(1)}, u32[]{:S(2)}, u32[]{:S(2)}) collective-permute-start(bf16[256,1664]{1,0:T(8,128)(2,1)} %dot_quarter.31.refs_1_), channel_id=1, source_target_pairs={{0,1},{1,0},{2,3},{3,2},{4,5},{5,4},{6,7},{7,6},{8,9},{9,8},{10,11... | collective-permute-start | bytes 2555912 | tf_op jit(solution)/shard_map/ppermute | solution.py:333
  103.3 15.7 %collective-permute-start.19 = (bf16[128,2048]{1,0:T(8,128)(2,1)S(1)}, bf16[128,2048]{1,0:T(8,128)(2,1)}, u32[]{:S(2)}, u32[]{:S(2)}) collective-permute-start(bf16[128,2048]{1,0:T(8,128)(2,1)S(1)} %copy-done.16), channel_id=1, source_target_pairs={{4,0},{8,4},{5,1},{9,5},{6,2},{10,6},{7,3},{11,7},{20,16},{24,20},... | collective-permute-start | bytes 1572872 | tf_op jit(solution)/shard_map/ppermute | solution.py:301
  105.5 15.7 %collective-permute-start.4 = (bf16[128,1664]{1,0:T(8,128)(2,1)S(1)}, bf16[128,1664]{1,0:T(8,128)(2,1)}, u32[]{:S(2)}, u32[]{:S(2)}) collective-permute-start(bf16[128,1664]{1,0:T(8,128)(2,1)S(1)} %copy-done.24), channel_id=1, source_target_pairs={{0,1},{1,0},{2,3},{3,2},{4,5},{5,4},{6,7},{7,6},{8,9},{9,8},{10,11... | collective-permute-start | bytes 1277960 | tf_op jit(solution)/shard_map/ppermute | solution.py:343
  105.6 31.7 %collective-permute-start.11 = (bf16[128,1664]{1,0:T(8,128)(2,1)S(1)}, bf16[128,1664]{1,0:T(8,128)(2,1)}, u32[]{:S(2)}, u32[]{:S(2)}) collective-permute-start(bf16[128,1664]{1,0:T(8,128)(2,1)S(1)} %copy-done.23), channel_id=1, source_target_pairs={{0,1},{1,0},{2,3},{3,2},{4,5},{5,4},{6,7},{7,6},{8,9},{9,8},{10,11... | collective-permute-start | bytes 1277960 | tf_op jit(solution)/shard_map/ppermute | solution.py:343
  114.0 44.2 %collective-permute-start.20 = (bf16[128,2048]{1,0:T(8,128)(2,1)S(1)}, bf16[128,2048]{1,0:T(8,128)(2,1)S(1)}, u32[]{:S(2)}, u32[]{:S(2)}) collective-permute-start(bf16[128,2048]{1,0:T(8,128)(2,1)S(1)} %copy-done.18), channel_id=1, source_target_pairs={{8,12},{9,13},{10,14},{11,15},{24,28},{25,29},{26,30},{27,31}} | collective-permute-start | bytes 1572872 | tf_op jit(solution)/shard_map/ppermute | solution.py:300
  119.0 39.2 %collective-permute-start.21 = (bf16[128,2048]{1,0:T(8,128)(2,1)S(1)}, bf16[128,2048]{1,0:T(8,128)(2,1)S(1)}, u32[]{:S(2)}, u32[]{:S(2)}) collective-permute-start(bf16[128,2048]{1,0:T(8,128)(2,1)S(1)} %copy-done.20), channel_id=1, source_target_pairs={{4,0},{5,1},{6,2},{7,3},{20,16},{21,17},{22,18},{23,19}} | collective-permute-start | bytes 1572872 | tf_op jit(solution)/shard_map/ppermute | solution.py:301
  121.2 36.9 %collective-permute-start.22 = (bf16[128,2048]{1,0:T(8,128)(2,1)}, bf16[128,2048]{1,0:T(8,128)(2,1)S(1)}, u32[]{:S(2)}, u32[]{:S(2)}) collective-permute-start(bf16[128,2048]{1,0:T(8,128)(2,1)} %collective-permute-done.18.refs_8_), channel_id=1, source_target_pairs={{8,12},{9,13},{10,14},{11,15},{24,28},{25,29},{26,30},{27,31}} | collective-permute-start | bytes 1572872 | tf_op jit(solution)/shard_map/ppermute | solution.py:300
  121.9 36.2 %collective-permute-start.23 = (bf16[128,2048]{1,0:T(8,128)(2,1)}, bf16[128,2048]{1,0:T(8,128)(2,1)S(1)}, u32[]{:S(2)}, u32[]{:S(2)}) collective-permute-start(bf16[128,2048]{1,0:T(8,128)(2,1)} %collective-permute-done.19.refs_9_), channel_id=1, source_target_pairs={{4,0},{5,1},{6,2},{7,3},{20,16},{21,17},{22,18},{23,19}} | collective-permute-start | bytes 1572872 | tf_op jit(solution)/shard_map/ppermute | solution.py:301
  197.0 51.0 %collective-permute-start.29 = (bf16[256,1664]{1,0:T(8,128)(2,1)S(1)}, bf16[256,1664]{1,0:T(8,128)(2,1)S(1)}, u32[]{:S(2)}, u32[]{:S(2)}) collective-permute-start(bf16[256,1664]{1,0:T(8,128)(2,1)S(1)} %copy-done.12), channel_id=1, source_target_pairs={{0,1},{1,0},{2,3},{3,2},{4,5},{5,4},{6,7},{7,6},{8,9},{9,8},{10,11... | collective-permute-start | bytes 2555912 | tf_op jit(solution)/shard_map/ppermute | solution.py:343
  197.4 52.1 %collective-permute-start.28 = (bf16[256,1664]{1,0:T(8,128)(2,1)S(1)}, bf16[256,1664]{1,0:T(8,128)(2,1)}, u32[]{:S(2)}, u32[]{:S(2)}) collective-permute-start(bf16[256,1664]{1,0:T(8,128)(2,1)S(1)} %copy-done.9), channel_id=1, source_target_pairs={{0,1},{1,0},{2,3},{3,2},{4,5},{5,4},{6,7},{7,6},{8,9},{9,8},{10,11... | collective-permute-start | bytes 2555912 | tf_op jit(solution)/shard_map/ppermute | solution.py:343
  225.5 24.6 %collective-permute-start.27 = (bf16[384,1664]{1,0:T(8,128)(2,1)}, bf16[384,1664]{1,0:T(8,128)(2,1)}, u32[]{:S(2)}, u32[]{:S(2)}) collective-permute-start(bf16[384,1664]{1,0:T(8,128)(2,1)} %dot_quarter.42.refs_0_), channel_id=1, source_target_pairs={{0,1},{1,0},{2,3},{3,2},{4,5},{5,4},{6,7},{7,6},{8,9},{9,8},{10,11... | collective-permute-start | bytes 3833864 | tf_op jit(solution)/shard_map/ppermute | solution.py:343
  244.5 25.8 %collective-permute-start.26 = (bf16[384,1664]{1,0:T(8,128)(2,1)}, bf16[384,1664]{1,0:T(8,128)(2,1)}, u32[]{:S(2)}, u32[]{:S(2)}) collective-permute-start(bf16[384,1664]{1,0:T(8,128)(2,1)} %dot_quarter.43.refs_1_), channel_id=1, source_target_pairs={{0,1},{1,0},{2,3},{3,2},{4,5},{5,4},{6,7},{7,6},{8,9},{9,8},{10,11... | collective-permute-start | bytes 3833864 | tf_op jit(solution)/shard_map/ppermute | solution.py:343
  247.4 108.3 %collective-permute-start.31 = (bf16[256,1664]{1,0:T(8,128)(2,1)S(1)}, bf16[256,1664]{1,0:T(8,128)(2,1)}, u32[]{:S(2)}, u32[]{:S(2)}) collective-permute-start(bf16[256,1664]{1,0:T(8,128)(2,1)S(1)} %copy-done.11), channel_id=1, source_target_pairs={{0,2},{1,3},{2,0},{3,1},{4,6},{5,7},{6,4},{7,5},{8,10},{9,11},{10,... | collective-permute-start | bytes 2555912 | tf_op jit(solution)/shard_map/ppermute | solution.py:337
  248.0 107.8 %collective-permute-start.30 = (bf16[256,1664]{1,0:T(8,128)(2,1)S(1)}, bf16[256,1664]{1,0:T(8,128)(2,1)}, u32[]{:S(2)}, u32[]{:S(2)}) collective-permute-start(bf16[256,1664]{1,0:T(8,128)(2,1)S(1)} %copy-done.10), channel_id=1, source_target_pairs={{0,2},{1,3},{2,0},{3,1},{4,6},{5,7},{6,4},{7,5},{8,10},{9,11},{10,... | collective-permute-start | bytes 2555912 | tf_op jit(solution)/shard_map/ppermute | solution.py:337
  249.6 111.7 %collective-permute-start.35 = (bf16[384,1664]{1,0:T(8,128)(2,1)S(1)}, bf16[384,1664]{1,0:T(8,128)(2,1)S(1)}, u32[]{:S(2)}, u32[]{:S(2)}) collective-permute-start(bf16[384,1664]{1,0:T(8,128)(2,1)S(1)} %copy-done.4), channel_id=1, source_target_pairs={{0,2},{1,3},{2,0},{3,1},{4,6},{5,7},{6,4},{7,5},{8,10},{9,11},{10,... | collective-permute-start | bytes 3833864 | tf_op jit(solution)/shard_map/ppermute | solution.py:337
  250.1 111.1 %collective-permute-start.34 = (bf16[384,1664]{1,0:T(8,128)(2,1)S(1)}, bf16[384,1664]{1,0:T(8,128)(2,1)S(1)}, u32[]{:S(2)}, u32[]{:S(2)}) collective-permute-start(bf16[384,1664]{1,0:T(8,128)(2,1)S(1)} %copy-done.3), channel_id=1, source_target_pairs={{0,2},{1,3},{2,0},{3,1},{4,6},{5,7},{6,4},{7,5},{8,10},{9,11},{10,... | collective-permute-start | bytes 3833864 | tf_op jit(solution)/shard_map/ppermute | solution.py:337
  270.3 80.5 %collective-permute-start.12 = (bf16[128,1664]{1,0:T(8,128)(2,1)S(1)}, bf16[128,1664]{1,0:T(8,128)(2,1)S(1)}, u32[]{:S(2)}, u32[]{:S(2)}) collective-permute-start(bf16[128,1664]{1,0:T(8,128)(2,1)S(1)} %copy-done.21), channel_id=1, source_target_pairs={{0,2},{1,3},{2,0},{3,1},{4,6},{5,7},{6,4},{7,5},{8,10},{9,11},{10,... | collective-permute-start | bytes 1277960 | tf_op jit(solution)/shard_map/ppermute | solution.py:337
  (62 other events, 756.1 us)

commit v2 on v0

--- a/solution.py
+++ b/solution.py
@@ -1,12 +1,491 @@
+import functools
 import math
 
 import jax
 import jax.numpy as jnp
 from jax import lax
+from jax.experimental import pallas as pl
+from jax.experimental.pallas import tpu as pltpu
 from jax.sharding import PartitionSpec as P
 
 RANK = 16
 BLOCK_ROWS = 128
+LIVE_ROWS = 768
+STEP_DEPTH = 512
+VMEM_LIMIT = 48 * 1024 * 1024
+
+SLOTS = (
+    (0, 0), (0, 1),
+    (-1, 0), (1, 0), (-1, 1), (1, 1),
+    (-2, 0), (-2, 1), (2, 0), (2, 1),
+    (-3, 0), (-3, 1), (3, 0), (3, 1),
+)
+CHUNKS = ((0, 128, 4), (128, 128, 6), (256, 256, 10), (512, 256, 14))
+ANY = pl.BlockSpec(memory_space=pl.ANY)
+COST = pl.CostEstimate(flops=0, bytes_accessed=0, transcendentals=0)
+
+
+def slot_table(ids, rows, tenants, mx_count):
+    place = ids[0]
+    start = jnp.int32(0)
+    table = []
+    for distance, half in SLOTS:
+        source = place + distance
+        valid = (source >= 0) & (source < mx_count)
+        block = jnp.clip(source, 0, mx_count - 1) * 2 + half
+        count = jnp.where(valid, rows[block], 0)
+        table.append((start, count, tenants[block], jnp.where(valid, block, -1)))
+        start = start + count
+    return table
+
+
+def row_tenants(table, first, shape):
+    row = lax.broadcasted_iota(jnp.int32, shape, 0) + first
+    tenant = jnp.full(shape, -1, jnp.int32)
+    for start, count, owner, _ in table:
+        tenant = jnp.where((row >= start) & (row < start + count), owner, tenant)
+    return tenant
+
+
+def pack_kernel(mx_count, first, rows_out, places, copied, ids, rows, tenants, *refs):
+    slots = len(places)
+    tokens = max(ref for ref, _ in places) + 1
+    token_refs = refs[:tokens]
+    down_ref = refs[tokens]
+    scratch = refs[-6:]
+    x_ref, low_ref = refs[-9:-7] if copied is not None else refs[-8:-6]
+    buffer, down, acc, sems, down_sem, copy_sem = scratch
+    table = slot_table(ids, rows, tenants, mx_count)
+    needed, copies = [], []
+    for slot, (ref, row) in enumerate(places):
+        start, count, _, _ = table[slot]
+        needed.append((count > 0) & (start < first + rows_out) & (start + count > first))
+        copies.append(
+            pltpu.make_async_copy(token_refs[ref].at[pl.ds(row, BLOCK_ROWS)], buffer.at[slot], sems.at[slot])
+        )
+    for need, copy in zip(needed, copies):
+        pl.when(need)(copy.start)
+    down_copy = pltpu.make_async_copy(down_ref, down, down_sem)
+    down_copy.start()
+    if copied is not None:
+        hand_on = pltpu.make_async_copy(token_refs[copied], refs[-7], copy_sem)
+        hand_on.start()
+    acc[...] = jnp.zeros_like(acc)
+    for slot in range(slots):
+        start, count, _, _ = table[slot]
+
+        @pl.when(needed[slot])
+        def _():
+            copies[slot].wait()
+            target = lax.broadcasted_iota(jnp.int32, (rows_out, BLOCK_ROWS), 0) + first
+            position = lax.broadcasted_iota(jnp.int32, (rows_out, BLOCK_ROWS), 1)
+            chosen = (position < count) & (target == position + start)
+            acc[...] += jnp.dot(
+                chosen.astype(jnp.bfloat16), buffer[slot], preferred_element_type=jnp.float32
+            )
+
+    x = acc[...].astype(jnp.bfloat16)
+    x_ref[...] = x
+    down_copy.wait()
+    for tile in range(rows_out // BLOCK_ROWS):
+        low = lax.dot_general(
+            x[tile * BLOCK_ROWS:(tile + 1) * BLOCK_ROWS], down[...], (((1,), (1,)), ((), ())),
+            preferred_element_type=jnp.float32,
+        )
+        tenant = row_tenants(table, first + tile * BLOCK_ROWS, low.shape)
+        lane = lax.broadcasted_iota(jnp.int32, low.shape, 1)
+        low = jnp.where(lane // (2 * RANK) == tenant, low, 0.0)
+        low = low[:, :128] + low[:, 128:]
+        low = low + pltpu.roll(low, 64, 1)
+        low = low + pltpu.roll(low, 32, 1)
+        group = lax.broadcasted_iota(jnp.int32, (32, 128), 1) // 32
+        packed = jnp.where(group == 0, low[0:32], 0.0)
+        for part in range(1, 4):
+            packed = jnp.where(group == part, low[part * 32:(part + 1) * 32], packed)
+        low_ref[tile * 32:(tile + 1) * 32, :] = packed
+    if copied is not None:
+        hand_on.wait()
+
+
+def pack_rows(mx_count, first, rows_out, scalars, tokens, places, down, after, copied=None):
+    width = down.shape[1]
+    outs = [
+        jax.ShapeDtypeStruct((rows_out, width), jnp.bfloat16),
+        jax.ShapeDtypeStruct((rows_out // 4, 128), jnp.float32),
+    ]
+    out_specs = [
+        pl.BlockSpec((rows_out, width), lambda i, *_: (0, 0)),
+        pl.BlockSpec((rows_out // 4, 128), lambda i, *_: (0, 0)),
+    ]
+    if copied is not None:
+        outs.append(jax.ShapeDtypeStruct(tokens[copied].shape, tokens[copied].dtype))
+        out_specs.append(ANY)
+    return pl.pallas_call(
+        functools.partial(pack_kernel, mx_count, first, rows_out, places, copied),
+        out_shape=outs,
+        grid_spec=pltpu.PrefetchScalarGridSpec(
+            num_scalar_prefetch=3,
+            grid=(1,),
+            in_specs=[ANY] * (len(tokens) + 1 + len(after)),
+            out_specs=out_specs,
+            scratch_shapes=[
+                pltpu.VMEM((len(places), BLOCK_ROWS, width), jnp.bfloat16),
+                pltpu.VMEM(down.shape, jnp.bfloat16),
+                pltpu.VMEM((rows_out, width), jnp.float32),
+                pltpu.SemaphoreType.DMA((len(places),)),
+                pltpu.SemaphoreType.DMA,
+                pltpu.SemaphoreType.DMA,
+            ],
+        ),
+        compiler_params=pltpu.CompilerParams(vmem_limit_bytes=VMEM_LIMIT),
+        cost_estimate=COST,
+        name="pack_rows",
+    )(*scalars, *tokens, down, *after)
+
+
+def dot_kernel(flip, row_counts, has_term, passed, joined, narrow, steps, ids, *refs):
+    x_refs, refs = refs[:len(row_counts)], refs[len(row_counts):]
+    w_refs, refs = refs[:2], refs[2:]
+    term_refs = refs[:2] if has_term else None
+    x, w, acc, out, x_sem, w_sem, term_sem, out_sem = refs[-8:]
+    if joined:
+        out_refs = [refs[-9 - passed].at[side] for side in range(2)]
+    else:
+        out_refs = refs[-10 - passed:-8 - passed]
+    left = pl.multiple_of((ids[1] ^ flip) * narrow, 128)
+
+    x_copies, row = [], 0
+    for part, (x_ref, count) in enumerate(zip(x_refs, row_counts)):
+        x_copies.append(pltpu.make_async_copy(x_ref, x.at[pl.ds(row, count)], x_sem.at[part]))
+        row += count
+    for copy in x_copies:
+        copy.start()
+
+    def piece(side, step):
+        return pltpu.make_async_copy(
+            w_refs[side].at[pl.ds(step * STEP_DEPTH, STEP_DEPTH), pl.ds(left, narrow)],
+            w.at[side * steps + step], w_sem.at[side * steps + step],
+        )
+
+    for side in range(2):
+        for step in range(steps):
+            piece(side, step).start()
+    if has_term:
+        term_copies = [
+            pltpu.make_async_copy(term_refs[side], out.at[side], term_sem.at[side]) for side in range(2)
+        ]
+        for copy in term_copies:
+            copy.start()
+        for side in range(2):
+            term_copies[side].wait()
+            acc[side] = out[side].astype(jnp.float32)
+    else:
+        acc[...] = jnp.zeros_like(acc)
+    for copy in x_copies:
+        copy.wait()
+
+    def out_copy(side):
+        source = acc if out_refs[side].dtype == jnp.float32 else out
+        return pltpu.make_async_copy(source.at[side], out_refs[side], out_sem.at[side])
+
+    for side in range(2):
+        @pl.loop(0, steps)
+        def _(step):
+            piece(side, step).wait()
+            columns = pl.ds(pl.multiple_of(step * STEP_DEPTH, STEP_DEPTH), STEP_DEPTH)
+            acc[side] += jnp.dot(x[:, columns], w[side * steps + step], preferred_element_type=jnp.float32)
+
+        if out_refs[side].dtype != jnp.float32:
+            out[side] = acc[side].astype(out.dtype)
+        out_copy(side).start()
+    for side in range(2):
+        out_copy(side).wait()
+
+
+def dot_pair(xs, weights, flip, narrow, ids, out_dtype, terms=(), after=(), passed=(), joined=False):
+    row_counts = tuple(x.shape[0] for x in xs)
+    rows, depth = sum(row_counts), xs[0].shape[1]
+    steps = depth // STEP_DEPTH
+    operands = [ids, *xs, *weights, *terms, *after]
+    if joined:
+        outs = [jax.ShapeDtypeStruct((2, rows, narrow), out_dtype)]
+    else:
+        outs = [jax.ShapeDtypeStruct((rows, narrow), out_dtype)] * 2
+    aliases = {len(operands) + i: len(outs) + i for i in range(len(passed))}
+    operands += list(passed)
+    return pl.pallas_call(
+        functools.partial(dot_kernel, flip, row_counts, len(terms) > 0, len(passed), joined, narrow, steps),
+        out_shape=outs + [jax.ShapeDtypeStruct(array.shape, array.dtype) for array in passed],
+        grid_spec=pltpu.PrefetchScalarGridSpec(
+            num_scalar_prefetch=1,
+            grid=(1,),
+            in_specs=[ANY] * (len(operands) - 1),
+            out_specs=[ANY] * (len(outs) + len(passed)),
+            scratch_shapes=[
+                pltpu.VMEM((rows, depth), jnp.bfloat16),
+                pltpu.VMEM((2 * steps, STEP_DEPTH, narrow), jnp.bfloat16),
+                pltpu.VMEM((2, rows, narrow), jnp.float32),
+                pltpu.VMEM((2, rows, narrow), jnp.bfloat16),
+                pltpu.SemaphoreType.DMA((len(xs),)),
+                pltpu.SemaphoreType.DMA((2 * steps,)),
+                pltpu.SemaphoreType.DMA((2,)),
+                pltpu.SemaphoreType.DMA((2,)),
+            ],
+        ),
+        input_output_aliases=aliases,
+        compiler_params=pltpu.CompilerParams(vmem_limit_bytes=VMEM_LIMIT),
+        cost_estimate=COST,
+        name="dot_pair",
+    )(*operands)
+
+
+def finish_tile(base, table, sums, far, low, up_ref, scale_ref, store):
+    group = lax.broadcasted_iota(jnp.int32, (32, 128), 1) // 32
+    spread = jnp.concatenate([jnp.where(group == part, low, 0.0) for part in range(4)], axis=0)
+    spread = spread.astype(jnp.bfloat16)
+    tenant = row_tenants(table, base, (BLOCK_ROWS, 128))
+    lane = lax.broadcasted_iota(jnp.int32, (BLOCK_ROWS, 128), 1)
+    source = lax.broadcasted_iota(jnp.int32, (128, 128), 0) % (2 * RANK)
+    goal = lax.broadcasted_iota(jnp.int32, (128, 128), 1) % RANK
+    expanded = []
+    for side in range(2):
+        table_side = (source == goal + side * RANK).astype(jnp.bfloat16)
+        full = jnp.dot(spread, table_side, preferred_element_type=jnp.float32)
+        expanded.append(jnp.where(lane // RANK == tenant, full, 0.0).astype(jnp.bfloat16))
+    pick = ((lane % 8 == tenant) & (lane < 24)).astype(jnp.bfloat16)
+    columns = scale_ref.shape[2]
+    for left in range(0, columns, 256):
+        right = min(left + 256, columns)
+        pre = []
+        for side in range(2):
+            scale = scale_ref[side, :, left:right]
+            high = scale.astype(jnp.bfloat16)
+            rest = scale - high.astype(jnp.float32)
+            middle = rest.astype(jnp.bfloat16)
+            final = (rest - middle.astype(jnp.float32)).astype(jnp.bfloat16)
+            stacked = jnp.concatenate(
+                [high.astype(jnp.float32), middle.astype(jnp.float32), final.astype(jnp.float32),
+                 jnp.zeros((104, right - left), jnp.float32)], axis=0
+            ).astype(jnp.bfloat16)
+            row_scale = jnp.dot(pick, stacked, preferred_element_type=jnp.float32)
+            maps = up_ref[:, side, :, left:right].reshape(8 * RANK, right - left)
+            adapted = jnp.dot(expanded[side], maps, preferred_element_type=jnp.float32)
+            total = sums(side, left, right) + far(side, left, right).astype(jnp.float32) + adapted
+            pre.append(total * row_scale)
+        hidden = pre[0] * (1.0 / (1.0 + jnp.exp(-pre[0]))) * pre[1]
+        store(left, right, hidden.astype(jnp.bfloat16))
+
+
+def finish_kernel(
+    mx_count, first, ids, rows, tenants, gate_sum, up_sum, far, low_a, low_b, up_ref, scale_ref, *refs
+):
+    out_ref = refs[-1]
+    sums = (gate_sum, up_sum)
+    base = first + pl.program_id(0) * BLOCK_ROWS
+    table = slot_table(ids, rows, tenants, mx_count)
+
+    def store(left, right, value):
+        out_ref[:, left:right] = value
+
+    finish_tile(
+        base, table, lambda side, left, right: sums[side][:, left:right],
+        lambda side, left, right: far[side, :, left:right], low_a[...] + low_b[...], up_ref, scale_ref, store,
+    )
+
+
+def finish_rows(mx_count, first, scalars, sums, far, lows, adapter_out, scale, after):
+    _, row_count, narrow = far.shape
+    tenants = adapter_out.shape[0]
+    place = first // BLOCK_ROWS
+    low_spec = pl.BlockSpec((32, 128), lambda i, *_: (place + i, 0))
+    in_specs = [
+        *[pl.BlockSpec((BLOCK_ROWS, narrow), lambda i, *_: (place + i, 0))] * 2,
+        pl.BlockSpec((2, BLOCK_ROWS, narrow), lambda i, *_: (0, i, 0)),
+        low_spec, low_spec,
+        pl.BlockSpec((tenants, 2, RANK, narrow), lambda i, ids, *_: (0, 0, 0, ids[1])),
+        pl.BlockSpec((2, tenants, narrow), lambda i, *_: (0, 0, 0)),
+    ]
+    return pl.pallas_call(
+        functools.partial(finish_kernel, mx_count, first),
+        out_shape=jax.ShapeDtypeStruct((row_count, narrow), jnp.bfloat16),
+        grid_spec=pltpu.PrefetchScalarGridSpec(
+            num_scalar_prefetch=3,
+            grid=(row_count // BLOCK_ROWS,),
+            in_specs=in_specs + [ANY] * len(after),
+            out_specs=pl.BlockSpec((BLOCK_ROWS, narrow), lambda i, *_: (i, 0)),
+        ),
+        compiler_params=pltpu.CompilerParams(vmem_limit_bytes=VMEM_LIMIT),
+        cost_estimate=COST,
+        name="finish_rows",
+    )(*scalars, *sums, far, *lows, adapter_out, scale, *after)
+
+
+def last_kernel(
+    mx_count, first, ids, rows, tenants, gate_sum, up_sum, far, low_a, low_b, up_ref, scale_ref, *refs
+):
+    earlier, out_ref, held = refs[:-2], refs[-2], refs[-1]
+    sums = (gate_sum, up_sum)
+    table = slot_table(ids, rows, tenants, mx_count)
+    block = pl.program_id(0)
+
+    @pl.when(block == 0)
+    def _():
+        row = 0
+        for part in earlier:
+            held[row:row + part.shape[0], :] = part[...]
+            row += part.shape[0]
+        held[LIVE_ROWS:, :] = jnp.zeros((BLOCK_ROWS, held.shape[1]), held.dtype)
+
+        @pl.loop(0, far.shape[1] // BLOCK_ROWS)
+        def _(tile):
+            here = pl.ds(pl.multiple_of(tile * BLOCK_ROWS, BLOCK_ROWS), BLOCK_ROWS)
+            there = pl.ds(pl.multiple_of(first + tile * BLOCK_ROWS, BLOCK_ROWS), BLOCK_ROWS)
+            lanes = pl.ds(pl.multiple_of(tile * 32, 32), 32)
+
+            def store(left, right, value):
+                held[there, left:right] = value
+
+            finish_tile(
+                first + tile * BLOCK_ROWS, table, lambda side, left, right: sums[side][here, left:right],
+                lambda side, left, right: far[side, here, left:right], low_a[lanes, :] + low_b[lanes, :],
+                up_ref, scale_ref, store,
+            )
+
+    start = jnp.int32(0)
+    for begin, _, _, owner in table:
+        start = jnp.where(owner == block, begin, start)
+    count = rows[block]
+    base = pl.multiple_of(jnp.minimum(start // BLOCK_ROWS * BLOCK_ROWS, LIVE_ROWS - BLOCK_ROWS), BLOCK_ROWS)
+    shape = (BLOCK_ROWS, 2 * BLOCK_ROWS)
+    position = lax.broadcasted_iota(jnp.int32, shape, 0)
+    column = lax.broadcasted_iota(jnp.int32, shape, 1) + base
+    chosen = (position < count) & (column == position + start)
+    out_ref[...] = jnp.dot(
+        chosen.astype(jnp.bfloat16), held[pl.ds(base, 2 * BLOCK_ROWS), :], preferred_element_type=jnp.float32
+    ).astype(jnp.bfloat16)
+
+
+def last_rows(mx_count, first, scalars, sums, far, lows, adapter_out, scale, earlier, blocks):
+    _, row_count, narrow = far.shape
+    tenants = adapter_out.shape[0]
+    place = first // row_count
+    low_spec = pl.BlockSpec((row_count // 4, 128), lambda i, *_: (place, 0))
+    in_specs = [
+        *[pl.BlockSpec((row_count, narrow), lambda i, *_: (0, 0))] * 2,
+        pl.BlockSpec((2, row_count, narrow), lambda i, *_: (0, 0, 0)),
+        low_spec, low_spec,
+        pl.BlockSpec((tenants, 2, RANK, narrow), lambda i, ids, *_: (0, 0, 0, ids[1])),
+        pl.BlockSpec((2, tenants, narrow), lambda i, *_: (0, 0, 0)),
+    ] + [pl.BlockSpec(part.shape, lambda i, *_: (0, 0)) for part in earlier]
+    return pl.pallas_call(
+        functools.partial(last_kernel, mx_count, first),
+        out_shape=jax.ShapeDtypeStruct((blocks * BLOCK_ROWS, narrow), jnp.bfloat16),
+        grid_spec=pltpu.PrefetchScalarGridSpec(
+            num_scalar_prefetch=3,
+            grid=(blocks,),
+            in_specs=in_specs,
+            out_specs=pl.BlockSpec((BLOCK_ROWS, narrow), lambda i, *_: (i, 0)),
+            scratch_shapes=[pltpu.VMEM((LIVE_ROWS + BLOCK_ROWS, narrow), jnp.bfloat16)],
+        ),
+        compiler_params=pltpu.CompilerParams(vmem_limit_bytes=VMEM_LIMIT),
+        cost_estimate=COST,
+        name="last_rows",
+    )(*scalars, *sums, far, *lows, adapter_out, scale, *earlier)
+
+
+def quarter(array, index, narrow):
+    return lax.dynamic_slice_in_dim(array, index * narrow, narrow, array.ndim - 1)
+
+
+def pipelined(
+    tokens, w_gate, w_up, adapter_in, adapter_out, magnitude, partial_norms, block_tenant, block_rows
+):
+    mx_count = lax.axis_size("mx")
+    my_count = lax.axis_size("my")
+    narrow = w_gate.shape[1] // my_count
+    mine = lax.axis_index("my")
+    ids = jnp.stack([lax.axis_index("mx"), mine]).astype(jnp.int32)
+    scalars = (ids, block_rows, block_tenant)
+    weights = (w_gate, w_up)
+    near = [(i, i ^ 1) for i in range(my_count)]
+    across = [(i, i ^ 2) for i in range(my_count)]
+
+    def hop(block, distance, least=0):
+        if distance > 0:
+            pairs = [(i, i + distance) for i in range(least, mx_count - distance)]
+        else:
+            pairs = [(i, i + distance) for i in range(-distance, mx_count - least)]
+        return lax.ppermute(block, "mx", pairs)
+
+    halves = [tokens[half * BLOCK_ROWS:(half + 1) * BLOCK_ROWS] for half in range(2)]
+    first_hop = [(hop(block, 1), hop(block, -1)) for block in halves]
+
+    norms = partial_norms[0]
+    pair = jnp.stack([quarter(norms, mine, narrow), quarter(norms, mine ^ 2, narrow)])
+    other = jnp.stack([quarter(norms, mine ^ 1, narrow), quarter(norms, mine ^ 3, narrow)])
+    pair = pair + lax.ppermute(other, "my", near)
+    norm_total = pair[0] + lax.ppermute(pair[1], "my", across)
+    scale = quarter(magnitude, mine, narrow) * lax.rsqrt(norm_total)
+    scale = jnp.transpose(scale, (1, 0, 2))
+
+    down = jnp.transpose(adapter_in, (0, 2, 1)).reshape(-1, adapter_in.shape[1])
+
+    def pack(c, blocks, places, after, copied=None):
+        first, row_count, slots = CHUNKS[c]
+        return pack_rows(mx_count, first, row_count, scalars, blocks, places[:slots], down, after, copied)
+
+    def swap(parts, pairs):
+        return [lax.ppermute(part, "my", pairs) for part in parts]
+
+    def send_far(x, passed=()):
+        parts = dot_pair([x], weights, 3, narrow, ids, jnp.bfloat16)
+        got = swap(parts, near)
+        part, *handed = dot_pair([x], weights, 2, narrow, ids, jnp.bfloat16, got, passed=passed, joined=True)
+        return part, lax.ppermute(part, "my", across), handed
+
+    blocks = [tokens, *first_hop[0]]
+    places = [(0, 0), (0, BLOCK_ROWS), (1, 0), (2, 0)]
+    x0, low0, again = pack(0, blocks, places, (scale,), copied=0)
+    second_hop = [hop(again, 2), hop(again, -2)]
+    mark, far0, _ = send_far(x0)
+
+    blocks += first_hop[1]
+    places += [(3, 0), (4, 0)]
+    x1, low1 = pack(1, blocks, places, (mark,))
+    mark, far1, second_hop = send_far(x1, passed=second_hop)
+    third_hop = [hop(second_hop[0], 1, 2), hop(second_hop[1], -1, 2)]
+
+    blocks += second_hop
+    places += [(5, 0), (5, BLOCK_ROWS), (6, 0), (6, BLOCK_ROWS)]
+    x2, low2 = pack(2, blocks, places, (mark, far0))
+    mark, far2, _ = send_far(x2)
+
+    early = [x0, x1, x2]
+    parts = dot_pair(early, weights, 1, narrow, ids, jnp.bfloat16, after=(mark,))
+    early_got = swap(parts, near)
+
+    blocks += third_hop
+    places += [(7, 0), (7, BLOCK_ROWS), (8, 0), (8, BLOCK_ROWS)]
+    x3, low3 = pack(3, blocks, places, (parts[0], far1))
+    mark, far3, _ = send_far(x3)
+
+    low = jnp.concatenate([low0, low1, low2, low3], axis=0)
+    low = low + lax.ppermute(low, "my", near)
+    lows = (low, lax.ppermute(low, "my", across))
+
+    parts = dot_pair([x3], weights, 1, narrow, ids, jnp.bfloat16, after=(mark,))
+    late_got = swap(parts, near)
+    early_sums = dot_pair(early, weights, 0, narrow, ids, jnp.float32, early_got, after=(parts[0],))
+    late_sums = dot_pair([x3], weights, 0, narrow, ids, jnp.float32, late_got, after=(early_sums[0], far2))
+    hidden, mark = [], late_sums[0]
+    for c, far in enumerate([far0, far1, far2]):
+        mark = finish_rows(
+            mx_count, CHUNKS[c][0], scalars, early_sums, far, lows, adapter_out, scale, (mark,)
+        )
+        hidden.append(mark)
+    return last_rows(
+        mx_count, CHUNKS[3][0], scalars, late_sums, far3, lows, adapter_out, scale, hidden, block_rows.shape[0]
+    )
 
 
 def adapter_low(rows_piece, aligned_row_total, adapter_in, block_tenant):
@@ -22,15 +501,8 @@
     return low_terms.reshape(row_count, tenant_tables.shape[2])
 
 
-def finish(
-    summed,
-    reduced_rank_factor,
-    norm_total,
-    mag_cols,
-    adapter_cols,
-    first_row,
-    block_tenant,
-    block_rows,
+def finish_plain(
+    summed, reduced_rank_factor, norm_total, mag_cols, adapter_cols, first_row, block_tenant, block_rows
 ):
     row_count = summed.shape[0]
     col_count = summed.shape[2]
@@ -55,16 +527,8 @@
     return hidden.reshape(row_count, col_count).astype(jnp.bfloat16)
 
 
-def on_device(
-    tokens,
-    w_gate,
-    w_up,
-    adapter_in,
-    adapter_out,
-    magnitude,
-    partial_norms,
-    block_tenant,
-    block_rows,
+def plain(
+    tokens, w_gate, w_up, adapter_in, adapter_out, magnitude, partial_norms, block_tenant, block_rows
 ):
     local_rows = tokens.shape[0]
     col_local = w_gate.shape[1]
@@ -81,9 +545,21 @@
     narrow = col_local // my_count
     mag_cols = lax.dynamic_slice_in_dim(magnitude, device_position * narrow, narrow, 2)
     adapter_cols = lax.dynamic_slice_in_dim(adapter_out, device_position * narrow, narrow, 3)
-    return finish(
+    return finish_plain(
         summed, reduced_rank_factor, norm_total, mag_cols, adapter_cols, 0, block_tenant, block_rows
     )
+
+
+def on_device(tokens, w_gate, *rest):
+    my_count = lax.axis_size("my")
+    fits = (
+        my_count == 4
+        and lax.axis_size("mx") == 4
+        and tokens.shape[0] == 2 * BLOCK_ROWS
+        and tokens.shape[1] % 512 == 0
+        and w_gate.shape[1] % (my_count * 128) == 0
+    )
+    return (pipelined if fits else plain)(tokens, w_gate, *rest)
 
 
 def solution(mesh):

time: 616 us -> 279 us (0.45)
  waiting for transfers between devices: 378 us -> 89.4 us
  Pallas kernels: 0 us -> 144 us
  matrix products: 94.7 us -> 0 us
  local copies, waits for them, and re-layouts: 66.1 us -> 5.02 us
  other arithmetic: 45.9 us -> 0.83 us
  starting transfers between devices: 0.09 us -> 34.2 us
  between operations: 14.9 us -> 0.79 us
  blocking collectives: 13.7 us -> 0 us
    reduce_scatter x1 -> x0, waiting for transfers between devices: 328 us -> none  [on_device(): summed = lax.psum_scatter(main_part, 'my', scatter_dimension=2, tiled=True)]
    pallas_call x0 -> x20, Pallas kernels: none -> 144 us  [the longest x12 103 us: dot_pair(): pl.pallas_call(functools.partial(dot_kernel, flip, row_counts, len(terms)...]
    dot_general x4 -> x0, matrix products: 94.7 us -> none  [the longest x1 40.8 us: on_device(): up_part = jnp.dot(rows_piece, w_up, preferred_element_type=jnp.float32)]
    ppermute x0 -> x28, waiting for transfers between devices: none -> 89.4 us  [the longest x8 49.6 us: hop(): return lax.ppermute(block, 'mx', pairs)]
    all_gather x1 -> x0, waiting for transfers between devices: 48.9 us -> none  [on_device(): rows_piece = lax.all_gather(tokens, 'mx', axis=0, tiled=True)]
    unnamed x13 -> x47, local copies, waits for them, and re-layouts: 45.7 us -> 2.57 us
    another operation x1 -> x2, other arithmetic: 37.1 us -> 0.76 us  [the longest x1 0.69 us: pipelined(): jnp.stack([quarter(norms, mine ^ 1, narrow), quarter(norms, mine ^ 3, nar...]
    ppermute x0 -> x28, starting transfers between devices: none -> 34.2 us  [the longest x8 22.8 us: hop(): return lax.ppermute(block, 'mx', pairs)]
  transfers between devices with their start and end apart: 3 -> 28, of which waited for: 2 -> 13; matrix products, arithmetic and copies ran while one was open for 29% -> 0% of each run, Pallas kernels for 0% -> 46%
where the time goes in v2:
time: 279 us; the launch traced here: 275 us
  Pallas kernels  144 us (52%)
  waiting for transfers between devices  89.4 us (32%)
  starting transfers between devices  34.2 us (12%)
  local copies, waits for them, and re-layouts  5.02 us (2%)
    pallas_call x12, Pallas kernels, dot_pair(): pl.pallas_call(functools.partial(dot_kernel, flip, row_counts, len(terms)...  103 us
    ppermute x8, waiting for transfers between devices, hop(): return lax.ppermute(block, 'mx', pairs)  49.6 us
    ppermute x1, waiting for transfers between devices, pipelined(): lows = (low, lax.ppermute(low, 'my', across))  28.3 us
    ppermute x8, starting transfers between devices, hop(): return lax.ppermute(block, 'mx', pairs)  22.8 us
    pallas_call x4, Pallas kernels, pack_rows(): pl.pallas_call(functools.partial(pack_kernel, mx_count, first, rows_out,...  22.6 us
    pallas_call x3, Pallas kernels, finish_rows(): pl.pallas_call(functools.partial(finish_kernel, mx_count, first), out_sha...  9.87 us
    pallas_call x1, Pallas kernels, last_rows(): pl.pallas_call(functools.partial(last_kernel, mx_count, first), out_shape...  8.72 us
    ppermute x12, waiting for transfers between devices, swap(): return [lax.ppermute(part, 'my', pairs) for part in parts]  6.43 us
  transfers between devices with their start and end apart: 28, of which 13 were waited for; matrix products, arithmetic and copies ran while one was open for 0% of the time, Pallas kernels for 46%

profile of v2, /device:TPU:8, one launch (start us, length us, event | category | flops | bytes accessed | tf_op | source)
XLA Modules:
  0.0 274.5 jit_solution(14466470717398255647)
XLA Ops:
  2.4 3.5 %collective-permute-start = (bf16[128,2048]{1,0:T(8,128)(2,1)}, bf16[128,2048]{1,0:T(8,128)(2,1)S(1)}, u32[]{:S(2)}, u32[]{:S(2)}) collective-permute-start(bf16[128,2048]{1,0:T(8,128)(2,1)} %get-tuple-element.62), channel_id=1, source_target_pairs={{0,4},{4,8},{8,12},{1,5},{5,9},{9,13},{2,6},{6,10},{10,14},{3,7},{... | collective-permute-start | bytes 1572872 | tf_op jit(solution)/shard_map/ppermute | solution.py:418
  12.5 3.4 %collective-permute-done.5 = f32[8,2,1664]{2,0,1:T(8,128)S(1)} collective-permute-done((f32[8,2,1664]{2,0,1:T(8,128)S(1)}, f32[8,2,1664]{2,0,1:T(8,128)S(1)}, u32[]{:S(2)}, u32[]{:S(2)}) %collective-permute-start.5) | collective-permute-done | bytes 106528 | tf_op jit(solution)/shard_map/ppermute | solution.py:427
  18.1 3.3 %collective-permute-done.1.refs_2_ = bf16[128,2048]{1,0:T(8,128)(2,1)} collective-permute-done((bf16[128,2048]{1,0:T(8,128)(2,1)}, bf16[128,2048]{1,0:T(8,128)(2,1)}, u32[]{:S(2)}, u32[]{:S(2)}) %collective-permute-start.1) | collective-permute-done | bytes 524320 | tf_op jit(solution)/shard_map/ppermute | solution.py:418
  23.7 6.5 %dot_pair.12 = (bf16[128,1664]{1,0:T(8,128)(2,1)S(1)}, bf16[128,1664]{1,0:T(8,128)(2,1)S(1)}) custom-call(s32[2]{0:T(128)S(1)} %pad_add_fusion.ids, bf16[128,2048]{1,0:T(8,128)(2,1)S(1)} %get-tuple-element.33.refs_0_, bf16[2048,6656]{1,0:T(8,128)(2,1)} %refs_1_.19, bf16[2048,6656]{1,0:T(8,128)(2,1)} %refs_2_.19), custom_call_target="tpu_custom_call" | custom-call | tf_op jit(solution)/shard_map/dot_pair/pallas_call | solution.py:216
  30.8 3.5 %collective-permute-start.10 = (bf16[256,2048]{1,0:T(8,128)(2,1)S(1)}, bf16[256,2048]{1,0:T(8,128)(2,1)}, u32[]{:S(2)}, u32[]{:S(2)}) collective-permute-start(bf16[256,2048]{1,0:T(8,128)(2,1)S(1)} %get-tuple-element.39), channel_id=1, source_target_pairs={{0,8},{4,12},{1,9},{5,13},{2,10},{6,14},{3,11},{7,15},{16,24},{20,... | collective-permute-start | bytes 3145736 | tf_op jit(solution)/shard_map/ppermute | solution.py:418
  35.5 6.2 %collective-permute-start.2 = (bf16[128,2048]{1,0:T(8,128)(2,1)S(1)}, bf16[128,2048]{1,0:T(8,128)(2,1)S(1)}, u32[]{:S(2)}, u32[]{:S(2)}) collective-permute-start(bf16[128,2048]{1,0:T(8,128)(2,1)S(1)} %copy-done.18), channel_id=1, source_target_pairs={{0,4},{4,8},{8,12},{1,5},{5,9},{9,13},{2,6},{6,10},{10,14},{3,7},{... | collective-permute-start | bytes 1572872 | tf_op jit(solution)/shard_map/ppermute | solution.py:418
  43.7 6.3 %dot_pair.13.refs_6_ = bf16[2,128,1664]{2,1,0:T(8,128)(2,1)S(1)} custom-call(s32[2]{0:T(128)S(1)} %pad_add_fusion.ids, bf16[128,2048]{1,0:T(8,128)(2,1)S(1)} %get-tuple-element.33.refs_0_, bf16[2048,6656]{1,0:T(8,128)(2,1)} %refs_1_.19, bf16[2048,6656]{1,0:T(8,128)(2,1)} %refs_2_.19, bf16[128,1664]{1,0:T(8,128)(2,1)S(1)} %collective-permute-done.6.refs_3_, ...), custom_call_target="tpu_custom_call" | custom-call | tf_op jit(solution)/shard_map/dot_pair/pallas_call | solution.py:216
  51.5 38.1 %collective-permute-done.2.refs_3_ = bf16[128,2048]{1,0:T(8,128)(2,1)S(1)} collective-permute-done((bf16[128,2048]{1,0:T(8,128)(2,1)S(1)}, bf16[128,2048]{1,0:T(8,128)(2,1)S(1)}, u32[]{:S(2)}, u32[]{:S(2)}) %collective-permute-start.2) | collective-permute-done | bytes 524320 | tf_op jit(solution)/shard_map/ppermute | solution.py:418
  89.6 6.0 %collective-permute-done.3.refs_4_ = bf16[128,2048]{1,0:T(8,128)(2,1)S(1)} collective-permute-done((bf16[128,2048]{1,0:T(8,128)(2,1)S(1)}, bf16[128,2048]{1,0:T(8,128)(2,1)S(1)}, u32[]{:S(2)}, u32[]{:S(2)}) %collective-permute-start.3) | collective-permute-done | bytes 524320 | tf_op jit(solution)/shard_map/ppermute | solution.py:418
  97.8 6.5 %dot_pair.14 = (bf16[128,1664]{1,0:T(8,128)(2,1)S(1)}, bf16[128,1664]{1,0:T(8,128)(2,1)S(1)}) custom-call(s32[2]{0:T(128)S(1)} %pad_add_fusion.ids, bf16[128,2048]{1,0:T(8,128)(2,1)S(1)} %get-tuple-element.36.refs_0_.refs_1_, bf16[2048,6656]{1,0:T(8,128)(2,1)} %refs_1_.19, bf16[2048,6656]{1,0:T(8,128)(2,1)} %refs_2_.19), custom_call_target="tpu_custom_call" | custom-call | tf_op jit(solution)/shard_map/dot_pair/pallas_call | solution.py:216
  106.7 6.3 %dot_pair.15 = (bf16[2,128,1664]{2,1,0:T(8,128)(2,1)S(1)}, bf16[256,2048]{1,0:T(8,128)(2,1)}, bf16[256,2048]{1,0:T(8,128)(2,1)S(1)}) custom-call(s32[2]{0:T(128)S(1)} %pad_add_fusion.ids, bf16[128,2048]{1,0:T(8,128)(2,1)S(1)} %get-tuple-element.36.refs_0_.refs_1_, bf16[2048,6656]{1,0:T(8,128)(2,1)} %refs_1_.19, ...), custom_call_target="tpu_custom_call", output_to_operand_aliasing={{1}: (6, {}), {2}: (7, {})} | custom-call | tf_op jit(solution)/shard_map/dot_pair/pallas_call | solution.py:216
  117.2 4.6 %pack_rows.6 = (bf16[256,2048]{1,0:T(8,128)(2,1)S(1)}, f32[64,128]{1,0:T(8,128)S(1)}) custom-call(s32[2]{0:T(128)S(1)} %pad_add_fusion.ids, s32[8]{0:T(128)S(1)} %copy-done.16, s32[8]{0:T(128)S(1)} %copy-done.17, bf16[256,2048]{1,0:T(8,128)(2,1)S(1)} %copy-done.3, bf16[128,2048]{1,0:T(8,128)(2,1)S(1)} %collective-permute-done.refs_1_, ...), custom_call_target="tpu_custom_call" | custom-call | tf_op jit(solution)/shard_map/pack_rows/pallas_call | solution.py:123
  121.8 7.8 %dot_pair.16 = (bf16[256,1664]{1,0:T(8,128)(2,1)S(1)}, bf16[256,1664]{1,0:T(8,128)(2,1)S(1)}) custom-call(s32[2]{0:T(128)S(1)} %pad_add_fusion.ids, bf16[256,2048]{1,0:T(8,128)(2,1)S(1)} %get-tuple-element.43.refs_0_.refs_2_, bf16[2048,6656]{1,0:T(8,128)(2,1)} %refs_1_.19, bf16[2048,6656]{1,0:T(8,128)(2,1)} %refs_2_.19), custom_call_target="tpu_custom_call" | custom-call | tf_op jit(solution)/shard_map/dot_pair/pallas_call | solution.py:216
  133.3 7.8 %dot_pair.17.refs_5_ = bf16[2,256,1664]{2,1,0:T(8,128)(2,1)S(1)} custom-call(s32[2]{0:T(128)S(1)} %pad_add_fusion.ids, bf16[256,2048]{1,0:T(8,128)(2,1)S(1)} %get-tuple-element.43.refs_0_.refs_2_, bf16[2048,6656]{1,0:T(8,128)(2,1)} %refs_1_.19, bf16[2048,6656]{1,0:T(8,128)(2,1)} %refs_2_.19, bf16[256,1664]{1,0:T(8,128)(2,1)S(1)} %collective-permute-done.15.refs_3_, ...), custom_call_target="tpu_custom_call" | custom-call | tf_op jit(solution)/shard_map/dot_pair/pallas_call | solution.py:216
  142.3 12.8 %dot_pair.18 = (bf16[512,1664]{1,0:T(8,128)(2,1)}, bf16[512,1664]{1,0:T(8,128)(2,1)}) custom-call(s32[2]{0:T(128)S(1)} %pad_add_fusion.ids, bf16[128,2048]{1,0:T(8,128)(2,1)S(1)} %get-tuple-element.33.refs_0_, bf16[128,2048]{1,0:T(8,128)(2,1)S(1)} %get-tuple-element.36.refs_0_.refs_1_, bf16[256,2048]{1,0:T(8,128)(2,1)S(1)} %get-tuple-element.43.refs_0_.refs_2_, ...), custom_call_target="tpu_custom_call" | custom-call | tf_op jit(solution)/shard_map/dot_pair/pallas_call | solution.py:216
  155.5 13.5 %pack_rows.7 = (bf16[256,2048]{1,0:T(8,128)(2,1)S(1)}, f32[64,128]{1,0:T(8,128)S(1)}) custom-call(s32[2]{0:T(128)S(1)} %pad_add_fusion.ids, s32[8]{0:T(128)S(1)} %copy-done.16, s32[8]{0:T(128)S(1)} %copy-done.17, bf16[256,2048]{1,0:T(8,128)(2,1)S(1)} %copy-done.3, bf16[128,2048]{1,0:T(8,128)(2,1)S(1)} %collective-permute-done.refs_1_, ...), custom_call_target="tpu_custom_call" | custom-call | tf_op jit(solution)/shard_map/pack_rows/pallas_call | solution.py:123
  169.0 7.8 %dot_pair.19 = (bf16[256,1664]{1,0:T(8,128)(2,1)S(1)}, bf16[256,1664]{1,0:T(8,128)(2,1)S(1)}) custom-call(s32[2]{0:T(128)S(1)} %pad_add_fusion.ids, bf16[256,2048]{1,0:T(8,128)(2,1)S(1)} %get-tuple-element.47.refs_0_, bf16[2048,6656]{1,0:T(8,128)(2,1)} %refs_1_.19, bf16[2048,6656]{1,0:T(8,128)(2,1)} %refs_2_.19), custom_call_target="tpu_custom_call" | custom-call | tf_op jit(solution)/shard_map/dot_pair/pallas_call | solution.py:216
  181.7 7.8 %dot_pair.20.refs_3_ = bf16[2,256,1664]{2,1,0:T(8,128)(2,1)S(1)} custom-call(s32[2]{0:T(128)S(1)} %pad_add_fusion.ids, bf16[256,2048]{1,0:T(8,128)(2,1)S(1)} %get-tuple-element.47.refs_0_, bf16[2048,6656]{1,0:T(8,128)(2,1)} %refs_1_.19, bf16[2048,6656]{1,0:T(8,128)(2,1)} %refs_2_.19, bf16[256,1664]{1,0:T(8,128)(2,1)S(1)} %collective-permute-done.18.refs_3_, ...), custom_call_target="tpu_custom_call" | custom-call | tf_op jit(solution)/shard_map/dot_pair/pallas_call | solution.py:216
  190.9 7.8 %dot_pair.21 = (bf16[256,1664]{1,0:T(8,128)(2,1)S(1)}, bf16[256,1664]{1,0:T(8,128)(2,1)S(1)}) custom-call(s32[2]{0:T(128)S(1)} %pad_add_fusion.ids, bf16[256,2048]{1,0:T(8,128)(2,1)S(1)} %get-tuple-element.47.refs_0_, bf16[2048,6656]{1,0:T(8,128)(2,1)} %refs_1_.19, bf16[2048,6656]{1,0:T(8,128)(2,1)} %refs_2_.19, bf16[2,256,1664]{2,1,0:T(8,128)(2,1)S(1)} %dot_pair.20.refs_3_), custom_call_target="tpu_custom_call" | custom-call | tf_op jit(solution)/shard_map/dot_pair/pallas_call | solution.py:216
  200.3 17.7 %dot_pair.22 = (f32[512,1664]{1,0:T(8,128)}, f32[512,1664]{1,0:T(8,128)}) custom-call(s32[2]{0:T(128)S(1)} %pad_add_fusion.ids, bf16[128,2048]{1,0:T(8,128)(2,1)S(1)} %get-tuple-element.33.refs_0_, bf16[128,2048]{1,0:T(8,128)(2,1)S(1)} %get-tuple-element.36.refs_0_.refs_1_, bf16[256,2048]{1,0:T(8,128)(2,1)S(1)} %get-tuple-element.43.refs_0_.refs_2_, ...), custom_call_target="tpu_custom_call" | custom-call | tf_op jit(solution)/shard_map/dot_pair/pallas_call | solution.py:216
  219.3 8.0 %dot_pair.23 = (f32[256,1664]{1,0:T(8,128)S(1)}, f32[256,1664]{1,0:T(8,128)S(1)}) custom-call(s32[2]{0:T(128)S(1)} %pad_add_fusion.ids, bf16[256,2048]{1,0:T(8,128)(2,1)S(1)} %get-tuple-element.47.refs_0_, bf16[2048,6656]{1,0:T(8,128)(2,1)} %refs_1_.19, bf16[2048,6656]{1,0:T(8,128)(2,1)} %refs_2_.19, bf16[256,1664]{1,0:T(8,128)(2,1)S(1)} %collective-permute-done.20.refs_3_, ...), custom_call_target="tpu_custom_call" | custom-call | tf_op jit(solution)/shard_map/dot_pair/pallas_call | solution.py:216
  227.3 28.3 %collective-permute-done.27.low_b = f32[192,128]{1,0:T(8,128)S(1)} collective-permute-done((f32[192,128]{1,0:T(8,128)S(1)}, f32[192,128]{1,0:T(8,128)S(1)}, u32[]{:S(2)}, u32[]{:S(2)}) %collective-permute-start.27) | collective-permute-done | bytes 98336 | tf_op jit(solution)/shard_map/ppermute | solution.py:474
  261.7 3.8 %finish_rows.5.refs_2_ = bf16[256,1664]{1,0:T(8,128)(2,1)S(1)} custom-call(s32[2]{0:T(128)S(1)} %pad_add_fusion.ids, s32[8]{0:T(128)S(1)} %copy-done.16, s32[8]{0:T(128)S(1)} %copy-done.17, f32[512,1664]{1,0:T(8,128)} %get-tuple-element.53.refs_5_.gate_sum, f32[512,1664]{1,0:T(8,128)} %get-tuple-element.60.up_sum, bf16[2,256,1664]{2,1,0:T(8,128)(2,1)S(1)} %copy-done.7, ...), custom_call_target="tpu_custom_call" | custom-call | tf_op jit(solution)/shard_map/finish_rows/pallas_call | solution.py:308
  265.6 8.7 %last_rows.1 = bf16[1024,1664]{1,0:T(8,128)(2,1)} custom-call(s32[2]{0:T(128)S(1)} %pad_add_fusion.ids, s32[8]{0:T(128)S(1)} %copy-done.16, s32[8]{0:T(128)S(1)} %copy-done.17, f32[256,1664]{1,0:T(8,128)S(1)} %get-tuple-element.54.refs_0_.gate_sum, f32[256,1664]{1,0:T(8,128)S(1)} %copy-done.15, bf16[2,256,1664]{2,1,0:T(8,128)(2,1)} %collective-permute-done.25.far, ...), custom_call_target="tpu_custom_call" | custom-call | tf_op jit(solution)/shard_map/last_rows/pallas_call | solution.py:380
  (109 shorter events, 47.7 us)
Async XLA Ops:
  2.4 15.8 %collective-permute-start = (bf16[128,2048]{1,0:T(8,128)(2,1)}, bf16[128,2048]{1,0:T(8,128)(2,1)S(1)}, u32[]{:S(2)}, u32[]{:S(2)}) collective-permute-start(bf16[128,2048]{1,0:T(8,128)(2,1)} %get-tuple-element.62), channel_id=1, source_target_pairs={{0,4},{4,8},{8,12},{1,5},{5,9},{9,13},{2,6},{6,10},{10,14},{3,7},{... | collective-permute-start | bytes 1572872 | tf_op jit(solution)/shard_map/ppermute | solution.py:418
  5.8 15.6 %collective-permute-start.1 = (bf16[128,2048]{1,0:T(8,128)(2,1)}, bf16[128,2048]{1,0:T(8,128)(2,1)}, u32[]{:S(2)}, u32[]{:S(2)}) collective-permute-start(bf16[128,2048]{1,0:T(8,128)(2,1)} %get-tuple-element.62), channel_id=1, source_target_pairs={{4,0},{8,4},{12,8},{5,1},{9,5},{13,9},{6,2},{10,6},{14,10},{7,3},{... | collective-permute-start | bytes 1572872 | tf_op jit(solution)/shard_map/ppermute | solution.py:418
  10.8 5.1 %collective-permute-start.5 = (f32[8,2,1664]{2,0,1:T(8,128)S(1)}, f32[8,2,1664]{2,0,1:T(8,128)S(1)}, u32[]{:S(2)}, u32[]{:S(2)}) collective-permute-start(f32[8,2,1664]{2,0,1:T(8,128)S(1)} %slice_bitcast_fusion), channel_id=1, source_target_pairs={{0,2},{1,3},{2,0},{3,1},{4,6},{5,7},{6,4},{7,5},{8,10},{9,11},{10,... | collective-permute-start | bytes 319496 | tf_op jit(solution)/shard_map/ppermute | solution.py:427
  30.2 11.6 %collective-permute-start.6 = (bf16[128,1664]{1,0:T(8,128)(2,1)S(1)}, bf16[128,1664]{1,0:T(8,128)(2,1)S(1)}, u32[]{:S(2)}, u32[]{:S(2)}) collective-permute-start(bf16[128,1664]{1,0:T(8,128)(2,1)S(1)} %get-tuple-element.34), channel_id=1, source_target_pairs={{0,1},{1,0},{2,3},{3,2},{4,5},{5,4},{6,7},{7,6},{8,9},{9,8},{10,11... | collective-permute-start | bytes 1277960 | tf_op jit(solution)/shard_map/ppermute | solution.py:438
  30.3 13.4 %collective-permute-start.7 = (bf16[128,1664]{1,0:T(8,128)(2,1)S(1)}, bf16[128,1664]{1,0:T(8,128)(2,1)S(1)}, u32[]{:S(2)}, u32[]{:S(2)}) collective-permute-start(bf16[128,1664]{1,0:T(8,128)(2,1)S(1)} %get-tuple-element.35), channel_id=1, source_target_pairs={{0,1},{1,0},{2,3},{3,2},{4,5},{5,4},{6,7},{7,6},{8,9},{9,8},{10,11... | collective-permute-start | bytes 1277960 | tf_op jit(solution)/shard_map/ppermute | solution.py:438
  30.8 75.9 %collective-permute-start.10 = (bf16[256,2048]{1,0:T(8,128)(2,1)S(1)}, bf16[256,2048]{1,0:T(8,128)(2,1)}, u32[]{:S(2)}, u32[]{:S(2)}) collective-permute-start(bf16[256,2048]{1,0:T(8,128)(2,1)S(1)} %get-tuple-element.39), channel_id=1, source_target_pairs={{0,8},{4,12},{1,9},{5,13},{2,10},{6,14},{3,11},{7,15},{16,24},{20,... | collective-permute-start | bytes 3145736 | tf_op jit(solution)/shard_map/ppermute | solution.py:418
  34.2 72.5 %collective-permute-start.11 = (bf16[256,2048]{1,0:T(8,128)(2,1)S(1)}, bf16[256,2048]{1,0:T(8,128)(2,1)S(1)}, u32[]{:S(2)}, u32[]{:S(2)}) collective-permute-start(bf16[256,2048]{1,0:T(8,128)(2,1)S(1)} %get-tuple-element.39), channel_id=1, source_target_pairs={{8,0},{12,4},{9,1},{13,5},{10,2},{14,6},{11,3},{15,7},{24,16},{28,... | collective-permute-start | bytes 3145736 | tf_op jit(solution)/shard_map/ppermute | solution.py:418
  35.5 54.1 %collective-permute-start.2 = (bf16[128,2048]{1,0:T(8,128)(2,1)S(1)}, bf16[128,2048]{1,0:T(8,128)(2,1)S(1)}, u32[]{:S(2)}, u32[]{:S(2)}) collective-permute-start(bf16[128,2048]{1,0:T(8,128)(2,1)S(1)} %copy-done.18), channel_id=1, source_target_pairs={{0,4},{4,8},{8,12},{1,5},{5,9},{9,13},{2,6},{6,10},{10,14},{3,7},{... | collective-permute-start | bytes 1572872 | tf_op jit(solution)/shard_map/ppermute | solution.py:418
  41.8 53.8 %collective-permute-start.3 = (bf16[128,2048]{1,0:T(8,128)(2,1)S(1)}, bf16[128,2048]{1,0:T(8,128)(2,1)S(1)}, u32[]{:S(2)}, u32[]{:S(2)}) collective-permute-start(bf16[128,2048]{1,0:T(8,128)(2,1)S(1)} %copy-done.18), channel_id=1, source_target_pairs={{4,0},{8,4},{12,8},{5,1},{9,5},{13,9},{6,2},{10,6},{14,10},{7,3},{... | collective-permute-start | bytes 1572872 | tf_op jit(solution)/shard_map/ppermute | solution.py:418
  50.1 67.1 %collective-permute-start.14 = (bf16[2,128,1664]{2,1,0:T(8,128)(2,1)S(1)}, bf16[2,128,1664]{2,1,0:T(8,128)(2,1)S(1)}, u32[]{:S(2)}, u32[]{:S(2)}) collective-permute-start(bf16[2,128,1664]{2,1,0:T(8,128)(2,1)S(1)} %dot_pair.13.refs_6_), channel_id=1, source_target_pairs={{0,2},{1,3},{2,0},{3,1},{4,6},{5,7},{6,4},{7,5},{8,10},{9,11},{10,... | collective-permute-start | bytes 2555912 | tf_op jit(solution)/shard_map/ppermute | solution.py:444
  113.1 42.4 %collective-permute-start.12 = (bf16[256,2048]{1,0:T(8,128)(2,1)}, bf16[256,2048]{1,0:T(8,128)(2,1)}, u32[]{:S(2)}, u32[]{:S(2)}) collective-permute-start(bf16[256,2048]{1,0:T(8,128)(2,1)} %get-tuple-element.40.refs_5_), channel_id=1, source_target_pairs={{8,12},{9,13},{10,14},{11,15},{24,28},{25,29},{26,30},{27,31}} | collective-permute-start | bytes 3145736 | tf_op jit(solution)/shard_map/ppermute | solution.py:418
  114.8 40.6 %collective-permute-start.13 = (bf16[256,2048]{1,0:T(8,128)(2,1)S(1)}, bf16[256,2048]{1,0:T(8,128)(2,1)}, u32[]{:S(2)}, u32[]{:S(2)}) collective-permute-start(bf16[256,2048]{1,0:T(8,128)(2,1)S(1)} %get-tuple-element.41.refs_6_), channel_id=1, source_target_pairs={{4,0},{5,1},{6,2},{7,3},{20,16},{21,17},{22,18},{23,19}} | collective-permute-start | bytes 3145736 | tf_op jit(solution)/shard_map/ppermute | solution.py:418
  129.7 2.4 collective-permute-start.15
  130.0 3.3 %collective-permute-start.16 = (bf16[256,1664]{1,0:T(8,128)(2,1)S(1)}, bf16[256,1664]{1,0:T(8,128)(2,1)S(1)}, u32[]{:S(2)}, u32[]{:S(2)}) collective-permute-start(bf16[256,1664]{1,0:T(8,128)(2,1)S(1)} %get-tuple-element.45), channel_id=1, source_target_pairs={{0,1},{1,0},{2,3},{3,2},{4,5},{5,4},{6,7},{7,6},{8,9},{9,8},{10,11... | collective-permute-start | bytes 2555912 | tf_op jit(solution)/shard_map/ppermute | solution.py:438
  130.2 25.2 %collective-permute-start.17 = (bf16[2,128,1664]{2,1,0:T(8,128)(2,1)S(1)}, bf16[2,128,1664]{2,1,0:T(8,128)(2,1)S(1)}, u32[]{:S(2)}, u32[]{:S(2)}) collective-permute-start(bf16[2,128,1664]{2,1,0:T(8,128)(2,1)S(1)} %get-tuple-element.42.refs_8_), channel_id=1, source_target_pairs={{0,2},{1,3},{2,0},{3,1},{4,6},{5,7},{6,4},{7,5},{8,10},{9,11},{10,... | collective-permute-start | bytes 2555912 | tf_op jit(solution)/shard_map/ppermute | solution.py:444
  155.1 44.2 %collective-permute-start.22 = (bf16[512,1664]{1,0:T(8,128)(2,1)}, bf16[512,1664]{1,0:T(8,128)(2,1)}, u32[]{:S(2)}, u32[]{:S(2)}) collective-permute-start(bf16[512,1664]{1,0:T(8,128)(2,1)} %get-tuple-element.46.refs_10_), channel_id=1, source_target_pairs={{0,1},{1,0},{2,3},{3,2},{4,5},{5,4},{6,7},{7,6},{8,9},{9,8},{10,11... | collective-permute-start | bytes 5111816 | tf_op jit(solution)/shard_map/ppermute | solution.py:438
  177.1 4.6 %collective-permute-start.19 = (bf16[256,1664]{1,0:T(8,128)(2,1)S(1)}, bf16[256,1664]{1,0:T(8,128)(2,1)S(1)}, u32[]{:S(2)}, u32[]{:S(2)}) collective-permute-start(bf16[256,1664]{1,0:T(8,128)(2,1)S(1)} %get-tuple-element.49), channel_id=1, source_target_pairs={{0,1},{1,0},{2,3},{3,2},{4,5},{5,4},{6,7},{7,6},{8,9},{9,8},{10,11... | collective-permute-start | bytes 2555912 | tf_op jit(solution)/shard_map/ppermute | solution.py:438
  177.4 22.0 %collective-permute-start.23 = (bf16[512,1664]{1,0:T(8,128)(2,1)}, bf16[512,1664]{1,0:T(8,128)(2,1)}, u32[]{:S(2)}, u32[]{:S(2)}) collective-permute-start(bf16[512,1664]{1,0:T(8,128)(2,1)} %get-tuple-element.52), channel_id=1, source_target_pairs={{0,1},{1,0},{2,3},{3,2},{4,5},{5,4},{6,7},{7,6},{8,9},{9,8},{10,11... | collective-permute-start | bytes 5111816 | tf_op jit(solution)/shard_map/ppermute | solution.py:438
  177.6 40.4 %collective-permute-start.24 = (bf16[2,256,1664]{2,1,0:T(8,128)(2,1)S(1)}, bf16[2,256,1664]{2,1,0:T(8,128)(2,1)S(1)}, u32[]{:S(2)}, u32[]{:S(2)}) collective-permute-start(bf16[2,256,1664]{2,1,0:T(8,128)(2,1)S(1)} %copy-done.9), channel_id=1, source_target_pairs={{0,2},{1,3},{2,0},{3,1},{4,6},{5,7},{6,4},{7,5},{8,10},{9,11},{10,... | collective-permute-start | bytes 5111816 | tf_op jit(solution)/shard_map/ppermute | solution.py:444
  189.5 76.1 %collective-permute-start.25 = (bf16[2,256,1664]{2,1,0:T(8,128)(2,1)S(1)}, bf16[2,256,1664]{2,1,0:T(8,128)(2,1)}, u32[]{:S(2)}, u32[]{:S(2)}) collective-permute-start(bf16[2,256,1664]{2,1,0:T(8,128)(2,1)S(1)} %dot_pair.20.refs_3_), channel_id=1, source_target_pairs={{0,2},{1,3},{2,0},{3,1},{4,6},{5,7},{6,4},{7,5},{8,10},{9,11},{10,... | collective-permute-start | bytes 5111816 | tf_op jit(solution)/shard_map/ppermute | solution.py:444
  190.8 8.0 %collective-permute-start.26 = (f32[192,128]{1,0:T(8,128)S(1)}, f32[192,128]{1,0:T(8,128)S(1)}, u32[]{:S(2)}, u32[]{:S(2)}) collective-permute-start(f32[192,128]{1,0:T(8,128)S(1)} %constant_dynamic-update-slice_fusion), channel_id=1, source_target_pairs={{0,1},{1,0},{2,3},{3,2},{4,5},{5,4},{6,7},{7,6},{8,9},{9,8},{10,11... | collective-permute-start | bytes 294920 | tf_op jit(solution)/shard_map/ppermute | solution.py:473
  198.8 19.2 %collective-permute-start.20 = (bf16[256,1664]{1,0:T(8,128)(2,1)S(1)}, bf16[256,1664]{1,0:T(8,128)(2,1)S(1)}, u32[]{:S(2)}, u32[]{:S(2)}) collective-permute-start(bf16[256,1664]{1,0:T(8,128)(2,1)S(1)} %get-tuple-element.50.refs_7_), channel_id=1, source_target_pairs={{0,1},{1,0},{2,3},{3,2},{4,5},{5,4},{6,7},{7,6},{8,9},{9,8},{10,11... | collective-permute-start | bytes 2555912 | tf_op jit(solution)/shard_map/ppermute | solution.py:438
  199.3 18.7 %collective-permute-start.21 = (bf16[256,1664]{1,0:T(8,128)(2,1)S(1)}, bf16[256,1664]{1,0:T(8,128)(2,1)S(1)}, u32[]{:S(2)}, u32[]{:S(2)}) collective-permute-start(bf16[256,1664]{1,0:T(8,128)(2,1)S(1)} %get-tuple-element.51), channel_id=1, source_target_pairs={{0,1},{1,0},{2,3},{3,2},{4,5},{5,4},{6,7},{7,6},{8,9},{9,8},{10,11... | collective-permute-start | bytes 2555912 | tf_op jit(solution)/shard_map/ppermute | solution.py:438
  199.4 56.2 %collective-permute-start.27 = (f32[192,128]{1,0:T(8,128)S(1)}, f32[192,128]{1,0:T(8,128)S(1)}, u32[]{:S(2)}, u32[]{:S(2)}) collective-permute-start(f32[192,128]{1,0:T(8,128)S(1)} %add.28.low_a), channel_id=1, source_target_pairs={{0,2},{1,3},{2,0},{3,1},{4,6},{5,7},{6,4},{7,5},{8,10},{9,11},{10,... | collective-permute-start | bytes 294920 | tf_op jit(solution)/shard_map/ppermute | solution.py:474
  (24 other events, 213.4 us)

commit v3 on v0

--- a/solution.py
+++ b/solution.py
@@ -1,12 +1,438 @@
+import functools
 import math
 
 import jax
 import jax.numpy as jnp
 from jax import lax
+from jax.experimental import pallas as pl
+from jax.experimental.pallas import tpu as pltpu
 from jax.sharding import PartitionSpec as P
 
 RANK = 16
 BLOCK_ROWS = 128
+LIVE_ROWS = 768
+TILE = 256
+VMEM_LIMIT = 52 * 1024 * 1024
+
+SLOTS = tuple((distance, half) for distance in (0, -1, 1, -2, 2, -3, 3) for half in range(2))
+CHUNKS = ((0, 256, 6), (256, 192, 10), (448, 320, 14))
+ANY = pl.BlockSpec(memory_space=pl.ANY)
+COST = pl.CostEstimate(flops=0, bytes_accessed=0, transcendentals=0)
+
+
+def fill_table(table, ids, rows, tenants, mx_count):
+    start = jnp.int32(0)
+    for slot, (distance, half) in enumerate(SLOTS):
+        source = ids[0] + distance
+        valid = (source >= 0) & (source < mx_count)
+        block = jnp.clip(source, 0, mx_count - 1) * 2 + half
+        count = jnp.where(valid, rows[block], 0)
+        table[0, slot] = start
+        table[1, slot] = count
+        table[2, slot] = tenants[block]
+        table[3, slot] = jnp.where(valid, block, -1)
+        start = start + count
+
+
+def pack_kernel(mx_count, first, rows_out, slots, passed, ids, rows, tenants, *refs):
+    token_refs, down_ref = refs[:slots // 2], refs[slots // 2]
+    outs, scratch = refs[-9 - passed:-6], refs[-6:]
+    x_ref, low_ref, pick_ref = outs[:3]
+    table, buffer, down, acc, sems, down_sem = scratch
+    fill_table(table, ids, rows, tenants, mx_count)
+
+    def needed(slot):
+        start, count = table[0, slot], table[1, slot]
+        return (count > 0) & (start < first + rows_out) & (start + count > first)
+
+    for slot in range(slots):
+        @pl.when(needed(slot))
+        def _():
+            here = pl.ds(slot % 2 * BLOCK_ROWS, BLOCK_ROWS)
+            pltpu.make_async_copy(token_refs[slot // 2].at[here], buffer.at[slot], sems.at[slot]).start()
+
+    down_copy = pltpu.make_async_copy(down_ref, down, down_sem)
+    down_copy.start()
+    acc[...] = jnp.zeros_like(acc)
+
+    @pl.loop(0, slots)
+    def _(slot):
+        @pl.when(needed(slot))
+        def _():
+            start, count = table[0, slot], table[1, slot]
+            pltpu.make_async_copy(buffer.at[slot], buffer.at[slot], sems.at[slot]).wait()
+            target = lax.broadcasted_iota(jnp.int32, (rows_out, BLOCK_ROWS), 0) + first
+            position = lax.broadcasted_iota(jnp.int32, (rows_out, BLOCK_ROWS), 1)
+            chosen = (position < count) & (target == position + start)
+            acc[...] += jnp.dot(
+                chosen.astype(jnp.bfloat16), buffer[slot], preferred_element_type=jnp.float32
+            )
+
+    x_ref[...] = acc[...].astype(jnp.bfloat16)
+    row = lax.broadcasted_iota(jnp.int32, (rows_out, 128), 0) + first
+
+    def own(slot, tenant):
+        start, count = table[0, slot], table[1, slot]
+        return jnp.where((row >= start) & (row < start + count), table[2, slot], tenant)
+
+    tenant = lax.fori_loop(0, slots, own, jnp.full((rows_out, 128), -1, jnp.int32))
+    lane = lax.broadcasted_iota(jnp.int32, (rows_out, 128), 1)
+    pick_ref[...] = ((lane % 8 == tenant) & (lane < 24)).astype(jnp.bfloat16)
+
+    down_copy.wait()
+    low = lax.dot_general(x_ref[...], down[...], (((1,), (1,)), ((), ())), preferred_element_type=jnp.float32)
+    owner = jnp.concatenate([lane // 32, lane // 32 + 4], axis=1)
+    low = jnp.where(owner == jnp.concatenate([tenant, tenant], axis=1), low, 0.0)
+    high = low.astype(jnp.bfloat16)
+    rest = (low - high.astype(jnp.float32)).astype(jnp.bfloat16)
+    source = lax.broadcasted_iota(jnp.int32, (256, 256), 0)
+    goal = lax.broadcasted_iota(jnp.int32, (256, 256), 1)
+    place = source // 32 * RANK + source % RANK
+    for side in range(2):
+        mine = source // RANK % 2 == side
+        to_high = (mine & (place == goal)).astype(jnp.bfloat16)
+        to_rest = (mine & (place + 128 == goal)).astype(jnp.bfloat16)
+        moved = jnp.dot(high, to_high, preferred_element_type=jnp.float32)
+        moved += jnp.dot(rest, to_rest, preferred_element_type=jnp.float32)
+        low_ref[side] = moved.astype(jnp.bfloat16)
+
+
+def pack_rows(mx_count, chunk, scalars, tokens, down, after=(), passed=()):
+    first, rows_out, slots = chunk
+    width = down.shape[1]
+    outs = [
+        jax.ShapeDtypeStruct((rows_out, width), jnp.bfloat16),
+        jax.ShapeDtypeStruct((2, rows_out, 256), jnp.bfloat16),
+        jax.ShapeDtypeStruct((rows_out, 128), jnp.bfloat16),
+    ]
+    out_specs = [
+        pl.BlockSpec((rows_out, width), lambda i, *_: (0, 0)),
+        pl.BlockSpec((2, rows_out, 256), lambda i, *_: (0, 0, 0)),
+        pl.BlockSpec((rows_out, 128), lambda i, *_: (0, 0)),
+    ] + [ANY] * len(passed)
+    return pl.pallas_call(
+        functools.partial(pack_kernel, mx_count, first, rows_out, slots, len(passed)),
+        out_shape=outs + [jax.ShapeDtypeStruct(tokens[i].shape, tokens[i].dtype) for i in passed],
+        grid_spec=pltpu.PrefetchScalarGridSpec(
+            num_scalar_prefetch=3,
+            grid=(1,),
+            in_specs=[ANY] * (len(tokens) + 1 + len(after)),
+            out_specs=out_specs,
+            scratch_shapes=[
+                pltpu.SMEM((4, len(SLOTS)), jnp.int32),
+                pltpu.VMEM((slots, BLOCK_ROWS, width), jnp.bfloat16),
+                pltpu.VMEM(down.shape, jnp.bfloat16),
+                pltpu.VMEM((rows_out, width), jnp.float32),
+                pltpu.SemaphoreType.DMA((slots,)),
+                pltpu.SemaphoreType.DMA,
+            ],
+        ),
+        input_output_aliases={3 + place: 3 + i for i, place in enumerate(passed)},
+        compiler_params=pltpu.CompilerParams(vmem_limit_bytes=VMEM_LIMIT),
+        cost_estimate=COST,
+        name="pack_rows",
+    )(*scalars, *tokens, down, *after)
+
+
+def activate(gate, up):
+    return (gate * (1.0 / (1.0 + jnp.exp(-gate))) * up).astype(jnp.bfloat16)
+
+
+def dot_kernel(flip, counts, splits, terms, far_counts, narrow, ids, *refs):
+    parts = len(counts)
+    finish = len(far_counts) > 0
+    x_refs, low_refs, refs = refs[:parts], refs[parts:2 * parts], refs[2 * parts:]
+    w_refs, up_ref, refs = refs[:2], refs[2], refs[3:]
+    term_refs, refs = refs[:2 * terms], refs[2 * terms:]
+    if finish:
+        far_refs, refs = refs[:parts], refs[parts:]
+        pick_refs, scale_ref, refs = refs[:parts], refs[parts], refs[parts + 1:]
+    x, low, w, maps, term, out, far, pick, scale, in_sem, w_sem, out_sem = refs[-12:]
+    outs = refs[-12 - max(1, 2 * len(splits)):-12]
+    rows, depth = x.shape
+    left = pl.multiple_of((ids[1] ^ flip) * narrow, 128)
+    tiles = [(at, min(TILE, narrow - at)) for at in range(0, narrow, TILE)]
+    whole = sum(size == TILE for _, size in tiles)
+
+    loads = []
+
+    def load(source, target):
+        copy = pltpu.make_async_copy(source, target, in_sem.at[len(loads)])
+        copy.start()
+        loads.append(copy)
+
+    row = 0
+    for part, count in enumerate(counts):
+        here = pl.ds(row, count)
+        load(x_refs[part], x.at[here])
+        load(low_refs[part], low.at[:, here])
+        row += count
+
+    def piece(side, at, size, place):
+        return pltpu.make_async_copy(
+            w_refs[side].at[:, pl.ds(pl.multiple_of(left + at, 128), size)],
+            w.at[side, :, pl.ds(at, size)], w_sem.at[side, place],
+        )
+
+    def start_piece(place):
+        for side in range(2):
+            piece(side, *tiles[place], place).start()
+
+    start_piece(0)
+    for side in range(2):
+        for copy in range(2):
+            load(up_ref.at[:, side, :, pl.ds(left, narrow)], maps.at[side, copy])
+    row = 0
+    if terms:
+        count = rows // terms
+        for side in range(2):
+            for part in range(terms):
+                load(term_refs[side * terms + part], term.at[side, pl.ds(part * count, count)])
+    if finish:
+        for part, count in enumerate(counts):
+            here = pl.ds(row, count)
+            load(far_refs[part], far.at[:, here])
+            load(pick_refs[part], pick.at[here])
+            row += count
+        load(scale_ref, scale)
+    for place in range(1, len(tiles)):
+        start_piece(place)
+    for copy in loads:
+        copy.wait()
+
+    def tile(at, size, place):
+        columns = pl.ds(at, size)
+        values = []
+        for side in range(2):
+            piece(side, at, size, place).wait()
+            value = jnp.dot(x[...], w[side, :, columns], preferred_element_type=jnp.float32)
+            value += jnp.dot(
+                low[side], maps[side, :, :, :, columns].reshape(256, size), preferred_element_type=jnp.float32
+            )
+            if terms:
+                value += term[side, :, columns].astype(jnp.float32)
+            if finish:
+                value += far[side, :, columns].astype(jnp.float32)
+                value *= jnp.dot(pick[...], scale[side, :, columns], preferred_element_type=jnp.float32)
+                values.append(value)
+            else:
+                out[side, :, columns] = value.astype(out.dtype)
+        if finish:
+            out[0, :, columns] = activate(*values)
+
+    @pl.loop(0, whole)
+    def _(place):
+        tile(pl.multiple_of(place * TILE, TILE), TILE, place)
+
+    for place in range(whole, len(tiles)):
+        tile(*tiles[place], place)
+
+    copies = []
+
+    def store(source, target):
+        copy = pltpu.make_async_copy(source, target, out_sem.at[len(copies)])
+        copy.start()
+        copies.append(copy)
+
+    if finish:
+        store(out.at[0], outs[0])
+    elif not splits:
+        store(out, outs[0])
+    else:
+        for side in range(2):
+            row = 0
+            for part, count in enumerate(splits):
+                store(out.at[side, pl.ds(row, count)], outs[side * len(splits) + part])
+                row += count
+    for copy in copies:
+        copy.wait()
+
+
+def dot_pair(chunks, weights, adapter_out, flip, narrow, ids, out_dtype, splits=(), terms=(), finish=None, after=()):
+    xs, lows, picks = zip(*chunks)
+    counts = tuple(x.shape[0] for x in xs)
+    rows, depth = sum(counts), xs[0].shape[1]
+    tenants = adapter_out.shape[0]
+    operands = [ids, *xs, *lows, *weights, adapter_out, *terms]
+    if finish is not None:
+        operands += [*finish[0], *picks, finish[1]]
+        out_shape = [jax.ShapeDtypeStruct((rows, narrow), out_dtype)]
+    elif splits:
+        out_shape = [jax.ShapeDtypeStruct((count, narrow), out_dtype) for _ in range(2) for count in splits]
+    else:
+        out_shape = [jax.ShapeDtypeStruct((2, rows, narrow), out_dtype)]
+    operands += list(after)
+    few = (8, 128)
+    pieces = -(-narrow // TILE)
+    return pl.pallas_call(
+        functools.partial(
+            dot_kernel, flip, counts, splits, len(terms) // 2, counts if finish is not None else (), narrow
+        ),
+        out_shape=out_shape,
+        grid_spec=pltpu.PrefetchScalarGridSpec(
+            num_scalar_prefetch=1,
+            grid=(1,),
+            in_specs=[ANY] * (len(operands) - 1),
+            out_specs=[ANY] * len(out_shape),
+            scratch_shapes=[
+                pltpu.VMEM((rows, depth), jnp.bfloat16),
+                pltpu.VMEM((2, rows, 256), jnp.bfloat16),
+                pltpu.VMEM((2, depth, narrow), jnp.bfloat16),
+                pltpu.VMEM((2, 2, tenants, RANK, narrow), jnp.bfloat16),
+                pltpu.VMEM((2, rows, narrow) if terms else few, jnp.bfloat16),
+                pltpu.VMEM((1 if finish is not None else 2, rows, narrow), out_dtype),
+                pltpu.VMEM((2, rows, narrow) if finish is not None else few, jnp.bfloat16),
+                pltpu.VMEM((rows, 128) if finish is not None else few, jnp.bfloat16),
+                pltpu.VMEM((2, 128, narrow) if finish is not None else few, jnp.bfloat16),
+                pltpu.SemaphoreType.DMA((4 * len(xs) + 8,)),
+                pltpu.SemaphoreType.DMA((2, pieces)),
+                pltpu.SemaphoreType.DMA((4,)),
+            ],
+        ),
+        compiler_params=pltpu.CompilerParams(vmem_limit_bytes=VMEM_LIMIT),
+        cost_estimate=COST,
+        name="finish_dots" if finish is not None else "dot_pair",
+    )(*operands)
+
+
+def last_kernel(mx_count, first, ids, rows, tenants, sums, far, pick, scale, earlier, out_ref, table, held):
+    block = pl.program_id(0)
+
+    @pl.when(block == 0)
+    def _():
+        fill_table(table, ids, rows, tenants, mx_count)
+        held[0:first, :] = earlier[...]
+        held[LIVE_ROWS:, :] = jnp.zeros((BLOCK_ROWS, held.shape[1]), held.dtype)
+        columns = held.shape[1]
+
+        @pl.loop(0, far.shape[1] // 64)
+        def _(tile):
+            here = pl.ds(pl.multiple_of(tile * 64, 64), 64)
+            there = pl.ds(pl.multiple_of(first + tile * 64, 64), 64)
+            for left in range(0, columns, TILE):
+                right = min(left + TILE, columns)
+                pre = [
+                    (sums[side, here, left:right] + far[side, here, left:right].astype(jnp.float32))
+                    * jnp.dot(pick[here, :], scale[side, :, left:right], preferred_element_type=jnp.float32)
+                    for side in range(2)
+                ]
+                held[there, left:right] = activate(*pre)
+
+    def find(slot, start):
+        return jnp.where(table[3, slot] == block, table[0, slot], start)
+
+    start = lax.fori_loop(0, len(SLOTS), find, jnp.int32(0))
+    count = rows[block]
+    base = pl.multiple_of(jnp.minimum(start // BLOCK_ROWS * BLOCK_ROWS, LIVE_ROWS - BLOCK_ROWS), BLOCK_ROWS)
+    shape = (BLOCK_ROWS, 2 * BLOCK_ROWS)
+    position = lax.broadcasted_iota(jnp.int32, shape, 0)
+    column = lax.broadcasted_iota(jnp.int32, shape, 1) + base
+    chosen = (position < count) & (column == position + start)
+    out_ref[...] = jnp.dot(
+        chosen.astype(jnp.bfloat16), held[pl.ds(base, 2 * BLOCK_ROWS), :], preferred_element_type=jnp.float32
+    ).astype(jnp.bfloat16)
+
+
+def last_rows(mx_count, first, scalars, sums, far, pick, scale, earlier, blocks):
+    narrow = far.shape[2]
+    operands = (sums, far, pick, scale, earlier)
+    return pl.pallas_call(
+        functools.partial(last_kernel, mx_count, first),
+        out_shape=jax.ShapeDtypeStruct((blocks * BLOCK_ROWS, narrow), jnp.bfloat16),
+        grid_spec=pltpu.PrefetchScalarGridSpec(
+            num_scalar_prefetch=3,
+            grid=(blocks,),
+            in_specs=[
+                pl.BlockSpec(part.shape, lambda i, *_, dims=part.ndim: (0,) * dims) for part in operands
+            ],
+            out_specs=pl.BlockSpec((BLOCK_ROWS, narrow), lambda i, *_: (i, 0)),
+            scratch_shapes=[
+                pltpu.SMEM((4, len(SLOTS)), jnp.int32),
+                pltpu.VMEM((LIVE_ROWS + BLOCK_ROWS, narrow), jnp.bfloat16),
+            ],
+        ),
+        compiler_params=pltpu.CompilerParams(vmem_limit_bytes=VMEM_LIMIT),
+        cost_estimate=COST,
+        name="last_rows",
+    )(*scalars, *operands)
+
+
+def quarter(array, index, narrow):
+    return lax.dynamic_slice_in_dim(array, index * narrow, narrow, array.ndim - 1)
+
+
+def pipelined(
+    tokens, w_gate, w_up, adapter_in, adapter_out, magnitude, partial_norms, block_tenant, block_rows
+):
+    mx_count = lax.axis_size("mx")
+    my_count = lax.axis_size("my")
+    narrow = w_gate.shape[1] // my_count
+    mine = lax.axis_index("my")
+    ids = jnp.stack([lax.axis_index("mx"), mine]).astype(jnp.int32)
+    scalars = (ids, block_rows, block_tenant)
+    near = [(i, i ^ 1) for i in range(my_count)]
+    across = [(i, i ^ 2) for i in range(my_count)]
+
+    def hop(block, distance, least=0):
+        if distance > 0:
+            pairs = [(i, i + distance) for i in range(least, mx_count - distance)]
+        else:
+            pairs = [(i, i + distance) for i in range(-distance, mx_count - least)]
+        return lax.ppermute(block, "mx", pairs)
+
+    blocks = [tokens] + [hop(tokens, distance) for distance in (1, -1, 2, -2)]
+
+    norms = partial_norms[0]
+    pair = jnp.stack([quarter(norms, mine, narrow), quarter(norms, mine ^ 2, narrow)])
+    other = jnp.stack([quarter(norms, mine ^ 1, narrow), quarter(norms, mine ^ 3, narrow)])
+    pair = pair + lax.ppermute(other, "my", near)
+    norm_total = pair[0] + lax.ppermute(pair[1], "my", across)
+    scale = quarter(magnitude, mine, narrow) * lax.rsqrt(norm_total)
+    scale = jnp.transpose(scale, (1, 0, 2))
+    high = lax.reduce_precision(scale, 8, 7)
+    middle = lax.reduce_precision(scale - high, 8, 7)
+    rest = scale - high - middle
+    scale = jnp.concatenate(
+        [high, middle, rest, jnp.zeros((2, 128 - 3 * scale.shape[1], narrow), jnp.float32)], axis=1
+    ).astype(jnp.bfloat16)
+
+    down = jnp.transpose(adapter_in, (0, 2, 1)).reshape(-1, adapter_in.shape[1])
+
+    dots = functools.partial(
+        dot_pair, weights=(w_gate, w_up), adapter_out=adapter_out, narrow=narrow, ids=ids
+    )
+
+    def swap(parts, pairs):
+        return [lax.ppermute(part, "my", pairs) for part in parts]
+
+    def send_far(chunk, pieces=1):
+        rows = chunk[0].shape[0] // pieces
+        parts = dots([chunk], flip=3, out_dtype=jnp.bfloat16, splits=(rows,) * pieces)
+        got = swap(parts, near)
+        part, = dots([chunk], flip=2, out_dtype=jnp.bfloat16, terms=got)
+        return part, lax.ppermute(part, "my", across)
+
+    *chunk0, = pack_rows(mx_count, CHUNKS[0], scalars, blocks[:3], down, after=(scale,))
+    mark, far0 = send_far(chunk0)
+
+    *chunk1, second, third = pack_rows(
+        mx_count, CHUNKS[1], scalars, blocks, down, after=(mark,), passed=(3, 4)
+    )
+    blocks = [*blocks[:3], second, third, hop(second, 1, 2), hop(third, -1, 2)]
+    mark, far1 = send_far(chunk1)
+
+    *chunk2, = pack_rows(mx_count, CHUNKS[2], scalars, blocks, down, after=(mark, far0))
+    mark, far2 = send_far(chunk2, 2)
+
+    first, last = CHUNKS[2][:2]
+    parts = dots([chunk0, chunk1, chunk2], flip=1, out_dtype=jnp.bfloat16, splits=(first, last), after=(mark, far1))
+    early_gate, late_gate, early_up, late_up = swap(parts, near)
+    sums, = dots([chunk2], flip=0, out_dtype=jnp.float32, terms=(late_gate, late_up))
+    hidden, = dots(
+        [chunk0, chunk1], flip=0, out_dtype=jnp.bfloat16, terms=(early_gate, early_up),
+        finish=((far0, far1), scale), after=(sums,),
+    )
+    return last_rows(mx_count, first, scalars, sums, far2, chunk2[2], scale, hidden, block_rows.shape[0])
 
 
 def adapter_low(rows_piece, aligned_row_total, adapter_in, block_tenant):
@@ -22,15 +448,8 @@
     return low_terms.reshape(row_count, tenant_tables.shape[2])
 
 
-def finish(
-    summed,
-    reduced_rank_factor,
-    norm_total,
-    mag_cols,
-    adapter_cols,
-    first_row,
-    block_tenant,
-    block_rows,
+def finish_plain(
+    summed, reduced_rank_factor, norm_total, mag_cols, adapter_cols, first_row, block_tenant, block_rows
 ):
     row_count = summed.shape[0]
     col_count = summed.shape[2]
@@ -55,16 +474,8 @@
     return hidden.reshape(row_count, col_count).astype(jnp.bfloat16)
 
 
-def on_device(
-    tokens,
-    w_gate,
-    w_up,
-    adapter_in,
-    adapter_out,
-    magnitude,
-    partial_norms,
-    block_tenant,
-    block_rows,
+def plain(
+    tokens, w_gate, w_up, adapter_in, adapter_out, magnitude, partial_norms, block_tenant, block_rows
 ):
     local_rows = tokens.shape[0]
     col_local = w_gate.shape[1]
@@ -81,9 +492,21 @@
     narrow = col_local // my_count
     mag_cols = lax.dynamic_slice_in_dim(magnitude, device_position * narrow, narrow, 2)
     adapter_cols = lax.dynamic_slice_in_dim(adapter_out, device_position * narrow, narrow, 3)
-    return finish(
+    return finish_plain(
         summed, reduced_rank_factor, norm_total, mag_cols, adapter_cols, 0, block_tenant, block_rows
     )
+
+
+def on_device(tokens, w_gate, *rest):
+    my_count = lax.axis_size("my")
+    fits = (
+        my_count == 4
+        and lax.axis_size("mx") == 4
+        and tokens.shape[0] == 2 * BLOCK_ROWS
+        and tokens.shape[1] % 512 == 0
+        and w_gate.shape[1] % (my_count * 128) == 0
+    )
+    return (pipelined if fits else plain)(tokens, w_gate, *rest)
 
 
 def solution(mesh):

time: 616 us -> 298 us (0.48)
  waiting for transfers between devices: 378 us -> 60.6 us
  Pallas kernels: 0 us -> 196 us
  matrix products: 94.7 us -> 0 us
  local copies, waits for them, and re-layouts: 66.1 us -> 12.4 us
  other arithmetic: 45.9 us -> 0.3 us
  starting transfers between devices: 0.09 us -> 25.1 us
  between operations: 14.9 us -> 0.47 us
  blocking collectives: 13.7 us -> 0 us
    reduce_scatter x1 -> x0, waiting for transfers between devices: 328 us -> none  [on_device(): summed = lax.psum_scatter(main_part, 'my', scatter_dimension=2, tiled=True)]
    pallas_call x0 -> x13, Pallas kernels: none -> 196 us  [the longest x9 171 us: dot_pair(): pl.pallas_call(functools.partial(dot_kernel, flip, counts, splits, len(te...]
    dot_general x4 -> x0, matrix products: 94.7 us -> none  [the longest x1 40.8 us: on_device(): up_part = jnp.dot(rows_piece, w_up, preferred_element_type=jnp.float32)]
    ppermute x0 -> x23, waiting for transfers between devices: none -> 60.6 us  [the longest x6 42.5 us: hop(): return lax.ppermute(block, 'mx', pairs)]
    all_gather x1 -> x0, waiting for transfers between devices: 48.9 us -> none  [on_device(): rows_piece = lax.all_gather(tokens, 'mx', axis=0, tiled=True)]
    another operation x1 -> x4, other arithmetic: 37.1 us -> 0.14 us  [the longest x1 0.07 us: pipelined(): ids = jnp.stack([lax.axis_index('mx'), mine]).astype(jnp.int32)]
    unnamed x13 -> x50, local copies, waits for them, and re-layouts: 45.7 us -> 11.2 us
    ppermute x0 -> x23, starting transfers between devices: none -> 25.1 us  [the longest x6 15.8 us: hop(): return lax.ppermute(block, 'mx', pairs)]
  transfers between devices with their start and end apart: 3 -> 23, of which waited for: 2 -> 13; matrix products, arithmetic and copies ran while one was open for 29% -> 1% of each run, Pallas kernels for 0% -> 57%
where the time goes in v3:
time: 298 us; the launch traced here: 294 us
  Pallas kernels  196 us (66%)
  waiting for transfers between devices  60.6 us (20%)
  starting transfers between devices  25.1 us (8%)
  local copies, waits for them, and re-layouts  12.4 us (4%)
    pallas_call x9, Pallas kernels, dot_pair(): pl.pallas_call(functools.partial(dot_kernel, flip, counts, splits, len(te...  171 us
    ppermute x6, waiting for transfers between devices, hop(): return lax.ppermute(block, 'mx', pairs)  42.5 us
    ppermute x6, starting transfers between devices, hop(): return lax.ppermute(block, 'mx', pairs)  15.8 us
    pallas_call x3, Pallas kernels, pack_rows(): pl.pallas_call(functools.partial(pack_kernel, mx_count, first, rows_out,...  14.4 us
    ppermute x12, waiting for transfers between devices, swap(): return [lax.ppermute(part, 'my', pairs) for part in parts]  13.3 us
    unnamed x50, local copies, waits for them, and re-layouts  11.2 us
    pallas_call x1, Pallas kernels, last_rows(): pl.pallas_call(functools.partial(last_kernel, mx_count, first), out_shape...  10.4 us
  transfers between devices with their start and end apart: 23, of which 13 were waited for; matrix products, arithmetic and copies ran while one was open for 1% of the time, Pallas kernels for 57%

profile of v3, /device:TPU:8, one launch (start us, length us, event | category | flops | bytes accessed | tf_op | source)
XLA Modules:
  0.0 294.5 jit_solution(6820349138136841865)
XLA Ops:
  0.0 2.0 collective-permute-start.1
  2.1 3.9 %collective-permute-start = (bf16[256,2048]{1,0:T(8,128)(2,1)}, bf16[256,2048]{1,0:T(8,128)(2,1)S(1)}, u32[]{:S(2)}, u32[]{:S(2)}) collective-permute-start(bf16[256,2048]{1,0:T(8,128)(2,1)} %refs_0_.5), channel_id=1, source_target_pairs={{0,4},{4,8},{8,12},{1,5},{5,9},{9,13},{2,6},{6,10},{10,14},{3,7},{... | collective-permute-start | bytes 3145736 | tf_op jit(solution)/shard_map/ppermute | solution.py:381
  10.4 3.4 %collective-permute-done.5 = f32[8,2,1664]{2,0,1:T(8,128)S(1)} collective-permute-done((f32[8,2,1664]{2,0,1:T(8,128)S(1)}, f32[8,2,1664]{2,0,1:T(8,128)S(1)}, u32[]{:S(2)}, u32[]{:S(2)}) %collective-permute-start.5) | collective-permute-done | bytes 106528 | tf_op jit(solution)/shard_map/ppermute | solution.py:389
  14.1 13.1 %collective-permute-done.1.refs_2_ = bf16[256,2048]{1,0:T(8,128)(2,1)S(1)} collective-permute-done((bf16[256,2048]{1,0:T(8,128)(2,1)}, bf16[256,2048]{1,0:T(8,128)(2,1)S(1)}, u32[]{:S(2)}, u32[]{:S(2)}) %collective-permute-start.1) | collective-permute-done | bytes 1048608 | tf_op jit(solution)/shard_map/ppermute | solution.py:381
  30.1 4.4 %pack_rows.3 = (bf16[256,2048]{1,0:T(8,128)(2,1)}, bf16[2,256,256]{2,1,0:T(8,128)(2,1)S(1)}, bf16[256,128]{1,0:T(8,128)(2,1)S(1)}) custom-call(s32[2]{0:T(128)S(1)} %pad_add_fusion.ids, s32[8]{0:T(128)S(1)} %copy-done.8, s32[8]{0:T(128)S(1)} %copy-done.9, bf16[256,2048]{1,0:T(8,128)(2,1)} %refs_0_.5, bf16[256,2048]{1,0:T(8,128)(2,1)} %copy-done.11, ...), custom_call_target="tpu_custom_call" | custom-call | tf_op jit(solution)/shard_map/pack_rows/pallas_call | solution.py:113
  34.5 13.6 %dot_pair.8 = (bf16[256,1664]{1,0:T(8,128)(2,1)S(1)}, bf16[256,1664]{1,0:T(8,128)(2,1)S(1)}) custom-call(s32[2]{0:T(128)S(1)} %pad_add_fusion.ids, bf16[256,2048]{1,0:T(8,128)(2,1)} %get-tuple-element.28.refs_0_, bf16[2,256,256]{2,1,0:T(8,128)(2,1)S(1)} %get-tuple-element.29.refs_1_.refs_3_.refs_2_, bf16[2048,6656]{1,0:T(8,128)(2,1)} %refs_4_.15, ...), custom_call_target="tpu_custom_call" | custom-call | tf_op jit(solution)/shard_map/dot_pair/pallas_call | solution.py:267
  50.0 5.6 %collective-permute-start.2 = (bf16[256,2048]{1,0:T(8,128)(2,1)S(1)}, bf16[256,2048]{1,0:T(8,128)(2,1)S(1)}, u32[]{:S(2)}, u32[]{:S(2)}) collective-permute-start(bf16[256,2048]{1,0:T(8,128)(2,1)S(1)} %copy-done.6), channel_id=1, source_target_pairs={{0,8},{4,12},{1,9},{5,13},{2,10},{6,14},{3,11},{7,15},{16,24},{20,... | collective-permute-start | bytes 3145736 | tf_op jit(solution)/shard_map/ppermute | solution.py:381
  55.6 14.5 %dot_pair.9.refs_6_ = bf16[2,256,1664]{2,1,0:T(8,128)(2,1)} custom-call(s32[2]{0:T(128)S(1)} %pad_add_fusion.ids, bf16[256,2048]{1,0:T(8,128)(2,1)} %get-tuple-element.28.refs_0_, bf16[2,256,256]{2,1,0:T(8,128)(2,1)S(1)} %get-tuple-element.29.refs_1_.refs_3_.refs_2_, bf16[2048,6656]{1,0:T(8,128)(2,1)} %refs_4_.15, bf16[2048,6656]{1,0:T(8,128)(2,1)} %refs_5_.1, ...), custom_call_target="tpu_custom_call" | custom-call | tf_op jit(solution)/shard_map/dot_pair/pallas_call | solution.py:267
  70.1 2.1 collective-permute-start.12
  72.2 4.5 %collective-permute-done.3.refs_4_ = bf16[256,2048]{1,0:T(8,128)(2,1)S(1)} collective-permute-done((bf16[256,2048]{1,0:T(8,128)(2,1)S(1)}, bf16[256,2048]{1,0:T(8,128)(2,1)S(1)}, u32[]{:S(2)}, u32[]{:S(2)}) %collective-permute-start.3) | collective-permute-done | bytes 1048608 | tf_op jit(solution)/shard_map/ppermute | solution.py:381
  76.7 23.0 %collective-permute-done.2.refs_3_ = bf16[256,2048]{1,0:T(8,128)(2,1)S(1)} collective-permute-done((bf16[256,2048]{1,0:T(8,128)(2,1)S(1)}, bf16[256,2048]{1,0:T(8,128)(2,1)S(1)}, u32[]{:S(2)}, u32[]{:S(2)}) %collective-permute-start.2) | collective-permute-done | bytes 1048608 | tf_op jit(solution)/shard_map/ppermute | solution.py:381
  100.6 4.1 %pack_rows.4 = (bf16[192,2048]{1,0:T(8,128)(2,1)S(1)}, bf16[2,192,256]{2,1,0:T(8,128)(2,1)S(1)}, bf16[192,128]{1,0:T(8,128)(2,1)S(1)}, bf16[256,2048]{1,0:T(8,128)(2,1)}, bf16[256,2048]{1,0:T(8,128)(2,1)}) custom-call(s32[2]{0:T(128)S(1)} %pad_add_fusion.ids, s32[8]{0:T(128)S(1)} %copy-done.8, ...), custom_call_target="tpu_custom_call", output_to_operand_aliasing={{3}: (6, {}), {4}: (7, {})} | custom-call | tf_op jit(solution)/shard_map/pack_rows/pallas_call | solution.py:113
  106.4 2.3 collective-permute-start.9
  108.6 11.7 %dot_pair.10 = (bf16[192,1664]{1,0:T(8,128)(2,1)S(1)}, bf16[192,1664]{1,0:T(8,128)(2,1)S(1)}) custom-call(s32[2]{0:T(128)S(1)} %pad_add_fusion.ids, bf16[192,2048]{1,0:T(8,128)(2,1)} %copy-done.4, bf16[2,192,256]{2,1,0:T(8,128)(2,1)S(1)} %get-tuple-element.35.refs_1_.refs_4_.refs_3_, bf16[2048,6656]{1,0:T(8,128)(2,1)} %refs_4_.15, ...), custom_call_target="tpu_custom_call" | custom-call | tf_op jit(solution)/shard_map/dot_pair/pallas_call | solution.py:267
  123.4 12.4 %dot_pair.11.refs_8_ = bf16[2,192,1664]{2,1,0:T(8,128)(2,1)} custom-call(s32[2]{0:T(128)S(1)} %pad_add_fusion.ids, bf16[192,2048]{1,0:T(8,128)(2,1)} %copy-done.4, bf16[2,192,256]{2,1,0:T(8,128)(2,1)S(1)} %get-tuple-element.35.refs_1_.refs_4_.refs_3_, bf16[2048,6656]{1,0:T(8,128)(2,1)} %refs_4_.15, bf16[2048,6656]{1,0:T(8,128)(2,1)} %refs_5_.1, ...), custom_call_target="tpu_custom_call" | custom-call | tf_op jit(solution)/shard_map/dot_pair/pallas_call | solution.py:267
  135.8 2.0 collective-permute-start.17
  140.3 5.9 %pack_rows.5 = (bf16[320,2048]{1,0:T(8,128)(2,1)}, bf16[2,320,256]{2,1,0:T(8,128)(2,1)S(1)}, bf16[320,128]{1,0:T(8,128)(2,1)S(1)}) custom-call(s32[2]{0:T(128)S(1)} %pad_add_fusion.ids, s32[8]{0:T(128)S(1)} %copy-done.8, s32[8]{0:T(128)S(1)} %copy-done.9, bf16[256,2048]{1,0:T(8,128)(2,1)S(1)} %copy-done.7, bf16[256,2048]{1,0:T(8,128)(2,1)} %copy-done.11, ...), custom_call_target="tpu_custom_call" | custom-call | tf_op jit(solution)/shard_map/pack_rows/pallas_call | solution.py:113
  146.2 17.0 %dot_pair.12 = (bf16[160,1664]{1,0:T(8,128)(2,1)S(1)}, bf16[160,1664]{1,0:T(8,128)(2,1)S(1)}, bf16[160,1664]{1,0:T(8,128)(2,1)S(1)}, bf16[160,1664]{1,0:T(8,128)(2,1)}) custom-call(s32[2]{0:T(128)S(1)} %pad_add_fusion.ids, bf16[320,2048]{1,0:T(8,128)(2,1)} %get-tuple-element.38.refs_0_.refs_2_, bf16[2,320,256]{2,1,0:T(8,128)(2,1)S(1)} %get-tuple-element.39.refs_1_.refs_5_, ...), custom_call_target="tpu_custom_call" | custom-call | tf_op jit(solution)/shard_map/dot_pair/pallas_call | solution.py:267
  168.3 20.3 %dot_pair.13.refs_9_ = bf16[2,320,1664]{2,1,0:T(8,128)(2,1)} custom-call(s32[2]{0:T(128)S(1)} %pad_add_fusion.ids, bf16[320,2048]{1,0:T(8,128)(2,1)} %get-tuple-element.38.refs_0_.refs_2_, bf16[2,320,256]{2,1,0:T(8,128)(2,1)S(1)} %get-tuple-element.39.refs_1_.refs_5_, bf16[2048,6656]{1,0:T(8,128)(2,1)} %refs_4_.15, bf16[2048,6656]{1,0:T(8,128)(2,1)} %refs_5_.1, ...), custom_call_target="tpu_custom_call" | custom-call | tf_op jit(solution)/shard_map/dot_pair/pallas_call | solution.py:267
  190.0 33.7 %dot_pair.14 = (bf16[448,1664]{1,0:T(8,128)(2,1)}, bf16[320,1664]{1,0:T(8,128)(2,1)}, bf16[448,1664]{1,0:T(8,128)(2,1)}, bf16[320,1664]{1,0:T(8,128)(2,1)}) custom-call(s32[2]{0:T(128)S(1)} %pad_add_fusion.ids, bf16[256,2048]{1,0:T(8,128)(2,1)} %get-tuple-element.28.refs_0_, bf16[192,2048]{1,0:T(8,128)(2,1)S(1)} %copy-done.5, ...), custom_call_target="tpu_custom_call" | custom-call | tf_op jit(solution)/shard_map/dot_pair/pallas_call | solution.py:267
  224.8 6.1 %collective-permute-done.18.refs_5_ = bf16[320,1664]{1,0:T(8,128)(2,1)S(1)} collective-permute-done((bf16[320,1664]{1,0:T(8,128)(2,1)}, bf16[320,1664]{1,0:T(8,128)(2,1)S(1)}, u32[]{:S(2)}, u32[]{:S(2)}) %collective-permute-start.18) | collective-permute-done | bytes 1064992 | tf_op jit(solution)/shard_map/ppermute | solution.py:406
  233.5 21.5 %dot_pair.15.refs_14_.sums = f32[2,320,1664]{2,1,0:T(8,128)} custom-call(s32[2]{0:T(128)S(1)} %pad_add_fusion.ids, bf16[320,2048]{1,0:T(8,128)(2,1)} %get-tuple-element.38.refs_0_.refs_2_, bf16[2,320,256]{2,1,0:T(8,128)(2,1)S(1)} %get-tuple-element.39.refs_1_.refs_5_, bf16[2048,6656]{1,0:T(8,128)(2,1)} %refs_4_.15, bf16[2048,6656]{1,0:T(8,128)(2,1)} %refs_5_.1, ...), custom_call_target="tpu_custom_call" | custom-call | tf_op jit(solution)/shard_map/dot_pair/pallas_call | solution.py:267
  256.6 26.2 %finish_dots.1.earlier = bf16[448,1664]{1,0:T(8,128)(2,1)} custom-call(s32[2]{0:T(128)S(1)} %pad_add_fusion.ids, bf16[256,2048]{1,0:T(8,128)(2,1)} %get-tuple-element.28.refs_0_, bf16[192,2048]{1,0:T(8,128)(2,1)S(1)} %copy-done.5, bf16[2,256,256]{2,1,0:T(8,128)(2,1)S(1)} %get-tuple-element.29.refs_1_.refs_3_.refs_2_, ...), custom_call_target="tpu_custom_call" | custom-call | tf_op jit(solution)/shard_map/finish_dots/pallas_call | solution.py:267
  284.1 10.4 %last_rows.1 = bf16[1024,1664]{1,0:T(8,128)(2,1)} custom-call(s32[2]{0:T(128)S(1)} %pad_add_fusion.ids, s32[8]{0:T(128)S(1)} %copy-done.8, s32[8]{0:T(128)S(1)} %copy-done.9, f32[2,320,1664]{2,1,0:T(8,128)} %dot_pair.15.refs_14_.sums, bf16[2,320,1664]{2,1,0:T(8,128)(2,1)} %copy-done.16, bf16[320,128]{1,0:T(8,128)(2,1)S(1)} %get-tuple-element.46.pick, ...), custom_call_target="tpu_custom_call" | custom-call | tf_op jit(solution)/shard_map/last_rows/pallas_call | solution.py:339
  (96 shorter events, 30.3 us)
Async XLA Ops:
  0.0 27.1 %collective-permute-start.1 = (bf16[256,2048]{1,0:T(8,128)(2,1)}, bf16[256,2048]{1,0:T(8,128)(2,1)S(1)}, u32[]{:S(2)}, u32[]{:S(2)}) collective-permute-start(bf16[256,2048]{1,0:T(8,128)(2,1)} %refs_0_.5), channel_id=1, source_target_pairs={{4,0},{8,4},{12,8},{5,1},{9,5},{13,9},{6,2},{10,6},{14,10},{7,3},{... | collective-permute-start | bytes 3145736 | tf_op jit(solution)/shard_map/ppermute | solution.py:381
  2.1 27.0 %collective-permute-start = (bf16[256,2048]{1,0:T(8,128)(2,1)}, bf16[256,2048]{1,0:T(8,128)(2,1)S(1)}, u32[]{:S(2)}, u32[]{:S(2)}) collective-permute-start(bf16[256,2048]{1,0:T(8,128)(2,1)} %refs_0_.5), channel_id=1, source_target_pairs={{0,4},{4,8},{8,12},{1,5},{5,9},{9,13},{2,6},{6,10},{10,14},{3,7},{... | collective-permute-start | bytes 3145736 | tf_op jit(solution)/shard_map/ppermute | solution.py:381
  7.2 1.5 collective-permute-start.4
  8.8 5.1 %collective-permute-start.5 = (f32[8,2,1664]{2,0,1:T(8,128)S(1)}, f32[8,2,1664]{2,0,1:T(8,128)S(1)}, u32[]{:S(2)}, u32[]{:S(2)}) collective-permute-start(f32[8,2,1664]{2,0,1:T(8,128)S(1)} %slice_bitcast_fusion), channel_id=1, source_target_pairs={{0,2},{1,3},{2,0},{3,1},{4,6},{5,7},{6,4},{7,5},{8,10},{9,11},{10,... | collective-permute-start | bytes 319496 | tf_op jit(solution)/shard_map/ppermute | solution.py:389
  48.1 7.5 %collective-permute-start.6 = (bf16[256,1664]{1,0:T(8,128)(2,1)S(1)}, bf16[256,1664]{1,0:T(8,128)(2,1)S(1)}, u32[]{:S(2)}, u32[]{:S(2)}) collective-permute-start(bf16[256,1664]{1,0:T(8,128)(2,1)S(1)} %get-tuple-element.30), channel_id=1, source_target_pairs={{0,1},{1,0},{2,3},{3,2},{4,5},{5,4},{6,7},{7,6},{8,9},{9,8},{10,11... | collective-permute-start | bytes 2555912 | tf_op jit(solution)/shard_map/ppermute | solution.py:406
  48.2 7.4 %collective-permute-start.7 = (bf16[256,1664]{1,0:T(8,128)(2,1)S(1)}, bf16[256,1664]{1,0:T(8,128)(2,1)S(1)}, u32[]{:S(2)}, u32[]{:S(2)}) collective-permute-start(bf16[256,1664]{1,0:T(8,128)(2,1)S(1)} %get-tuple-element.31), channel_id=1, source_target_pairs={{0,1},{1,0},{2,3},{3,2},{4,5},{5,4},{6,7},{7,6},{8,9},{9,8},{10,11... | collective-permute-start | bytes 2555912 | tf_op jit(solution)/shard_map/ppermute | solution.py:406
  48.7 28.0 %collective-permute-start.3 = (bf16[256,2048]{1,0:T(8,128)(2,1)S(1)}, bf16[256,2048]{1,0:T(8,128)(2,1)S(1)}, u32[]{:S(2)}, u32[]{:S(2)}) collective-permute-start(bf16[256,2048]{1,0:T(8,128)(2,1)S(1)} %copy-done.6), channel_id=1, source_target_pairs={{8,0},{12,4},{9,1},{13,5},{10,2},{14,6},{11,3},{15,7},{24,16},{28,... | collective-permute-start | bytes 3145736 | tf_op jit(solution)/shard_map/ppermute | solution.py:381
  50.0 49.7 %collective-permute-start.2 = (bf16[256,2048]{1,0:T(8,128)(2,1)S(1)}, bf16[256,2048]{1,0:T(8,128)(2,1)S(1)}, u32[]{:S(2)}, u32[]{:S(2)}) collective-permute-start(bf16[256,2048]{1,0:T(8,128)(2,1)S(1)} %copy-done.6), channel_id=1, source_target_pairs={{0,8},{4,12},{1,9},{5,13},{2,10},{6,14},{3,11},{7,15},{16,24},{20,... | collective-permute-start | bytes 3145736 | tf_op jit(solution)/shard_map/ppermute | solution.py:381
  70.1 67.7 %collective-permute-start.12 = (bf16[2,256,1664]{2,1,0:T(8,128)(2,1)}, bf16[2,256,1664]{2,1,0:T(8,128)(2,1)S(1)}, u32[]{:S(2)}, u32[]{:S(2)}) collective-permute-start(bf16[2,256,1664]{2,1,0:T(8,128)(2,1)} %dot_pair.9.refs_6_), channel_id=1, source_target_pairs={{0,2},{1,3},{2,0},{3,1},{4,6},{5,7},{6,4},{7,5},{8,10},{9,11},{10,... | collective-permute-start | bytes 5111816 | tf_op jit(solution)/shard_map/ppermute | solution.py:413
  105.6 32.1 %collective-permute-start.8 = (bf16[256,2048]{1,0:T(8,128)(2,1)}, bf16[256,2048]{1,0:T(8,128)(2,1)S(1)}, u32[]{:S(2)}, u32[]{:S(2)}) collective-permute-start(bf16[256,2048]{1,0:T(8,128)(2,1)} %get-tuple-element.32.refs_3_), channel_id=1, source_target_pairs={{8,12},{9,13},{10,14},{11,15},{24,28},{25,29},{26,30},{27,31}} | collective-permute-start | bytes 3145736 | tf_op jit(solution)/shard_map/ppermute | solution.py:381
  106.4 31.4 %collective-permute-start.9 = (bf16[256,2048]{1,0:T(8,128)(2,1)}, bf16[256,2048]{1,0:T(8,128)(2,1)S(1)}, u32[]{:S(2)}, u32[]{:S(2)}) collective-permute-start(bf16[256,2048]{1,0:T(8,128)(2,1)} %get-tuple-element.33.refs_4_), channel_id=1, source_target_pairs={{4,0},{5,1},{6,2},{7,3},{20,16},{21,17},{22,18},{23,19}} | collective-permute-start | bytes 3145736 | tf_op jit(solution)/shard_map/ppermute | solution.py:381
  120.3 2.1 collective-permute-start.10
  120.4 3.0 %collective-permute-start.11 = (bf16[192,1664]{1,0:T(8,128)(2,1)S(1)}, bf16[192,1664]{1,0:T(8,128)(2,1)S(1)}, u32[]{:S(2)}, u32[]{:S(2)}) collective-permute-start(bf16[192,1664]{1,0:T(8,128)(2,1)S(1)} %get-tuple-element.37), channel_id=1, source_target_pairs={{0,1},{1,0},{2,3},{3,2},{4,5},{5,4},{6,7},{7,6},{8,9},{9,8},{10,11... | collective-permute-start | bytes 1916936 | tf_op jit(solution)/shard_map/ppermute | solution.py:406
  135.8 53.2 %collective-permute-start.17 = (bf16[2,192,1664]{2,1,0:T(8,128)(2,1)}, bf16[2,192,1664]{2,1,0:T(8,128)(2,1)S(1)}, u32[]{:S(2)}, u32[]{:S(2)}) collective-permute-start(bf16[2,192,1664]{2,1,0:T(8,128)(2,1)} %dot_pair.11.refs_8_), channel_id=1, source_target_pairs={{0,2},{1,3},{2,0},{3,1},{4,6},{5,7},{6,4},{7,5},{8,10},{9,11},{10,... | collective-permute-start | bytes 3833864 | tf_op jit(solution)/shard_map/ppermute | solution.py:413
  163.2 2.0 collective-permute-start.13
  163.3 3.4 %collective-permute-start.14 = (bf16[160,1664]{1,0:T(8,128)(2,1)S(1)}, bf16[160,1664]{1,0:T(8,128)(2,1)S(1)}, u32[]{:S(2)}, u32[]{:S(2)}) collective-permute-start(bf16[160,1664]{1,0:T(8,128)(2,1)S(1)} %get-tuple-element.41), channel_id=1, source_target_pairs={{0,1},{1,0},{2,3},{3,2},{4,5},{5,4},{6,7},{7,6},{8,9},{9,8},{10,11... | collective-permute-start | bytes 1597448 | tf_op jit(solution)/shard_map/ppermute | solution.py:406
  163.8 3.7 %collective-permute-start.15 = (bf16[160,1664]{1,0:T(8,128)(2,1)S(1)}, bf16[160,1664]{1,0:T(8,128)(2,1)S(1)}, u32[]{:S(2)}, u32[]{:S(2)}) collective-permute-start(bf16[160,1664]{1,0:T(8,128)(2,1)S(1)} %get-tuple-element.42), channel_id=1, source_target_pairs={{0,1},{1,0},{2,3},{3,2},{4,5},{5,4},{6,7},{7,6},{8,9},{9,8},{10,11... | collective-permute-start | bytes 1597448 | tf_op jit(solution)/shard_map/ppermute | solution.py:406
  163.9 3.6 %collective-permute-start.16 = (bf16[160,1664]{1,0:T(8,128)(2,1)}, bf16[160,1664]{1,0:T(8,128)(2,1)S(1)}, u32[]{:S(2)}, u32[]{:S(2)}) collective-permute-start(bf16[160,1664]{1,0:T(8,128)(2,1)} %get-tuple-element.43), channel_id=1, source_target_pairs={{0,1},{1,0},{2,3},{3,2},{4,5},{5,4},{6,7},{7,6},{8,9},{9,8},{10,11... | collective-permute-start | bytes 1597448 | tf_op jit(solution)/shard_map/ppermute | solution.py:406
  188.6 94.1 %collective-permute-start.20 = (bf16[2,320,1664]{2,1,0:T(8,128)(2,1)}, bf16[2,320,1664]{2,1,0:T(8,128)(2,1)S(1)}, u32[]{:S(2)}, u32[]{:S(2)}) collective-permute-start(bf16[2,320,1664]{2,1,0:T(8,128)(2,1)} %dot_pair.13.refs_9_), channel_id=1, source_target_pairs={{0,2},{1,3},{2,0},{3,1},{4,6},{5,7},{6,4},{7,5},{8,10},{9,11},{10,... | collective-permute-start | bytes 6389768 | tf_op jit(solution)/shard_map/ppermute | solution.py:413
  223.7 31.2 %collective-permute-start.21 = (bf16[448,1664]{1,0:T(8,128)(2,1)}, bf16[448,1664]{1,0:T(8,128)(2,1)S(1)}, u32[]{:S(2)}, u32[]{:S(2)}) collective-permute-start(bf16[448,1664]{1,0:T(8,128)(2,1)} %get-tuple-element.47), channel_id=1, source_target_pairs={{0,1},{1,0},{2,3},{3,2},{4,5},{5,4},{6,7},{7,6},{8,9},{9,8},{10,11... | collective-permute-start | bytes 4472840 | tf_op jit(solution)/shard_map/ppermute | solution.py:406
  223.8 31.2 %collective-permute-start.22 = (bf16[448,1664]{1,0:T(8,128)(2,1)}, bf16[448,1664]{1,0:T(8,128)(2,1)S(1)}, u32[]{:S(2)}, u32[]{:S(2)}) collective-permute-start(bf16[448,1664]{1,0:T(8,128)(2,1)} %get-tuple-element.48), channel_id=1, source_target_pairs={{0,1},{1,0},{2,3},{3,2},{4,5},{5,4},{6,7},{7,6},{8,9},{9,8},{10,11... | collective-permute-start | bytes 4472840 | tf_op jit(solution)/shard_map/ppermute | solution.py:406
  224.3 6.6 %collective-permute-start.18 = (bf16[320,1664]{1,0:T(8,128)(2,1)}, bf16[320,1664]{1,0:T(8,128)(2,1)S(1)}, u32[]{:S(2)}, u32[]{:S(2)}) collective-permute-start(bf16[320,1664]{1,0:T(8,128)(2,1)} %get-tuple-element.44), channel_id=1, source_target_pairs={{0,1},{1,0},{2,3},{3,2},{4,5},{5,4},{6,7},{7,6},{8,9},{9,8},{10,11... | collective-permute-start | bytes 3194888 | tf_op jit(solution)/shard_map/ppermute | solution.py:406
  224.4 8.1 %collective-permute-start.19 = (bf16[320,1664]{1,0:T(8,128)(2,1)}, bf16[320,1664]{1,0:T(8,128)(2,1)S(1)}, u32[]{:S(2)}, u32[]{:S(2)}) collective-permute-start(bf16[320,1664]{1,0:T(8,128)(2,1)} %get-tuple-element.45), channel_id=1, source_target_pairs={{0,1},{1,0},{2,3},{3,2},{4,5},{5,4},{6,7},{7,6},{8,9},{9,8},{10,11... | collective-permute-start | bytes 3194888 | tf_op jit(solution)/shard_map/ppermute | solution.py:406
  256.6 27.6 %copy-start.3 = (bf16[2,128,1664]{2,1,0:T(8,128)(2,1)S(1)}, bf16[2,128,1664]{2,1,0:T(8,128)(2,1)}, u32[]{:S(2)}) copy-start(bf16[2,128,1664]{2,1,0:T(8,128)(2,1)} %copy-done.2) | copy-start | bytes 2555908
  (22 other events, 182.3 us)

commit v4 on v3

--- a/solution.py
+++ b/solution.py
@@ -12,7 +12,7 @@
 BLOCK_ROWS = 128
 LIVE_ROWS = 768
 TILE = 256
-VMEM_LIMIT = 52 * 1024 * 1024
+VMEM_LIMIT = 60 * 1024 * 1024
 
 SLOTS = tuple((distance, half) for distance in (0, -1, 1, -2, 2, -3, 3) for half in range(2))
 CHUNKS = ((0, 256, 6), (256, 192, 10), (448, 320, 14))
@@ -171,7 +171,7 @@
     def piece(side, at, size, place):
         return pltpu.make_async_copy(
             w_refs[side].at[:, pl.ds(pl.multiple_of(left + at, 128), size)],
-            w.at[side, :, pl.ds(at, size)], w_sem.at[side, place],
+            w.at[place, :, pl.ds(side * size, size)], w_sem.at[side, place],
         )
 
     def start_piece(place):
@@ -205,7 +205,9 @@
         values = []
         for side in range(2):
             piece(side, at, size, place).wait()
-            value = jnp.dot(x[...], w[side, :, columns], preferred_element_type=jnp.float32)
+        both = jnp.dot(x[...], w[place, :, 0:2 * size], preferred_element_type=jnp.float32)
+        for side in range(2):
+            value = both[:, side * size:(side + 1) * size]
             value += jnp.dot(
                 low[side], maps[side, :, :, :, columns].reshape(256, size), preferred_element_type=jnp.float32
             )
@@ -277,7 +279,7 @@
             scratch_shapes=[
                 pltpu.VMEM((rows, depth), jnp.bfloat16),
                 pltpu.VMEM((2, rows, 256), jnp.bfloat16),
-                pltpu.VMEM((2, depth, narrow), jnp.bfloat16),
+                pltpu.VMEM((pieces, depth, 2 * TILE), jnp.bfloat16),
                 pltpu.VMEM((2, 2, tenants, RANK, narrow), jnp.bfloat16),
                 pltpu.VMEM((2, rows, narrow) if terms else few, jnp.bfloat16),
                 pltpu.VMEM((1 if finish is not None else 2, rows, narrow), out_dtype),
@@ -380,7 +382,8 @@
             pairs = [(i, i + distance) for i in range(-distance, mx_count - least)]
         return lax.ppermute(block, "mx", pairs)
 
-    blocks = [tokens] + [hop(tokens, distance) for distance in (1, -1, 2, -2)]
+    first_up, first_down = hop(tokens, 1), hop(tokens, -1)
+    blocks = [tokens, first_up, first_down, hop(first_up, 1, 1), hop(first_down, -1, 1)]
 
     norms = partial_norms[0]
     pair = jnp.stack([quarter(norms, mine, narrow), quarter(norms, mine ^ 2, narrow)])

time: 298 us -> 228 us (0.77)
  Pallas kernels: 196 us -> 153 us
  waiting for transfers between devices: 60.6 us -> 38.1 us
  local copies, waits for them, and re-layouts: 12.4 us -> 7.67 us
    pallas_call x9, Pallas kernels: 171 us -> 126 us  [dot_pair(): pl.pallas_call(functools.partial(dot_kernel, flip, counts, splits, len(te...]
    ppermute x6, waiting for transfers between devices: 42.5 us -> 19.9 us  [hop(): return lax.ppermute(block, 'mx', pairs)]
    unnamed x50 -> x40, local copies, waits for them, and re-layouts: 11.2 us -> 6.47 us
  transfers between devices with their start and end apart: 23 -> 23, of which waited for: 13 -> 14; matrix products, arithmetic and copies ran while one was open for 1% -> 1% of each run, Pallas kernels for 57% -> 56%
where the time goes in v4:
time: 228 us; the launch traced here: 226 us
  Pallas kernels  153 us (67%)
  waiting for transfers between devices  38.1 us (17%)
  starting transfers between devices  24.9 us (11%)
  local copies, waits for them, and re-layouts  7.67 us (3%)
    pallas_call x9, Pallas kernels, dot_pair(): pl.pallas_call(functools.partial(dot_kernel, flip, counts, splits, len(te...  126 us
    ppermute x6, waiting for transfers between devices, hop(): return lax.ppermute(block, 'mx', pairs)  19.9 us
    pallas_call x3, Pallas kernels, pack_rows(): pl.pallas_call(functools.partial(pack_kernel, mx_count, first, rows_out,...  16.5 us
    ppermute x6, starting transfers between devices, hop(): return lax.ppermute(block, 'mx', pairs)  15.7 us
    ppermute x12, waiting for transfers between devices, swap(): return [lax.ppermute(part, 'my', pairs) for part in parts]  13.9 us
    pallas_call x1, Pallas kernels, last_rows(): pl.pallas_call(functools.partial(last_kernel, mx_count, first), out_shape...  10.9 us
    unnamed x40, local copies, waits for them, and re-layouts  6.47 us
  transfers between devices with their start and end apart: 23, of which 14 were waited for; matrix products, arithmetic and copies ran while one was open for 1% of the time, Pallas kernels for 56%

profile of v4, /device:TPU:8, one launch (start us, length us, event | category | flops | bytes accessed | tf_op | source)
XLA Modules:
  0.0 225.7 jit_solution(14583681350582480755)
XLA Ops:
  0.0 2.0 collective-permute-start.1
  2.1 3.9 %collective-permute-start = (bf16[256,2048]{1,0:T(8,128)(2,1)}, bf16[256,2048]{1,0:T(8,128)(2,1)S(1)}, u32[]{:S(2)}, u32[]{:S(2)}) collective-permute-start(bf16[256,2048]{1,0:T(8,128)(2,1)} %refs_0_.5), channel_id=1, source_target_pairs={{0,4},{4,8},{8,12},{1,5},{5,9},{9,13},{2,6},{6,10},{10,14},{3,7},{... | collective-permute-start | bytes 3145736 | tf_op jit(solution)/shard_map/ppermute | solution.py:383
  10.9 3.0 %collective-permute-done.5 = f32[8,2,1664]{2,0,1:T(8,128)S(1)} collective-permute-done((f32[8,2,1664]{2,0,1:T(8,128)S(1)}, f32[8,2,1664]{2,0,1:T(8,128)S(1)}, u32[]{:S(2)}, u32[]{:S(2)}) %collective-permute-start.5) | collective-permute-done | bytes 106528 | tf_op jit(solution)/shard_map/ppermute | solution.py:392
  14.9 12.2 %collective-permute-done.1.refs_2_ = bf16[256,2048]{1,0:T(8,128)(2,1)S(1)} collective-permute-done((bf16[256,2048]{1,0:T(8,128)(2,1)}, bf16[256,2048]{1,0:T(8,128)(2,1)S(1)}, u32[]{:S(2)}, u32[]{:S(2)}) %collective-permute-start.1) | collective-permute-done | bytes 1048608 | tf_op jit(solution)/shard_map/ppermute | solution.py:383
  30.1 5.2 %pack_rows.3 = (bf16[256,2048]{1,0:T(8,128)(2,1)}, bf16[2,256,256]{2,1,0:T(8,128)(2,1)}, bf16[256,128]{1,0:T(8,128)(2,1)}) custom-call(s32[2]{0:T(128)} %pad_add_fusion.ids, s32[8]{0:T(128)} %rows.7, s32[8]{0:T(128)} %tenants.7, bf16[256,2048]{1,0:T(8,128)(2,1)} %refs_0_.5, bf16[256,2048]{1,0:T(8,128)(2,1)} %copy-done.4, bf16[256,2048]{1,0:T(8,128)(2,1)} %copy-done.2, ...), custom_call_target="tpu_custom_call" | custom-call | tf_op jit(solution)/shard_map/pack_rows/pallas_call | solution.py:113
  35.3 9.9 %dot_pair.8 = (bf16[256,1664]{1,0:T(8,128)(2,1)}, bf16[256,1664]{1,0:T(8,128)(2,1)}) custom-call(s32[2]{0:T(128)} %pad_add_fusion.ids, bf16[256,2048]{1,0:T(8,128)(2,1)} %get-tuple-element.28.refs_0_, bf16[2,256,256]{2,1,0:T(8,128)(2,1)} %get-tuple-element.29.refs_1_.refs_3_.refs_2_, bf16[2048,6656]{1,0:T(8,128)(2,1)} %refs_4_.15, ...), custom_call_target="tpu_custom_call" | custom-call | tf_op jit(solution)/shard_map/dot_pair/pallas_call | solution.py:269
  47.7 5.0 %collective-permute-start.2 = (bf16[256,2048]{1,0:T(8,128)(2,1)S(1)}, bf16[256,2048]{1,0:T(8,128)(2,1)}, u32[]{:S(2)}, u32[]{:S(2)}) collective-permute-start(bf16[256,2048]{1,0:T(8,128)(2,1)S(1)} %copy-done.5), channel_id=1, source_target_pairs={{4,8},{8,12},{5,9},{9,13},{6,10},{10,14},{7,11},{11,15},{20,24},{2... | collective-permute-start | bytes 3145736 | tf_op jit(solution)/shard_map/ppermute | solution.py:383
  52.7 13.6 %dot_pair.9.refs_6_ = bf16[2,256,1664]{2,1,0:T(8,128)(2,1)} custom-call(s32[2]{0:T(128)} %pad_add_fusion.ids, bf16[256,2048]{1,0:T(8,128)(2,1)} %get-tuple-element.28.refs_0_, bf16[2,256,256]{2,1,0:T(8,128)(2,1)} %get-tuple-element.29.refs_1_.refs_3_.refs_2_, bf16[2048,6656]{1,0:T(8,128)(2,1)} %refs_4_.15, bf16[2048,6656]{1,0:T(8,128)(2,1)} %refs_5_.1, ...), custom_call_target="tpu_custom_call" | custom-call | tf_op jit(solution)/shard_map/dot_pair/pallas_call | solution.py:269
  66.3 2.0 collective-permute-start.12
  68.3 4.5 %collective-permute-done.3.refs_4_ = bf16[256,2048]{1,0:T(8,128)(2,1)S(1)} collective-permute-done((bf16[256,2048]{1,0:T(8,128)(2,1)S(1)}, bf16[256,2048]{1,0:T(8,128)(2,1)S(1)}, u32[]{:S(2)}, u32[]{:S(2)}) %collective-permute-start.3) | collective-permute-done | bytes 1048608 | tf_op jit(solution)/shard_map/ppermute | solution.py:383
  74.1 5.3 %pack_rows.4 = (bf16[192,2048]{1,0:T(8,128)(2,1)}, bf16[2,192,256]{2,1,0:T(8,128)(2,1)}, bf16[192,128]{1,0:T(8,128)(2,1)}, bf16[256,2048]{1,0:T(8,128)(2,1)}, bf16[256,2048]{1,0:T(8,128)(2,1)}) custom-call(s32[2]{0:T(128)} %pad_add_fusion.ids, s32[8]{0:T(128)} %rows.7, s32[8]{0:T(128)} %tenants.7, ...), custom_call_target="tpu_custom_call", output_to_operand_aliasing={{3}: (6, {}), {4}: (7, {})} | custom-call | tf_op jit(solution)/shard_map/pack_rows/pallas_call | solution.py:113
  80.1 2.1 collective-permute-start.9
  82.2 8.6 %dot_pair.10 = (bf16[192,1664]{1,0:T(8,128)(2,1)}, bf16[192,1664]{1,0:T(8,128)(2,1)}) custom-call(s32[2]{0:T(128)} %pad_add_fusion.ids, bf16[192,2048]{1,0:T(8,128)(2,1)} %get-tuple-element.34.refs_0_.refs_1_, bf16[2,192,256]{2,1,0:T(8,128)(2,1)} %get-tuple-element.35.refs_1_.refs_4_.refs_3_, bf16[2048,6656]{1,0:T(8,128)(2,1)} %refs_4_.15, ...), custom_call_target="tpu_custom_call" | custom-call | tf_op jit(solution)/shard_map/dot_pair/pallas_call | solution.py:269
  95.0 12.4 %dot_pair.11.refs_8_ = bf16[2,192,1664]{2,1,0:T(8,128)(2,1)} custom-call(s32[2]{0:T(128)} %pad_add_fusion.ids, bf16[192,2048]{1,0:T(8,128)(2,1)} %get-tuple-element.34.refs_0_.refs_1_, bf16[2,192,256]{2,1,0:T(8,128)(2,1)} %get-tuple-element.35.refs_1_.refs_4_.refs_3_, bf16[2048,6656]{1,0:T(8,128)(2,1)} %refs_4_.15, bf16[2048,6656]{1,0:T(8,128)(2,1)} %refs_5_.1, ...), custom_call_target="tpu_custom_call" | custom-call | tf_op jit(solution)/shard_map/dot_pair/pallas_call | solution.py:269
  107.4 2.1 collective-permute-start.17
  110.8 6.0 %pack_rows.5 = (bf16[320,2048]{1,0:T(8,128)(2,1)}, bf16[2,320,256]{2,1,0:T(8,128)(2,1)}, bf16[320,128]{1,0:T(8,128)(2,1)}) custom-call(s32[2]{0:T(128)} %pad_add_fusion.ids, s32[8]{0:T(128)} %rows.7, s32[8]{0:T(128)} %tenants.7, bf16[256,2048]{1,0:T(8,128)(2,1)} %refs_0_.5, bf16[256,2048]{1,0:T(8,128)(2,1)} %copy-done.4, bf16[256,2048]{1,0:T(8,128)(2,1)} %copy-done.2, ...), custom_call_target="tpu_custom_call" | custom-call | tf_op jit(solution)/shard_map/pack_rows/pallas_call | solution.py:113
  116.9 11.0 %dot_pair.12 = (bf16[160,1664]{1,0:T(8,128)(2,1)}, bf16[160,1664]{1,0:T(8,128)(2,1)}, bf16[160,1664]{1,0:T(8,128)(2,1)}, bf16[160,1664]{1,0:T(8,128)(2,1)}) custom-call(s32[2]{0:T(128)} %pad_add_fusion.ids, bf16[320,2048]{1,0:T(8,128)(2,1)} %get-tuple-element.38.refs_0_.refs_2_, bf16[2,320,256]{2,1,0:T(8,128)(2,1)} %get-tuple-element.39.refs_1_.refs_5_, ...), custom_call_target="tpu_custom_call" | custom-call | tf_op jit(solution)/shard_map/dot_pair/pallas_call | solution.py:269
  133.2 14.9 %dot_pair.13.refs_9_ = bf16[2,320,1664]{2,1,0:T(8,128)(2,1)} custom-call(s32[2]{0:T(128)} %pad_add_fusion.ids, bf16[320,2048]{1,0:T(8,128)(2,1)} %get-tuple-element.38.refs_0_.refs_2_, bf16[2,320,256]{2,1,0:T(8,128)(2,1)} %get-tuple-element.39.refs_1_.refs_5_, bf16[2048,6656]{1,0:T(8,128)(2,1)} %refs_4_.15, bf16[2048,6656]{1,0:T(8,128)(2,1)} %refs_5_.1, ...), custom_call_target="tpu_custom_call" | custom-call | tf_op jit(solution)/shard_map/dot_pair/pallas_call | solution.py:269
  149.5 19.9 %dot_pair.14 = (bf16[448,1664]{1,0:T(8,128)(2,1)}, bf16[320,1664]{1,0:T(8,128)(2,1)}, bf16[448,1664]{1,0:T(8,128)(2,1)}, bf16[320,1664]{1,0:T(8,128)(2,1)}) custom-call(s32[2]{0:T(128)} %pad_add_fusion.ids, bf16[256,2048]{1,0:T(8,128)(2,1)} %get-tuple-element.28.refs_0_, bf16[192,2048]{1,0:T(8,128)(2,1)} %get-tuple-element.34.refs_0_.refs_1_, ...), custom_call_target="tpu_custom_call" | custom-call | tf_op jit(solution)/shard_map/dot_pair/pallas_call | solution.py:269
  170.5 5.5 %collective-permute-done.18.refs_5_ = bf16[320,1664]{1,0:T(8,128)(2,1)S(1)} collective-permute-done((bf16[320,1664]{1,0:T(8,128)(2,1)}, bf16[320,1664]{1,0:T(8,128)(2,1)S(1)}, u32[]{:S(2)}, u32[]{:S(2)}) %collective-permute-start.18) | collective-permute-done | bytes 1064992 | tf_op jit(solution)/shard_map/ppermute | solution.py:409
  176.0 2.3 %collective-permute-done.19.refs_6_ = bf16[320,1664]{1,0:T(8,128)(2,1)} collective-permute-done((bf16[320,1664]{1,0:T(8,128)(2,1)}, bf16[320,1664]{1,0:T(8,128)(2,1)}, u32[]{:S(2)}, u32[]{:S(2)}) %collective-permute-start.19) | collective-permute-done | bytes 1064992 | tf_op jit(solution)/shard_map/ppermute | solution.py:409
  178.3 15.7 %dot_pair.15.refs_14_.sums = f32[2,320,1664]{2,1,0:T(8,128)} custom-call(s32[2]{0:T(128)} %pad_add_fusion.ids, bf16[320,2048]{1,0:T(8,128)(2,1)} %get-tuple-element.38.refs_0_.refs_2_, bf16[2,320,256]{2,1,0:T(8,128)(2,1)} %get-tuple-element.39.refs_1_.refs_5_, bf16[2048,6656]{1,0:T(8,128)(2,1)} %refs_4_.15, bf16[2048,6656]{1,0:T(8,128)(2,1)} %refs_5_.1, ...), custom_call_target="tpu_custom_call" | custom-call | tf_op jit(solution)/shard_map/dot_pair/pallas_call | solution.py:269
  194.0 19.4 %finish_dots.1.earlier = bf16[448,1664]{1,0:T(8,128)(2,1)} custom-call(s32[2]{0:T(128)} %pad_add_fusion.ids, bf16[256,2048]{1,0:T(8,128)(2,1)} %get-tuple-element.28.refs_0_, bf16[192,2048]{1,0:T(8,128)(2,1)} %get-tuple-element.34.refs_0_.refs_1_, bf16[2,256,256]{2,1,0:T(8,128)(2,1)} %get-tuple-element.29.refs_1_.refs_3_.refs_2_, ...), custom_call_target="tpu_custom_call" | custom-call | tf_op jit(solution)/shard_map/finish_dots/pallas_call | solution.py:269
  214.8 10.9 %last_rows.1 = bf16[1024,1664]{1,0:T(8,128)(2,1)} custom-call(s32[2]{0:T(128)} %pad_add_fusion.ids, s32[8]{0:T(128)} %rows.7, s32[8]{0:T(128)} %tenants.7, f32[2,320,1664]{2,1,0:T(8,128)} %dot_pair.15.refs_14_.sums, bf16[2,320,1664]{2,1,0:T(8,128)(2,1)} %copy-done.8, bf16[320,128]{1,0:T(8,128)(2,1)} %get-tuple-element.46.pick, ...), custom_call_target="tpu_custom_call" | custom-call | tf_op jit(solution)/shard_map/last_rows/pallas_call | solution.py:341
  (86 shorter events, 27.8 us)
Async XLA Ops:
  0.0 27.1 %collective-permute-start.1 = (bf16[256,2048]{1,0:T(8,128)(2,1)}, bf16[256,2048]{1,0:T(8,128)(2,1)S(1)}, u32[]{:S(2)}, u32[]{:S(2)}) collective-permute-start(bf16[256,2048]{1,0:T(8,128)(2,1)} %refs_0_.5), channel_id=1, source_target_pairs={{4,0},{8,4},{12,8},{5,1},{9,5},{13,9},{6,2},{10,6},{14,10},{7,3},{... | collective-permute-start | bytes 3145736 | tf_op jit(solution)/shard_map/ppermute | solution.py:383
  2.1 27.0 %collective-permute-start = (bf16[256,2048]{1,0:T(8,128)(2,1)}, bf16[256,2048]{1,0:T(8,128)(2,1)S(1)}, u32[]{:S(2)}, u32[]{:S(2)}) collective-permute-start(bf16[256,2048]{1,0:T(8,128)(2,1)} %refs_0_.5), channel_id=1, source_target_pairs={{0,4},{4,8},{8,12},{1,5},{5,9},{9,13},{2,6},{6,10},{10,14},{3,7},{... | collective-permute-start | bytes 3145736 | tf_op jit(solution)/shard_map/ppermute | solution.py:383
  7.2 1.5 collective-permute-start.4
  8.8 5.1 %collective-permute-start.5 = (f32[8,2,1664]{2,0,1:T(8,128)S(1)}, f32[8,2,1664]{2,0,1:T(8,128)S(1)}, u32[]{:S(2)}, u32[]{:S(2)}) collective-permute-start(f32[8,2,1664]{2,0,1:T(8,128)S(1)} %slice_bitcast_fusion), channel_id=1, source_target_pairs={{0,2},{1,3},{2,0},{3,1},{4,6},{5,7},{6,4},{7,5},{8,10},{9,11},{10,... | collective-permute-start | bytes 319496 | tf_op jit(solution)/shard_map/ppermute | solution.py:392
  35.3 12.5 %copy-start.5 = (bf16[256,2048]{1,0:T(8,128)(2,1)S(1)}, bf16[256,2048]{1,0:T(8,128)(2,1)}, u32[]{:S(2)}) copy-start(bf16[256,2048]{1,0:T(8,128)(2,1)} %copy-done.4) | copy-start | bytes 3145732
  45.2 7.5 %collective-permute-start.6 = (bf16[256,1664]{1,0:T(8,128)(2,1)}, bf16[256,1664]{1,0:T(8,128)(2,1)}, u32[]{:S(2)}, u32[]{:S(2)}) collective-permute-start(bf16[256,1664]{1,0:T(8,128)(2,1)} %get-tuple-element.30), channel_id=1, source_target_pairs={{0,1},{1,0},{2,3},{3,2},{4,5},{5,4},{6,7},{7,6},{8,9},{9,8},{10,11... | collective-permute-start | bytes 2555912 | tf_op jit(solution)/shard_map/ppermute | solution.py:409
  45.3 7.4 %collective-permute-start.7 = (bf16[256,1664]{1,0:T(8,128)(2,1)}, bf16[256,1664]{1,0:T(8,128)(2,1)}, u32[]{:S(2)}, u32[]{:S(2)}) collective-permute-start(bf16[256,1664]{1,0:T(8,128)(2,1)} %get-tuple-element.31), channel_id=1, source_target_pairs={{0,1},{1,0},{2,3},{3,2},{4,5},{5,4},{6,7},{7,6},{8,9},{9,8},{10,11... | collective-permute-start | bytes 2555912 | tf_op jit(solution)/shard_map/ppermute | solution.py:409
  45.8 27.0 %collective-permute-start.3 = (bf16[256,2048]{1,0:T(8,128)(2,1)S(1)}, bf16[256,2048]{1,0:T(8,128)(2,1)S(1)}, u32[]{:S(2)}, u32[]{:S(2)}) collective-permute-start(bf16[256,2048]{1,0:T(8,128)(2,1)S(1)} %copy-done.3), channel_id=1, source_target_pairs={{4,0},{8,4},{5,1},{9,5},{6,2},{10,6},{7,3},{11,7},{20,16},{24,20},... | collective-permute-start | bytes 3145736 | tf_op jit(solution)/shard_map/ppermute | solution.py:383
  47.7 26.4 %collective-permute-start.2 = (bf16[256,2048]{1,0:T(8,128)(2,1)S(1)}, bf16[256,2048]{1,0:T(8,128)(2,1)}, u32[]{:S(2)}, u32[]{:S(2)}) collective-permute-start(bf16[256,2048]{1,0:T(8,128)(2,1)S(1)} %copy-done.5), channel_id=1, source_target_pairs={{4,8},{8,12},{5,9},{9,13},{6,10},{10,14},{7,11},{11,15},{20,24},{2... | collective-permute-start | bytes 3145736 | tf_op jit(solution)/shard_map/ppermute | solution.py:383
  66.3 43.2 %collective-permute-start.12 = (bf16[2,256,1664]{2,1,0:T(8,128)(2,1)}, bf16[2,256,1664]{2,1,0:T(8,128)(2,1)}, u32[]{:S(2)}, u32[]{:S(2)}) collective-permute-start(bf16[2,256,1664]{2,1,0:T(8,128)(2,1)} %dot_pair.9.refs_6_), channel_id=1, source_target_pairs={{0,2},{1,3},{2,0},{3,1},{4,6},{5,7},{6,4},{7,5},{8,10},{9,11},{10,... | collective-permute-start | bytes 5111816 | tf_op jit(solution)/shard_map/ppermute | solution.py:416
  79.4 30.1 %collective-permute-start.8 = (bf16[256,2048]{1,0:T(8,128)(2,1)}, bf16[256,2048]{1,0:T(8,128)(2,1)S(1)}, u32[]{:S(2)}, u32[]{:S(2)}) collective-permute-start(bf16[256,2048]{1,0:T(8,128)(2,1)} %get-tuple-element.32.refs_3_), channel_id=1, source_target_pairs={{8,12},{9,13},{10,14},{11,15},{24,28},{25,29},{26,30},{27,31}} | collective-permute-start | bytes 3145736 | tf_op jit(solution)/shard_map/ppermute | solution.py:383
  80.1 29.4 %collective-permute-start.9 = (bf16[256,2048]{1,0:T(8,128)(2,1)}, bf16[256,2048]{1,0:T(8,128)(2,1)S(1)}, u32[]{:S(2)}, u32[]{:S(2)}) collective-permute-start(bf16[256,2048]{1,0:T(8,128)(2,1)} %get-tuple-element.33.refs_4_), channel_id=1, source_target_pairs={{4,0},{5,1},{6,2},{7,3},{20,16},{21,17},{22,18},{23,19}} | collective-permute-start | bytes 3145736 | tf_op jit(solution)/shard_map/ppermute | solution.py:383
  90.9 2.4 %collective-permute-start.10 = (bf16[192,1664]{1,0:T(8,128)(2,1)}, bf16[192,1664]{1,0:T(8,128)(2,1)S(1)}, u32[]{:S(2)}, u32[]{:S(2)}) collective-permute-start(bf16[192,1664]{1,0:T(8,128)(2,1)} %get-tuple-element.36), channel_id=1, source_target_pairs={{0,1},{1,0},{2,3},{3,2},{4,5},{5,4},{6,7},{7,6},{8,9},{9,8},{10,11... | collective-permute-start | bytes 1916936 | tf_op jit(solution)/shard_map/ppermute | solution.py:409
  91.0 3.2 %collective-permute-start.11 = (bf16[192,1664]{1,0:T(8,128)(2,1)}, bf16[192,1664]{1,0:T(8,128)(2,1)S(1)}, u32[]{:S(2)}, u32[]{:S(2)}) collective-permute-start(bf16[192,1664]{1,0:T(8,128)(2,1)} %get-tuple-element.37), channel_id=1, source_target_pairs={{0,1},{1,0},{2,3},{3,2},{4,5},{5,4},{6,7},{7,6},{8,9},{9,8},{10,11... | collective-permute-start | bytes 1916936 | tf_op jit(solution)/shard_map/ppermute | solution.py:409
  107.4 41.0 %collective-permute-start.17 = (bf16[2,192,1664]{2,1,0:T(8,128)(2,1)}, bf16[2,192,1664]{2,1,0:T(8,128)(2,1)S(1)}, u32[]{:S(2)}, u32[]{:S(2)}) collective-permute-start(bf16[2,192,1664]{2,1,0:T(8,128)(2,1)} %dot_pair.11.refs_8_), channel_id=1, source_target_pairs={{0,2},{1,3},{2,0},{3,1},{4,6},{5,7},{6,4},{7,5},{8,10},{9,11},{10,... | collective-permute-start | bytes 3833864 | tf_op jit(solution)/shard_map/ppermute | solution.py:416
  127.9 2.2 collective-permute-start.13
  127.9 2.9 %collective-permute-start.14 = (bf16[160,1664]{1,0:T(8,128)(2,1)}, bf16[160,1664]{1,0:T(8,128)(2,1)S(1)}, u32[]{:S(2)}, u32[]{:S(2)}) collective-permute-start(bf16[160,1664]{1,0:T(8,128)(2,1)} %get-tuple-element.41), channel_id=1, source_target_pairs={{0,1},{1,0},{2,3},{3,2},{4,5},{5,4},{6,7},{7,6},{8,9},{9,8},{10,11... | collective-permute-start | bytes 1597448 | tf_op jit(solution)/shard_map/ppermute | solution.py:409
  128.4 3.1 %collective-permute-start.15 = (bf16[160,1664]{1,0:T(8,128)(2,1)}, bf16[160,1664]{1,0:T(8,128)(2,1)S(1)}, u32[]{:S(2)}, u32[]{:S(2)}) collective-permute-start(bf16[160,1664]{1,0:T(8,128)(2,1)} %get-tuple-element.42), channel_id=1, source_target_pairs={{0,1},{1,0},{2,3},{3,2},{4,5},{5,4},{6,7},{7,6},{8,9},{9,8},{10,11... | collective-permute-start | bytes 1597448 | tf_op jit(solution)/shard_map/ppermute | solution.py:409
  128.5 3.8 %collective-permute-start.16 = (bf16[160,1664]{1,0:T(8,128)(2,1)}, bf16[160,1664]{1,0:T(8,128)(2,1)S(1)}, u32[]{:S(2)}, u32[]{:S(2)}) collective-permute-start(bf16[160,1664]{1,0:T(8,128)(2,1)} %get-tuple-element.43), channel_id=1, source_target_pairs={{0,1},{1,0},{2,3},{3,2},{4,5},{5,4},{6,7},{7,6},{8,9},{9,8},{10,11... | collective-permute-start | bytes 1597448 | tf_op jit(solution)/shard_map/ppermute | solution.py:409
  148.1 65.3 %collective-permute-start.20 = (bf16[2,320,1664]{2,1,0:T(8,128)(2,1)}, bf16[2,320,1664]{2,1,0:T(8,128)(2,1)S(1)}, u32[]{:S(2)}, u32[]{:S(2)}) collective-permute-start(bf16[2,320,1664]{2,1,0:T(8,128)(2,1)} %dot_pair.13.refs_9_), channel_id=1, source_target_pairs={{0,2},{1,3},{2,0},{3,1},{4,6},{5,7},{6,4},{7,5},{8,10},{9,11},{10,... | collective-permute-start | bytes 6389768 | tf_op jit(solution)/shard_map/ppermute | solution.py:416
  169.4 24.6 %collective-permute-start.21 = (bf16[448,1664]{1,0:T(8,128)(2,1)}, bf16[448,1664]{1,0:T(8,128)(2,1)}, u32[]{:S(2)}, u32[]{:S(2)}) collective-permute-start(bf16[448,1664]{1,0:T(8,128)(2,1)} %get-tuple-element.47), channel_id=1, source_target_pairs={{0,1},{1,0},{2,3},{3,2},{4,5},{5,4},{6,7},{7,6},{8,9},{9,8},{10,11... | collective-permute-start | bytes 4472840 | tf_op jit(solution)/shard_map/ppermute | solution.py:409
  169.5 24.5 %collective-permute-start.22 = (bf16[448,1664]{1,0:T(8,128)(2,1)}, bf16[448,1664]{1,0:T(8,128)(2,1)}, u32[]{:S(2)}, u32[]{:S(2)}) collective-permute-start(bf16[448,1664]{1,0:T(8,128)(2,1)} %get-tuple-element.48), channel_id=1, source_target_pairs={{0,1},{1,0},{2,3},{3,2},{4,5},{5,4},{6,7},{7,6},{8,9},{9,8},{10,11... | collective-permute-start | bytes 4472840 | tf_op jit(solution)/shard_map/ppermute | solution.py:409
  170.0 6.0 %collective-permute-start.18 = (bf16[320,1664]{1,0:T(8,128)(2,1)}, bf16[320,1664]{1,0:T(8,128)(2,1)S(1)}, u32[]{:S(2)}, u32[]{:S(2)}) collective-permute-start(bf16[320,1664]{1,0:T(8,128)(2,1)} %get-tuple-element.44), channel_id=1, source_target_pairs={{0,1},{1,0},{2,3},{3,2},{4,5},{5,4},{6,7},{7,6},{8,9},{9,8},{10,11... | collective-permute-start | bytes 3194888 | tf_op jit(solution)/shard_map/ppermute | solution.py:409
  170.0 8.2 %collective-permute-start.19 = (bf16[320,1664]{1,0:T(8,128)(2,1)}, bf16[320,1664]{1,0:T(8,128)(2,1)}, u32[]{:S(2)}, u32[]{:S(2)}) collective-permute-start(bf16[320,1664]{1,0:T(8,128)(2,1)} %get-tuple-element.45), channel_id=1, source_target_pairs={{0,1},{1,0},{2,3},{3,2},{4,5},{5,4},{6,7},{7,6},{8,9},{9,8},{10,11... | collective-permute-start | bytes 3194888 | tf_op jit(solution)/shard_map/ppermute | solution.py:409
  (17 other events, 47.2 us)

commit v5 on v4

--- a/solution.py
+++ b/solution.py
@@ -161,12 +161,9 @@
         copy.start()
         loads.append(copy)
 
-    row = 0
-    for part, count in enumerate(counts):
-        here = pl.ds(row, count)
-        load(x_refs[part], x.at[here])
-        load(low_refs[part], low.at[:, here])
-        row += count
+    def wait_loads(begin, end):
+        for copy in loads[begin:end]:
+            copy.wait()
 
     def piece(side, at, size, place):
         return pltpu.make_async_copy(
@@ -174,38 +171,35 @@
             w.at[place, :, pl.ds(side * size, size)], w_sem.at[side, place],
         )
 
-    def start_piece(place):
+    def start_piece(at, size, place):
         for side in range(2):
-            piece(side, *tiles[place], place).start()
-
-    start_piece(0)
-    for side in range(2):
-        for copy in range(2):
-            load(up_ref.at[:, side, :, pl.ds(left, narrow)], maps.at[side, copy])
-    row = 0
-    if terms:
-        count = rows // terms
-        for side in range(2):
-            for part in range(terms):
-                load(term_refs[side * terms + part], term.at[side, pl.ds(part * count, count)])
-    if finish:
-        for part, count in enumerate(counts):
-            here = pl.ds(row, count)
-            load(far_refs[part], far.at[:, here])
-            load(pick_refs[part], pick.at[here])
-            row += count
-        load(scale_ref, scale)
-    for place in range(1, len(tiles)):
-        start_piece(place)
-    for copy in loads:
-        copy.wait()
-
-    def tile(at, size, place):
+            piece(side, at, size, place).start()
+
+    def stores(at, size, place):
+        columns = pl.ds(at, size)
+        if finish:
+            pairs = [(out.at[0, :, columns], outs[0].at[:, columns])]
+        elif not splits:
+            pairs = [(out.at[side, :, columns], outs[0].at[side, :, columns]) for side in range(2)]
+        else:
+            pairs = []
+            for side in range(2):
+                row = 0
+                for part, count in enumerate(splits):
+                    target = outs[side * len(splits) + part].at[:, columns]
+                    pairs.append((out.at[side, pl.ds(row, count), columns], target))
+                    row += count
+        return [
+            pltpu.make_async_copy(source, target, out_sem.at[place, i]) for i, (source, target) in enumerate(pairs)
+        ]
+
+    def tile(at, size, place, before_sums=lambda: None):
         columns = pl.ds(at, size)
         values = []
         for side in range(2):
             piece(side, at, size, place).wait()
         both = jnp.dot(x[...], w[place, :, 0:2 * size], preferred_element_type=jnp.float32)
+        before_sums()
         for side in range(2):
             value = both[:, side * size:(side + 1) * size]
             value += jnp.dot(
@@ -221,33 +215,65 @@
                 out[side, :, columns] = value.astype(out.dtype)
         if finish:
             out[0, :, columns] = activate(*values)
-
-    @pl.loop(0, whole)
+        for copy in stores(at, size, place):
+            copy.start()
+
+    row = 0
+    for part, count in enumerate(counts):
+        load(x_refs[part], x.at[pl.ds(row, count)])
+        row += count
+    start_piece(*tiles[0], 0)
+    first_loads = len(loads)
+    start_piece(*tiles[1], 1)
+    row = 0
+    for part, count in enumerate(counts):
+        load(low_refs[part], low.at[:, pl.ds(row, count)])
+        row += count
+    for side in range(2):
+        load(up_ref.at[:, side, :, pl.ds(left, narrow)], maps.at[side, 0])
+    if terms:
+        count = rows // terms
+        for side in range(2):
+            for part in range(terms):
+                load(term_refs[side * terms + part], term.at[side, pl.ds(part * count, count)])
+    if finish:
+        row = 0
+        for part, count in enumerate(counts):
+            here = pl.ds(row, count)
+            load(far_refs[part], far.at[:, here])
+            load(pick_refs[part], pick.at[here])
+            row += count
+        load(scale_ref, scale)
+    wait_loads(0, first_loads)
+
+    def rest():
+        start_piece(*tiles[2], 2)
+        wait_loads(first_loads, len(loads))
+        for side in range(2):
+            maps[side, 1] = maps[side, 0]
+
+    tile(*tiles[0], 0, rest)
+
+    @pl.loop(1, whole)
     def _(place):
-        tile(pl.multiple_of(place * TILE, TILE), TILE, place)
+        at = pl.multiple_of(place * TILE, TILE)
+
+        @pl.when(place + 2 < whole)
+        def _():
+            start_piece(pl.multiple_of(at + 2 * TILE, TILE), TILE, place + 2)
+
+        if whole < len(tiles):
+            @pl.when(place + 2 == whole)
+            def _():
+                start_piece(*tiles[whole], whole)
+
+        tile(at, TILE, place)
 
     for place in range(whole, len(tiles)):
         tile(*tiles[place], place)
-
-    copies = []
-
-    def store(source, target):
-        copy = pltpu.make_async_copy(source, target, out_sem.at[len(copies)])
-        copy.start()
-        copies.append(copy)
-
-    if finish:
-        store(out.at[0], outs[0])
-    elif not splits:
-        store(out, outs[0])
-    else:
-        for side in range(2):
-            row = 0
-            for part, count in enumerate(splits):
-                store(out.at[side, pl.ds(row, count)], outs[side * len(splits) + part])
-                row += count
-    for copy in copies:
-        copy.wait()
+    for place, (at, size) in enumerate(tiles):
+        for copy in stores(at, size, place):
+            copy.wait()
 
 
 def dot_pair(chunks, weights, adapter_out, flip, narrow, ids, out_dtype, splits=(), terms=(), finish=None, after=()):
@@ -288,7 +314,7 @@
                 pltpu.VMEM((2, 128, narrow) if finish is not None else few, jnp.bfloat16),
                 pltpu.SemaphoreType.DMA((4 * len(xs) + 8,)),
                 pltpu.SemaphoreType.DMA((2, pieces)),
-                pltpu.SemaphoreType.DMA((4,)),
+                pltpu.SemaphoreType.DMA((pieces, 4)),
             ],
         ),
         compiler_params=pltpu.CompilerParams(vmem_limit_bytes=VMEM_LIMIT),
@@ -428,13 +454,15 @@
     mark, far2 = send_far(chunk2, 2)
 
     first, last = CHUNKS[2][:2]
-    parts = dots([chunk0, chunk1, chunk2], flip=1, out_dtype=jnp.bfloat16, splits=(first, last), after=(mark, far1))
-    early_gate, late_gate, early_up, late_up = swap(parts, near)
-    sums, = dots([chunk2], flip=0, out_dtype=jnp.float32, terms=(late_gate, late_up))
+    parts = dots([chunk0, chunk1], flip=1, out_dtype=jnp.bfloat16, splits=(first,), after=(mark, far1))
+    early = swap(parts, near)
+    parts = dots([chunk2], flip=1, out_dtype=jnp.bfloat16, splits=(last,), after=(parts[0],))
+    late = swap(parts, near)
     hidden, = dots(
-        [chunk0, chunk1], flip=0, out_dtype=jnp.bfloat16, terms=(early_gate, early_up),
-        finish=((far0, far1), scale), after=(sums,),
-    )
+        [chunk0, chunk1], flip=0, out_dtype=jnp.bfloat16, terms=early, finish=((far0, far1), scale),
+        after=(parts[0],),
+    )
+    sums, = dots([chunk2], flip=0, out_dtype=jnp.float32, terms=late, after=(hidden,))
     return last_rows(mx_count, first, scalars, sums, far2, chunk2[2], scale, hidden, block_rows.shape[0])
 
 

time: 228 us -> 209 us (0.917)
  Pallas kernels: 153 us -> 137 us
  waiting for transfers between devices: 38.1 us -> 33.8 us
    pallas_call x9 -> x10, Pallas kernels: 126 us -> 110 us  [dot_pair(): pl.pallas_call(functools.partial(dot_kernel, flip, counts, splits, len(te...]
    ppermute x12, waiting for transfers between devices: 13.9 us -> 6.09 us  [swap(): return [lax.ppermute(part, 'my', pairs) for part in parts]]
    ppermute x6, waiting for transfers between devices: 19.9 us -> 23.5 us  [hop(): return lax.ppermute(block, 'mx', pairs)]
  transfers between devices with their start and end apart: 23 -> 23, of which waited for: 14 -> 12; matrix products, arithmetic and copies ran while one was open for 1% -> 1% of each run, Pallas kernels for 56% -> 54%
where the time goes in v5:
time: 209 us; the launch traced here: 207 us
  Pallas kernels  137 us (66%)
  waiting for transfers between devices  33.8 us (16%)
  starting transfers between devices  25.1 us (12%)
  local copies, waits for them, and re-layouts  8.62 us (4%)
    pallas_call x10, Pallas kernels, dot_pair(): pl.pallas_call(functools.partial(dot_kernel, flip, counts, splits, len(te...  110 us
    ppermute x6, waiting for transfers between devices, hop(): return lax.ppermute(block, 'mx', pairs)  23.5 us
    pallas_call x3, Pallas kernels, pack_rows(): pl.pallas_call(functools.partial(pack_kernel, mx_count, first, rows_out,...  16.7 us
    ppermute x6, starting transfers between devices, hop(): return lax.ppermute(block, 'mx', pairs)  16.1 us
    pallas_call x1, Pallas kernels, last_rows(): pl.pallas_call(functools.partial(last_kernel, mx_count, first), out_shape...  10.9 us
    unnamed x40, local copies, waits for them, and re-layouts  7.42 us
    ppermute x12, waiting for transfers between devices, swap(): return [lax.ppermute(part, 'my', pairs) for part in parts]  6.09 us
  transfers between devices with their start and end apart: 23, of which 12 were waited for; matrix products, arithmetic and copies ran while one was open for 1% of the time, Pallas kernels for 54%

profile of v5, /device:TPU:8, one launch (start us, length us, event | category | flops | bytes accessed | tf_op | source)
XLA Modules:
  0.0 207.0 jit_solution(1881766451146118940)
XLA Ops:
  0.0 2.0 collective-permute-start.1
  2.1 3.9 %collective-permute-start = (bf16[256,2048]{1,0:T(8,128)(2,1)}, bf16[256,2048]{1,0:T(8,128)(2,1)S(1)}, u32[]{:S(2)}, u32[]{:S(2)}) collective-permute-start(bf16[256,2048]{1,0:T(8,128)(2,1)} %refs_0_.5), channel_id=1, source_target_pairs={{0,4},{4,8},{8,12},{1,5},{5,9},{9,13},{2,6},{6,10},{10,14},{3,7},{... | collective-permute-start | bytes 3145736 | tf_op jit(solution)/shard_map/ppermute | solution.py:409
  10.9 2.9 %collective-permute-done.5 = f32[8,2,1664]{2,0,1:T(8,128)S(1)} collective-permute-done((f32[8,2,1664]{2,0,1:T(8,128)S(1)}, f32[8,2,1664]{2,0,1:T(8,128)S(1)}, u32[]{:S(2)}, u32[]{:S(2)}) %collective-permute-start.5) | collective-permute-done | bytes 106528 | tf_op jit(solution)/shard_map/ppermute | solution.py:418
  14.9 12.2 %collective-permute-done.1.refs_2_ = bf16[256,2048]{1,0:T(8,128)(2,1)S(1)} collective-permute-done((bf16[256,2048]{1,0:T(8,128)(2,1)}, bf16[256,2048]{1,0:T(8,128)(2,1)S(1)}, u32[]{:S(2)}, u32[]{:S(2)}) %collective-permute-start.1) | collective-permute-done | bytes 1048608 | tf_op jit(solution)/shard_map/ppermute | solution.py:409
  27.1 1.9 collective-permute-done.refs_1_
  30.1 5.6 %pack_rows.3 = (bf16[256,2048]{1,0:T(8,128)(2,1)}, bf16[2,256,256]{2,1,0:T(8,128)(2,1)}, bf16[256,128]{1,0:T(8,128)(2,1)}) custom-call(s32[2]{0:T(128)} %pad_add_fusion.ids, s32[8]{0:T(128)} %rows.7, s32[8]{0:T(128)} %tenants.7, bf16[256,2048]{1,0:T(8,128)(2,1)} %refs_0_.5, bf16[256,2048]{1,0:T(8,128)(2,1)} %copy-done.4, bf16[256,2048]{1,0:T(8,128)(2,1)} %copy-done.2, ...), custom_call_target="tpu_custom_call" | custom-call | tf_op jit(solution)/shard_map/pack_rows/pallas_call | solution.py:113
  35.7 9.9 %dot_pair.9 = (bf16[256,1664]{1,0:T(8,128)(2,1)}, bf16[256,1664]{1,0:T(8,128)(2,1)}) custom-call(s32[2]{0:T(128)} %pad_add_fusion.ids, bf16[256,2048]{1,0:T(8,128)(2,1)} %get-tuple-element.28.refs_0_, bf16[2,256,256]{2,1,0:T(8,128)(2,1)} %get-tuple-element.29.refs_1_.refs_2_, bf16[2048,6656]{1,0:T(8,128)(2,1)} %refs_2_.15, bf16[2048,6656]{1,0:T(8,128)(2,1)} %refs_3_.15, ...), custom_call_target="tpu_custom_call" | custom-call | tf_op jit(solution)/shard_map/dot_pair/pallas_call | solution.py:295
  46.2 1.9 collective-permute-start.3
  48.1 5.0 %collective-permute-start.2 = (bf16[256,2048]{1,0:T(8,128)(2,1)S(1)}, bf16[256,2048]{1,0:T(8,128)(2,1)}, u32[]{:S(2)}, u32[]{:S(2)}) collective-permute-start(bf16[256,2048]{1,0:T(8,128)(2,1)S(1)} %copy-done.5), channel_id=1, source_target_pairs={{4,8},{8,12},{5,9},{9,13},{6,10},{10,14},{7,11},{11,15},{20,24},{2... | collective-permute-start | bytes 3145736 | tf_op jit(solution)/shard_map/ppermute | solution.py:409
  53.1 10.1 %dot_pair.10.refs_6_ = bf16[2,256,1664]{2,1,0:T(8,128)(2,1)} custom-call(s32[2]{0:T(128)} %pad_add_fusion.ids, bf16[256,2048]{1,0:T(8,128)(2,1)} %get-tuple-element.28.refs_0_, bf16[2,256,256]{2,1,0:T(8,128)(2,1)} %get-tuple-element.29.refs_1_.refs_2_, bf16[2048,6656]{1,0:T(8,128)(2,1)} %refs_2_.15, bf16[2048,6656]{1,0:T(8,128)(2,1)} %refs_3_.15, ...), custom_call_target="tpu_custom_call" | custom-call | tf_op jit(solution)/shard_map/dot_pair/pallas_call | solution.py:295
  63.2 1.9 collective-permute-start.12
  65.1 8.1 %collective-permute-done.3.refs_4_ = bf16[256,2048]{1,0:T(8,128)(2,1)S(1)} collective-permute-done((bf16[256,2048]{1,0:T(8,128)(2,1)S(1)}, bf16[256,2048]{1,0:T(8,128)(2,1)S(1)}, u32[]{:S(2)}, u32[]{:S(2)}) %collective-permute-start.3) | collective-permute-done | bytes 1048608 | tf_op jit(solution)/shard_map/ppermute | solution.py:409
  74.5 4.6 %pack_rows.4 = (bf16[192,2048]{1,0:T(8,128)(2,1)}, bf16[2,192,256]{2,1,0:T(8,128)(2,1)}, bf16[192,128]{1,0:T(8,128)(2,1)}, bf16[256,2048]{1,0:T(8,128)(2,1)}, bf16[256,2048]{1,0:T(8,128)(2,1)}) custom-call(s32[2]{0:T(128)} %pad_add_fusion.ids, s32[8]{0:T(128)} %rows.7, s32[8]{0:T(128)} %tenants.7, ...), custom_call_target="tpu_custom_call", output_to_operand_aliasing={{3}: (6, {}), {4}: (7, {})} | custom-call | tf_op jit(solution)/shard_map/pack_rows/pallas_call | solution.py:113
  79.8 2.5 %collective-permute-start.9 = (bf16[256,2048]{1,0:T(8,128)(2,1)}, bf16[256,2048]{1,0:T(8,128)(2,1)S(1)}, u32[]{:S(2)}, u32[]{:S(2)}) collective-permute-start(bf16[256,2048]{1,0:T(8,128)(2,1)} %get-tuple-element.33.refs_4_), channel_id=1, source_target_pairs={{4,0},{5,1},{6,2},{7,3},{20,16},{21,17},{22,18},{23,19}} | collective-permute-start | bytes 3145736 | tf_op jit(solution)/shard_map/ppermute | solution.py:409
  82.3 9.2 %dot_pair.11 = (bf16[192,1664]{1,0:T(8,128)(2,1)}, bf16[192,1664]{1,0:T(8,128)(2,1)}) custom-call(s32[2]{0:T(128)} %pad_add_fusion.ids, bf16[192,2048]{1,0:T(8,128)(2,1)} %get-tuple-element.34.refs_0_.refs_1_, bf16[2,192,256]{2,1,0:T(8,128)(2,1)} %get-tuple-element.35.refs_1_.refs_3_, bf16[2048,6656]{1,0:T(8,128)(2,1)} %refs_2_.15, ...), custom_call_target="tpu_custom_call" | custom-call | tf_op jit(solution)/shard_map/dot_pair/pallas_call | solution.py:295
  95.6 9.6 %dot_pair.12.refs_8_ = bf16[2,192,1664]{2,1,0:T(8,128)(2,1)} custom-call(s32[2]{0:T(128)} %pad_add_fusion.ids, bf16[192,2048]{1,0:T(8,128)(2,1)} %get-tuple-element.34.refs_0_.refs_1_, bf16[2,192,256]{2,1,0:T(8,128)(2,1)} %get-tuple-element.35.refs_1_.refs_3_, bf16[2048,6656]{1,0:T(8,128)(2,1)} %refs_2_.15, bf16[2048,6656]{1,0:T(8,128)(2,1)} %refs_3_.15, ...), custom_call_target="tpu_custom_call" | custom-call | tf_op jit(solution)/shard_map/dot_pair/pallas_call | solution.py:295
  108.3 6.5 %pack_rows.5 = (bf16[320,2048]{1,0:T(8,128)(2,1)}, bf16[2,320,256]{2,1,0:T(8,128)(2,1)}, bf16[320,128]{1,0:T(8,128)(2,1)}) custom-call(s32[2]{0:T(128)} %pad_add_fusion.ids, s32[8]{0:T(128)} %rows.7, s32[8]{0:T(128)} %tenants.7, bf16[256,2048]{1,0:T(8,128)(2,1)} %refs_0_.5, bf16[256,2048]{1,0:T(8,128)(2,1)} %copy-done.4, bf16[256,2048]{1,0:T(8,128)(2,1)} %copy-done.2, ...), custom_call_target="tpu_custom_call" | custom-call | tf_op jit(solution)/shard_map/pack_rows/pallas_call | solution.py:113
  114.8 10.3 %dot_pair.13 = (bf16[160,1664]{1,0:T(8,128)(2,1)}, bf16[160,1664]{1,0:T(8,128)(2,1)}, bf16[160,1664]{1,0:T(8,128)(2,1)}, bf16[160,1664]{1,0:T(8,128)(2,1)}) custom-call(s32[2]{0:T(128)} %pad_add_fusion.ids, bf16[320,2048]{1,0:T(8,128)(2,1)} %get-tuple-element.38.refs_0_, bf16[2,320,256]{2,1,0:T(8,128)(2,1)} %get-tuple-element.39.refs_1_, ...), custom_call_target="tpu_custom_call" | custom-call | tf_op jit(solution)/shard_map/dot_pair/pallas_call | solution.py:295
  130.5 10.9 %dot_pair.14.refs_7_ = bf16[2,320,1664]{2,1,0:T(8,128)(2,1)} custom-call(s32[2]{0:T(128)} %pad_add_fusion.ids, bf16[320,2048]{1,0:T(8,128)(2,1)} %get-tuple-element.38.refs_0_, bf16[2,320,256]{2,1,0:T(8,128)(2,1)} %get-tuple-element.39.refs_1_, bf16[2048,6656]{1,0:T(8,128)(2,1)} %refs_2_.15, bf16[2048,6656]{1,0:T(8,128)(2,1)} %refs_3_.15, ...), custom_call_target="tpu_custom_call" | custom-call | tf_op jit(solution)/shard_map/dot_pair/pallas_call | solution.py:295
  143.0 12.3 %dot_pair.15 = (bf16[448,1664]{1,0:T(8,128)(2,1)}, bf16[448,1664]{1,0:T(8,128)(2,1)}) custom-call(s32[2]{0:T(128)} %pad_add_fusion.ids, bf16[256,2048]{1,0:T(8,128)(2,1)} %get-tuple-element.28.refs_0_, bf16[192,2048]{1,0:T(8,128)(2,1)} %get-tuple-element.34.refs_0_.refs_1_, bf16[2,256,256]{2,1,0:T(8,128)(2,1)} %get-tuple-element.29.refs_1_.refs_2_, ...), custom_call_target="tpu_custom_call" | custom-call | tf_op jit(solution)/shard_map/dot_pair/pallas_call | solution.py:295
  155.9 10.6 %dot_pair.16 = (bf16[320,1664]{1,0:T(8,128)(2,1)}, bf16[320,1664]{1,0:T(8,128)(2,1)}) custom-call(s32[2]{0:T(128)} %pad_add_fusion.ids, bf16[320,2048]{1,0:T(8,128)(2,1)} %get-tuple-element.38.refs_0_, bf16[2,320,256]{2,1,0:T(8,128)(2,1)} %get-tuple-element.39.refs_1_, bf16[2048,6656]{1,0:T(8,128)(2,1)} %refs_2_.15, bf16[2048,6656]{1,0:T(8,128)(2,1)} %refs_3_.15, ...), custom_call_target="tpu_custom_call" | custom-call | tf_op jit(solution)/shard_map/dot_pair/pallas_call | solution.py:295
  167.1 15.4 %finish_dots.1.refs_7_.earlier = bf16[448,1664]{1,0:T(8,128)(2,1)} custom-call(s32[2]{0:T(128)} %pad_add_fusion.ids, bf16[256,2048]{1,0:T(8,128)(2,1)} %get-tuple-element.28.refs_0_, bf16[192,2048]{1,0:T(8,128)(2,1)} %get-tuple-element.34.refs_0_.refs_1_, bf16[2,256,256]{2,1,0:T(8,128)(2,1)} %get-tuple-element.29.refs_1_.refs_2_, ...), custom_call_target="tpu_custom_call" | custom-call | tf_op jit(solution)/shard_map/finish_dots/pallas_call | solution.py:295
  183.5 11.2 %dot_pair.17.sums = f32[2,320,1664]{2,1,0:T(8,128)} custom-call(s32[2]{0:T(128)} %pad_add_fusion.ids, bf16[320,2048]{1,0:T(8,128)(2,1)} %get-tuple-element.38.refs_0_, bf16[2,320,256]{2,1,0:T(8,128)(2,1)} %get-tuple-element.39.refs_1_, bf16[2048,6656]{1,0:T(8,128)(2,1)} %refs_2_.15, bf16[2048,6656]{1,0:T(8,128)(2,1)} %refs_3_.15, ...), custom_call_target="tpu_custom_call" | custom-call | tf_op jit(solution)/shard_map/dot_pair/pallas_call | solution.py:295
  196.1 10.9 %last_rows.1 = bf16[1024,1664]{1,0:T(8,128)(2,1)} custom-call(s32[2]{0:T(128)} %pad_add_fusion.ids, s32[8]{0:T(128)} %rows.7, s32[8]{0:T(128)} %tenants.7, f32[2,320,1664]{2,1,0:T(8,128)} %dot_pair.17.sums, bf16[2,320,1664]{2,1,0:T(8,128)(2,1)} %copy-done.8, bf16[320,128]{1,0:T(8,128)(2,1)} %get-tuple-element.50.pick, ...), custom_call_target="tpu_custom_call" | custom-call | tf_op jit(solution)/shard_map/last_rows/pallas_call | solution.py:367
  (87 shorter events, 26.9 us)
Async XLA Ops:
  0.0 27.1 %collective-permute-start.1 = (bf16[256,2048]{1,0:T(8,128)(2,1)}, bf16[256,2048]{1,0:T(8,128)(2,1)S(1)}, u32[]{:S(2)}, u32[]{:S(2)}) collective-permute-start(bf16[256,2048]{1,0:T(8,128)(2,1)} %refs_0_.5), channel_id=1, source_target_pairs={{4,0},{8,4},{12,8},{5,1},{9,5},{13,9},{6,2},{10,6},{14,10},{7,3},{... | collective-permute-start | bytes 3145736 | tf_op jit(solution)/shard_map/ppermute | solution.py:409
  2.1 27.0 %collective-permute-start = (bf16[256,2048]{1,0:T(8,128)(2,1)}, bf16[256,2048]{1,0:T(8,128)(2,1)S(1)}, u32[]{:S(2)}, u32[]{:S(2)}) collective-permute-start(bf16[256,2048]{1,0:T(8,128)(2,1)} %refs_0_.5), channel_id=1, source_target_pairs={{0,4},{4,8},{8,12},{1,5},{5,9},{9,13},{2,6},{6,10},{10,14},{3,7},{... | collective-permute-start | bytes 3145736 | tf_op jit(solution)/shard_map/ppermute | solution.py:409
  7.2 1.5 collective-permute-start.4
  8.8 5.1 %collective-permute-start.5 = (f32[8,2,1664]{2,0,1:T(8,128)S(1)}, f32[8,2,1664]{2,0,1:T(8,128)S(1)}, u32[]{:S(2)}, u32[]{:S(2)}) collective-permute-start(f32[8,2,1664]{2,0,1:T(8,128)S(1)} %slice_bitcast_fusion), channel_id=1, source_target_pairs={{0,2},{1,3},{2,0},{3,1},{4,6},{5,7},{6,4},{7,5},{8,10},{9,11},{10,... | collective-permute-start | bytes 319496 | tf_op jit(solution)/shard_map/ppermute | solution.py:418
  35.7 12.4 %copy-start.5 = (bf16[256,2048]{1,0:T(8,128)(2,1)S(1)}, bf16[256,2048]{1,0:T(8,128)(2,1)}, u32[]{:S(2)}) copy-start(bf16[256,2048]{1,0:T(8,128)(2,1)} %copy-done.4) | copy-start | bytes 3145732
  45.6 7.5 %collective-permute-start.6 = (bf16[256,1664]{1,0:T(8,128)(2,1)}, bf16[256,1664]{1,0:T(8,128)(2,1)}, u32[]{:S(2)}, u32[]{:S(2)}) collective-permute-start(bf16[256,1664]{1,0:T(8,128)(2,1)} %get-tuple-element.30), channel_id=1, source_target_pairs={{0,1},{1,0},{2,3},{3,2},{4,5},{5,4},{6,7},{7,6},{8,9},{9,8},{10,11... | collective-permute-start | bytes 2555912 | tf_op jit(solution)/shard_map/ppermute | solution.py:435
  45.7 7.4 %collective-permute-start.7 = (bf16[256,1664]{1,0:T(8,128)(2,1)}, bf16[256,1664]{1,0:T(8,128)(2,1)}, u32[]{:S(2)}, u32[]{:S(2)}) collective-permute-start(bf16[256,1664]{1,0:T(8,128)(2,1)} %get-tuple-element.31), channel_id=1, source_target_pairs={{0,1},{1,0},{2,3},{3,2},{4,5},{5,4},{6,7},{7,6},{8,9},{9,8},{10,11... | collective-permute-start | bytes 2555912 | tf_op jit(solution)/shard_map/ppermute | solution.py:435
  46.2 27.0 %collective-permute-start.3 = (bf16[256,2048]{1,0:T(8,128)(2,1)S(1)}, bf16[256,2048]{1,0:T(8,128)(2,1)S(1)}, u32[]{:S(2)}, u32[]{:S(2)}) collective-permute-start(bf16[256,2048]{1,0:T(8,128)(2,1)S(1)} %copy-done.3), channel_id=1, source_target_pairs={{4,0},{8,4},{5,1},{9,5},{6,2},{10,6},{7,3},{11,7},{20,16},{24,20},... | collective-permute-start | bytes 3145736 | tf_op jit(solution)/shard_map/ppermute | solution.py:409
  48.1 26.4 %collective-permute-start.2 = (bf16[256,2048]{1,0:T(8,128)(2,1)S(1)}, bf16[256,2048]{1,0:T(8,128)(2,1)}, u32[]{:S(2)}, u32[]{:S(2)}) collective-permute-start(bf16[256,2048]{1,0:T(8,128)(2,1)S(1)} %copy-done.5), channel_id=1, source_target_pairs={{4,8},{8,12},{5,9},{9,13},{6,10},{10,14},{7,11},{11,15},{20,24},{2... | collective-permute-start | bytes 3145736 | tf_op jit(solution)/shard_map/ppermute | solution.py:409
  63.2 43.8 %collective-permute-start.12 = (bf16[2,256,1664]{2,1,0:T(8,128)(2,1)}, bf16[2,256,1664]{2,1,0:T(8,128)(2,1)}, u32[]{:S(2)}, u32[]{:S(2)}) collective-permute-start(bf16[2,256,1664]{2,1,0:T(8,128)(2,1)} %dot_pair.10.refs_6_), channel_id=1, source_target_pairs={{0,2},{1,3},{2,0},{3,1},{4,6},{5,7},{6,4},{7,5},{8,10},{9,11},{10,... | collective-permute-start | bytes 5111816 | tf_op jit(solution)/shard_map/ppermute | solution.py:442
  79.0 27.9 %collective-permute-start.8 = (bf16[256,2048]{1,0:T(8,128)(2,1)}, bf16[256,2048]{1,0:T(8,128)(2,1)S(1)}, u32[]{:S(2)}, u32[]{:S(2)}) collective-permute-start(bf16[256,2048]{1,0:T(8,128)(2,1)} %get-tuple-element.32.refs_3_), channel_id=1, source_target_pairs={{8,12},{9,13},{10,14},{11,15},{24,28},{25,29},{26,30},{27,31}} | collective-permute-start | bytes 3145736 | tf_op jit(solution)/shard_map/ppermute | solution.py:409
  79.8 27.2 %collective-permute-start.9 = (bf16[256,2048]{1,0:T(8,128)(2,1)}, bf16[256,2048]{1,0:T(8,128)(2,1)S(1)}, u32[]{:S(2)}, u32[]{:S(2)}) collective-permute-start(bf16[256,2048]{1,0:T(8,128)(2,1)} %get-tuple-element.33.refs_4_), channel_id=1, source_target_pairs={{4,0},{5,1},{6,2},{7,3},{20,16},{21,17},{22,18},{23,19}} | collective-permute-start | bytes 3145736 | tf_op jit(solution)/shard_map/ppermute | solution.py:409
  91.5 2.4 %collective-permute-start.10 = (bf16[192,1664]{1,0:T(8,128)(2,1)}, bf16[192,1664]{1,0:T(8,128)(2,1)S(1)}, u32[]{:S(2)}, u32[]{:S(2)}) collective-permute-start(bf16[192,1664]{1,0:T(8,128)(2,1)} %get-tuple-element.36), channel_id=1, source_target_pairs={{0,1},{1,0},{2,3},{3,2},{4,5},{5,4},{6,7},{7,6},{8,9},{9,8},{10,11... | collective-permute-start | bytes 1916936 | tf_op jit(solution)/shard_map/ppermute | solution.py:435
  91.6 3.2 %collective-permute-start.11 = (bf16[192,1664]{1,0:T(8,128)(2,1)}, bf16[192,1664]{1,0:T(8,128)(2,1)S(1)}, u32[]{:S(2)}, u32[]{:S(2)}) collective-permute-start(bf16[192,1664]{1,0:T(8,128)(2,1)} %get-tuple-element.37), channel_id=1, source_target_pairs={{0,1},{1,0},{2,3},{3,2},{4,5},{5,4},{6,7},{7,6},{8,9},{9,8},{10,11... | collective-permute-start | bytes 1916936 | tf_op jit(solution)/shard_map/ppermute | solution.py:435
  105.2 36.7 %collective-permute-start.17 = (bf16[2,192,1664]{2,1,0:T(8,128)(2,1)}, bf16[2,192,1664]{2,1,0:T(8,128)(2,1)S(1)}, u32[]{:S(2)}, u32[]{:S(2)}) collective-permute-start(bf16[2,192,1664]{2,1,0:T(8,128)(2,1)} %dot_pair.12.refs_8_), channel_id=1, source_target_pairs={{0,2},{1,3},{2,0},{3,1},{4,6},{5,7},{6,4},{7,5},{8,10},{9,11},{10,... | collective-permute-start | bytes 3833864 | tf_op jit(solution)/shard_map/ppermute | solution.py:442
  125.1 2.2 %collective-permute-start.13 = (bf16[160,1664]{1,0:T(8,128)(2,1)}, bf16[160,1664]{1,0:T(8,128)(2,1)S(1)}, u32[]{:S(2)}, u32[]{:S(2)}) collective-permute-start(bf16[160,1664]{1,0:T(8,128)(2,1)} %get-tuple-element.40), channel_id=1, source_target_pairs={{0,1},{1,0},{2,3},{3,2},{4,5},{5,4},{6,7},{7,6},{8,9},{9,8},{10,11... | collective-permute-start | bytes 1597448 | tf_op jit(solution)/shard_map/ppermute | solution.py:435
  125.2 2.9 %collective-permute-start.14 = (bf16[160,1664]{1,0:T(8,128)(2,1)}, bf16[160,1664]{1,0:T(8,128)(2,1)S(1)}, u32[]{:S(2)}, u32[]{:S(2)}) collective-permute-start(bf16[160,1664]{1,0:T(8,128)(2,1)} %get-tuple-element.41), channel_id=1, source_target_pairs={{0,1},{1,0},{2,3},{3,2},{4,5},{5,4},{6,7},{7,6},{8,9},{9,8},{10,11... | collective-permute-start | bytes 1597448 | tf_op jit(solution)/shard_map/ppermute | solution.py:435
  125.7 3.1 %collective-permute-start.15 = (bf16[160,1664]{1,0:T(8,128)(2,1)}, bf16[160,1664]{1,0:T(8,128)(2,1)S(1)}, u32[]{:S(2)}, u32[]{:S(2)}) collective-permute-start(bf16[160,1664]{1,0:T(8,128)(2,1)} %get-tuple-element.42), channel_id=1, source_target_pairs={{0,1},{1,0},{2,3},{3,2},{4,5},{5,4},{6,7},{7,6},{8,9},{9,8},{10,11... | collective-permute-start | bytes 1597448 | tf_op jit(solution)/shard_map/ppermute | solution.py:435
  125.8 3.8 %collective-permute-start.16 = (bf16[160,1664]{1,0:T(8,128)(2,1)}, bf16[160,1664]{1,0:T(8,128)(2,1)S(1)}, u32[]{:S(2)}, u32[]{:S(2)}) collective-permute-start(bf16[160,1664]{1,0:T(8,128)(2,1)} %get-tuple-element.43), channel_id=1, source_target_pairs={{0,1},{1,0},{2,3},{3,2},{4,5},{5,4},{6,7},{7,6},{8,9},{9,8},{10,11... | collective-permute-start | bytes 1597448 | tf_op jit(solution)/shard_map/ppermute | solution.py:435
  141.5 53.2 %collective-permute-start.22 = (bf16[2,320,1664]{2,1,0:T(8,128)(2,1)}, bf16[2,320,1664]{2,1,0:T(8,128)(2,1)S(1)}, u32[]{:S(2)}, u32[]{:S(2)}) collective-permute-start(bf16[2,320,1664]{2,1,0:T(8,128)(2,1)} %dot_pair.14.refs_7_), channel_id=1, source_target_pairs={{0,2},{1,3},{2,0},{3,1},{4,6},{5,7},{6,4},{7,5},{8,10},{9,11},{10,... | collective-permute-start | bytes 6389768 | tf_op jit(solution)/shard_map/ppermute | solution.py:442
  155.3 11.8 %collective-permute-start.21 = (bf16[448,1664]{1,0:T(8,128)(2,1)}, bf16[448,1664]{1,0:T(8,128)(2,1)}, u32[]{:S(2)}, u32[]{:S(2)}) collective-permute-start(bf16[448,1664]{1,0:T(8,128)(2,1)} %get-tuple-element.47), channel_id=1, source_target_pairs={{0,1},{1,0},{2,3},{3,2},{4,5},{5,4},{6,7},{7,6},{8,9},{9,8},{10,11... | collective-permute-start | bytes 4472840 | tf_op jit(solution)/shard_map/ppermute | solution.py:435
  155.4 11.7 %collective-permute-start.20 = (bf16[448,1664]{1,0:T(8,128)(2,1)}, bf16[448,1664]{1,0:T(8,128)(2,1)}, u32[]{:S(2)}, u32[]{:S(2)}) collective-permute-start(bf16[448,1664]{1,0:T(8,128)(2,1)} %get-tuple-element.44.refs_5_), channel_id=1, source_target_pairs={{0,1},{1,0},{2,3},{3,2},{4,5},{5,4},{6,7},{7,6},{8,9},{9,8},{10,11... | collective-permute-start | bytes 4472840 | tf_op jit(solution)/shard_map/ppermute | solution.py:435
  166.5 16.0 %collective-permute-start.19 = (bf16[320,1664]{1,0:T(8,128)(2,1)}, bf16[320,1664]{1,0:T(8,128)(2,1)S(1)}, u32[]{:S(2)}, u32[]{:S(2)}) collective-permute-start(bf16[320,1664]{1,0:T(8,128)(2,1)} %get-tuple-element.46), channel_id=1, source_target_pairs={{0,1},{1,0},{2,3},{3,2},{4,5},{5,4},{6,7},{7,6},{8,9},{9,8},{10,11... | collective-permute-start | bytes 3194888 | tf_op jit(solution)/shard_map/ppermute | solution.py:435
  166.7 15.8 %collective-permute-start.18 = (bf16[320,1664]{1,0:T(8,128)(2,1)}, bf16[320,1664]{1,0:T(8,128)(2,1)}, u32[]{:S(2)}, u32[]{:S(2)}) collective-permute-start(bf16[320,1664]{1,0:T(8,128)(2,1)} %get-tuple-element.45.refs_14_), channel_id=1, source_target_pairs={{0,1},{1,0},{2,3},{3,2},{4,5},{5,4},{6,7},{7,6},{8,9},{9,8},{10,11... | collective-permute-start | bytes 3194888 | tf_op jit(solution)/shard_map/ppermute | solution.py:435
  (17 other events, 45.9 us)

commit v6 on v5

--- a/solution.py
+++ b/solution.py
@@ -12,12 +12,15 @@
 BLOCK_ROWS = 128
 LIVE_ROWS = 768
 TILE = 256
+AHEAD = 3
+CUTS = 2
 VMEM_LIMIT = 60 * 1024 * 1024
 
 SLOTS = tuple((distance, half) for distance in (0, -1, 1, -2, 2, -3, 3) for half in range(2))
-CHUNKS = ((0, 256, 6), (256, 192, 10), (448, 320, 14))
+CHUNKS = ((0, 256, 6), (256, 256, 10), (512, 256, 14))
 ANY = pl.BlockSpec(memory_space=pl.ANY)
 COST = pl.CostEstimate(flops=0, bytes_accessed=0, transcendentals=0)
+LONG = pl.CostEstimate(flops=10**12, bytes_accessed=0, transcendentals=0)
 
 
 def fill_table(table, ids, rows, tenants, mx_count):
@@ -41,31 +44,33 @@
     table, buffer, down, acc, sems, down_sem = scratch
     fill_table(table, ids, rows, tenants, mx_count)
 
-    def needed(slot):
-        start, count = table[0, slot], table[1, slot]
+    def needed(source):
+        start, count = table[0, 2 * source], table[1, 2 * source] + table[1, 2 * source + 1]
         return (count > 0) & (start < first + rows_out) & (start + count > first)
 
-    for slot in range(slots):
-        @pl.when(needed(slot))
+    for source in range(slots // 2):
+        @pl.when(needed(source))
         def _():
-            here = pl.ds(slot % 2 * BLOCK_ROWS, BLOCK_ROWS)
-            pltpu.make_async_copy(token_refs[slot // 2].at[here], buffer.at[slot], sems.at[slot]).start()
+            pltpu.make_async_copy(token_refs[source], buffer.at[source], sems.at[source]).start()
 
     down_copy = pltpu.make_async_copy(down_ref, down, down_sem)
     down_copy.start()
     acc[...] = jnp.zeros_like(acc)
 
-    @pl.loop(0, slots)
-    def _(slot):
-        @pl.when(needed(slot))
+    @pl.loop(0, slots // 2)
+    def _(source):
+        @pl.when(needed(source))
         def _():
-            start, count = table[0, slot], table[1, slot]
-            pltpu.make_async_copy(buffer.at[slot], buffer.at[slot], sems.at[slot]).wait()
-            target = lax.broadcasted_iota(jnp.int32, (rows_out, BLOCK_ROWS), 0) + first
-            position = lax.broadcasted_iota(jnp.int32, (rows_out, BLOCK_ROWS), 1)
+            pltpu.make_async_copy(buffer.at[source], buffer.at[source], sems.at[source]).wait()
+            target = lax.broadcasted_iota(jnp.int32, (rows_out, 2 * BLOCK_ROWS), 0) + first
+            place = lax.broadcasted_iota(jnp.int32, (rows_out, 2 * BLOCK_ROWS), 1)
+            upper = place >= BLOCK_ROWS
+            position = jnp.where(upper, place - BLOCK_ROWS, place)
+            start = jnp.where(upper, table[0, 2 * source + 1], table[0, 2 * source])
+            count = jnp.where(upper, table[1, 2 * source + 1], table[1, 2 * source])
             chosen = (position < count) & (target == position + start)
             acc[...] += jnp.dot(
-                chosen.astype(jnp.bfloat16), buffer[slot], preferred_element_type=jnp.float32
+                chosen.astype(jnp.bfloat16), buffer[source], preferred_element_type=jnp.float32
             )
 
     x_ref[...] = acc[...].astype(jnp.bfloat16)
@@ -97,7 +102,7 @@
         low_ref[side] = moved.astype(jnp.bfloat16)
 
 
-def pack_rows(mx_count, chunk, scalars, tokens, down, after=(), passed=()):
+def pack_rows(mx_count, chunk, scalars, tokens, down, after=(), passed=(), cost=COST):
     first, rows_out, slots = chunk
     width = down.shape[1]
     outs = [
@@ -120,16 +125,16 @@
             out_specs=out_specs,
             scratch_shapes=[
                 pltpu.SMEM((4, len(SLOTS)), jnp.int32),
-                pltpu.VMEM((slots, BLOCK_ROWS, width), jnp.bfloat16),
+                pltpu.VMEM((slots // 2, 2 * BLOCK_ROWS, width), jnp.bfloat16),
                 pltpu.VMEM(down.shape, jnp.bfloat16),
                 pltpu.VMEM((rows_out, width), jnp.float32),
-                pltpu.SemaphoreType.DMA((slots,)),
+                pltpu.SemaphoreType.DMA((slots // 2,)),
                 pltpu.SemaphoreType.DMA,
             ],
         ),
         input_output_aliases={3 + place: 3 + i for i, place in enumerate(passed)},
         compiler_params=pltpu.CompilerParams(vmem_limit_bytes=VMEM_LIMIT),
-        cost_estimate=COST,
+        cost_estimate=cost,
         name="pack_rows",
     )(*scalars, *tokens, down, *after)
 
@@ -165,15 +170,19 @@
         for copy in loads[begin:end]:
             copy.wait()
 
-    def piece(side, at, size, place):
-        return pltpu.make_async_copy(
-            w_refs[side].at[:, pl.ds(pl.multiple_of(left + at, 128), size)],
-            w.at[place, :, pl.ds(side * size, size)], w_sem.at[side, place],
-        )
-
-    def start_piece(at, size, place):
-        for side in range(2):
-            piece(side, at, size, place).start()
+    def pieces(at, size, place):
+        cut = depth // CUTS
+        return [
+            pltpu.make_async_copy(
+                w_refs[side].at[pl.ds(part * cut, cut), pl.ds(pl.multiple_of(left + at, 128), size)],
+                w.at[place, pl.ds(part * cut, cut), pl.ds(side * size, size)], w_sem.at[place, side, part],
+            )
+            for part in range(CUTS) for side in range(2)
+        ]
+
+    def start_pieces(at, size, place):
+        for copy in pieces(at, size, place):
+            copy.start()
 
     def stores(at, size, place):
         columns = pl.ds(at, size)
@@ -196,8 +205,8 @@
     def tile(at, size, place, before_sums=lambda: None):
         columns = pl.ds(at, size)
         values = []
-        for side in range(2):
-            piece(side, at, size, place).wait()
+        for copy in pieces(at, size, place):
+            copy.wait()
         both = jnp.dot(x[...], w[place, :, 0:2 * size], preferred_element_type=jnp.float32)
         before_sums()
         for side in range(2):
@@ -222,9 +231,9 @@
     for part, count in enumerate(counts):
         load(x_refs[part], x.at[pl.ds(row, count)])
         row += count
-    start_piece(*tiles[0], 0)
     first_loads = len(loads)
-    start_piece(*tiles[1], 1)
+    for place in range(AHEAD):
+        start_pieces(*tiles[place], place)
     row = 0
     for part, count in enumerate(counts):
         load(low_refs[part], low.at[:, pl.ds(row, count)])
@@ -247,7 +256,7 @@
     wait_loads(0, first_loads)
 
     def rest():
-        start_piece(*tiles[2], 2)
+        start_pieces(*tiles[AHEAD], AHEAD)
         wait_loads(first_loads, len(loads))
         for side in range(2):
             maps[side, 1] = maps[side, 0]
@@ -258,14 +267,14 @@
     def _(place):
         at = pl.multiple_of(place * TILE, TILE)
 
-        @pl.when(place + 2 < whole)
+        @pl.when(place + AHEAD < whole)
         def _():
-            start_piece(pl.multiple_of(at + 2 * TILE, TILE), TILE, place + 2)
+            start_pieces(pl.multiple_of(at + AHEAD * TILE, TILE), TILE, place + AHEAD)
 
         if whole < len(tiles):
-            @pl.when(place + 2 == whole)
+            @pl.when(place + AHEAD == whole)
             def _():
-                start_piece(*tiles[whole], whole)
+                start_pieces(*tiles[whole], whole)
 
         tile(at, TILE, place)
 
@@ -276,7 +285,7 @@
             copy.wait()
 
 
-def dot_pair(chunks, weights, adapter_out, flip, narrow, ids, out_dtype, splits=(), terms=(), finish=None, after=()):
+def dot_pair(chunks, weights, adapter_out, flip, narrow, ids, out_dtype, splits=(), terms=(), finish=None, after=(), cost=COST):
     xs, lows, picks = zip(*chunks)
     counts = tuple(x.shape[0] for x in xs)
     rows, depth = sum(counts), xs[0].shape[1]
@@ -291,7 +300,7 @@
         out_shape = [jax.ShapeDtypeStruct((2, rows, narrow), out_dtype)]
     operands += list(after)
     few = (8, 128)
-    pieces = -(-narrow // TILE)
+    places = -(-narrow // TILE)
     return pl.pallas_call(
         functools.partial(
             dot_kernel, flip, counts, splits, len(terms) // 2, counts if finish is not None else (), narrow
@@ -305,7 +314,7 @@
             scratch_shapes=[
                 pltpu.VMEM((rows, depth), jnp.bfloat16),
                 pltpu.VMEM((2, rows, 256), jnp.bfloat16),
-                pltpu.VMEM((pieces, depth, 2 * TILE), jnp.bfloat16),
+                pltpu.VMEM((places, depth, 2 * TILE), jnp.bfloat16),
                 pltpu.VMEM((2, 2, tenants, RANK, narrow), jnp.bfloat16),
                 pltpu.VMEM((2, rows, narrow) if terms else few, jnp.bfloat16),
                 pltpu.VMEM((1 if finish is not None else 2, rows, narrow), out_dtype),
@@ -313,38 +322,57 @@
                 pltpu.VMEM((rows, 128) if finish is not None else few, jnp.bfloat16),
                 pltpu.VMEM((2, 128, narrow) if finish is not None else few, jnp.bfloat16),
                 pltpu.SemaphoreType.DMA((4 * len(xs) + 8,)),
-                pltpu.SemaphoreType.DMA((2, pieces)),
-                pltpu.SemaphoreType.DMA((pieces, 4)),
+                pltpu.SemaphoreType.DMA((places, 2, CUTS)),
+                pltpu.SemaphoreType.DMA((places, 4)),
             ],
         ),
         compiler_params=pltpu.CompilerParams(vmem_limit_bytes=VMEM_LIMIT),
-        cost_estimate=COST,
+        cost_estimate=cost,
         name="finish_dots" if finish is not None else "dot_pair",
     )(*operands)
 
 
-def last_kernel(mx_count, first, ids, rows, tenants, sums, far, pick, scale, earlier, out_ref, table, held):
+def last_kernel(
+    mx_count, first, ids, rows, tenants, sums_ref, far_ref, pick, scale, earlier_ref, out_ref, table, sums, far, held,
+    tile_sem, held_sem,
+):
     block = pl.program_id(0)
+    tiles = far.shape[1] // 64
+
+    def tile_copies(tile):
+        here = pl.ds(pl.multiple_of(tile * 64, 64), 64)
+        return [
+            pltpu.make_async_copy(source.at[:, here], target.at[:, here], tile_sem.at[tile, i])
+            for i, (source, target) in enumerate([(sums_ref, sums), (far_ref, far)])
+        ]
 
     @pl.when(block == 0)
     def _():
+        for tile in range(tiles):
+            for copy in tile_copies(tile):
+                copy.start()
+        held_copy = pltpu.make_async_copy(earlier_ref, held.at[pl.ds(0, first)], held_sem)
+        held_copy.start()
         fill_table(table, ids, rows, tenants, mx_count)
-        held[0:first, :] = earlier[...]
         held[LIVE_ROWS:, :] = jnp.zeros((BLOCK_ROWS, held.shape[1]), held.dtype)
         columns = held.shape[1]
 
-        @pl.loop(0, far.shape[1] // 64)
+        @pl.loop(0, tiles)
         def _(tile):
+            for copy in tile_copies(tile):
+                copy.wait()
             here = pl.ds(pl.multiple_of(tile * 64, 64), 64)
             there = pl.ds(pl.multiple_of(first + tile * 64, 64), 64)
-            for left in range(0, columns, TILE):
-                right = min(left + TILE, columns)
+            for left in range(0, columns, 2 * TILE):
+                right = min(left + 2 * TILE, columns)
                 pre = [
                     (sums[side, here, left:right] + far[side, here, left:right].astype(jnp.float32))
                     * jnp.dot(pick[here, :], scale[side, :, left:right], preferred_element_type=jnp.float32)
                     for side in range(2)
                 ]
                 held[there, left:right] = activate(*pre)
+
+        held_copy.wait()
 
     def find(slot, start):
         return jnp.where(table[3, slot] == block, table[0, slot], start)
@@ -371,12 +399,19 @@
             num_scalar_prefetch=3,
             grid=(blocks,),
             in_specs=[
-                pl.BlockSpec(part.shape, lambda i, *_, dims=part.ndim: (0,) * dims) for part in operands
+                ANY, ANY,
+                pl.BlockSpec(pick.shape, lambda i, *_: (0, 0)),
+                pl.BlockSpec(scale.shape, lambda i, *_: (0, 0, 0)),
+                ANY,
             ],
             out_specs=pl.BlockSpec((BLOCK_ROWS, narrow), lambda i, *_: (i, 0)),
             scratch_shapes=[
                 pltpu.SMEM((4, len(SLOTS)), jnp.int32),
+                pltpu.VMEM(sums.shape, sums.dtype),
+                pltpu.VMEM(far.shape, far.dtype),
                 pltpu.VMEM((LIVE_ROWS + BLOCK_ROWS, narrow), jnp.bfloat16),
+                pltpu.SemaphoreType.DMA((far.shape[1] // 64, 2)),
+                pltpu.SemaphoreType.DMA,
             ],
         ),
         compiler_params=pltpu.CompilerParams(vmem_limit_bytes=VMEM_LIMIT),
@@ -445,18 +480,19 @@
     mark, far0 = send_far(chunk0)
 
     *chunk1, second, third = pack_rows(
-        mx_count, CHUNKS[1], scalars, blocks, down, after=(mark,), passed=(3, 4)
+        mx_count, CHUNKS[1], scalars, blocks, down, after=(mark,), passed=(3, 4), cost=LONG
     )
     blocks = [*blocks[:3], second, third, hop(second, 1, 2), hop(third, -1, 2)]
     mark, far1 = send_far(chunk1)
 
-    *chunk2, = pack_rows(mx_count, CHUNKS[2], scalars, blocks, down, after=(mark, far0))
-    mark, far2 = send_far(chunk2, 2)
+    parts = dots([chunk0, chunk1], flip=1, out_dtype=jnp.bfloat16, splits=(CHUNKS[2][0],), after=(mark,))
+    early = swap(parts, near)
+
+    *chunk2, = pack_rows(mx_count, CHUNKS[2], scalars, blocks, down, after=(parts[0], far0))
+    mark, far2 = send_far(chunk2)
 
     first, last = CHUNKS[2][:2]
-    parts = dots([chunk0, chunk1], flip=1, out_dtype=jnp.bfloat16, splits=(first,), after=(mark, far1))
-    early = swap(parts, near)
-    parts = dots([chunk2], flip=1, out_dtype=jnp.bfloat16, splits=(last,), after=(parts[0],))
+    parts = dots([chunk2], flip=1, out_dtype=jnp.bfloat16, splits=(last,), after=(mark, far1))
     late = swap(parts, near)
     hidden, = dots(
         [chunk0, chunk1], flip=0, out_dtype=jnp.bfloat16, terms=early, finish=((far0, far1), scale),
@@ -536,6 +572,7 @@
         and tokens.shape[0] == 2 * BLOCK_ROWS
         and tokens.shape[1] % 512 == 0
         and w_gate.shape[1] % (my_count * 128) == 0
+        and w_gate.shape[1] // my_count >= (AHEAD + 1) * TILE
     )
     return (pipelined if fits else plain)(tokens, w_gate, *rest)
 

time: 209 us -> 204 us (0.976)
  waiting for transfers between devices: 33.8 us -> 28.4 us
  Pallas kernels: 137 us -> 141 us
  local copies, waits for them, and re-layouts: 8.62 us -> 6.11 us
    ppermute x6, waiting for transfers between devices: 23.5 us -> 13.3 us  [hop(): return lax.ppermute(block, 'mx', pairs)]
    pallas_call x10, Pallas kernels: 110 us -> 116 us  [dot_pair(): pl.pallas_call(functools.partial(dot_kernel, flip, counts, splits, len(te...]
    ppermute x12 -> x10, waiting for transfers between devices: 6.09 us -> 10.9 us  [swap(): return [lax.ppermute(part, 'my', pairs) for part in parts]]
    unnamed x40 -> x28, local copies, waits for them, and re-layouts: 7.42 us -> 4.91 us
  transfers between devices with their start and end apart: 23 -> 21, of which waited for: 12 -> 9; matrix products, arithmetic and copies ran while one was open for 1% -> 1% of each run, Pallas kernels for 54% -> 65%
where the time goes in v6:
time: 204 us; the launch traced here: 203 us
  Pallas kernels  141 us (69%)
  waiting for transfers between devices  28.4 us (14%)
  starting transfers between devices  25.1 us (12%)
  local copies, waits for them, and re-layouts  6.11 us (3%)
    pallas_call x10, Pallas kernels, dot_pair(): pl.pallas_call(functools.partial(dot_kernel, flip, counts, splits, len(te...  116 us
    ppermute x6, starting transfers between devices, hop(): return lax.ppermute(block, 'mx', pairs)  16.7 us
    pallas_call x3, Pallas kernels, pack_rows(): pl.pallas_call(functools.partial(pack_kernel, mx_count, first, rows_out,...  15.1 us
    ppermute x6, waiting for transfers between devices, hop(): return lax.ppermute(block, 'mx', pairs)  13.3 us
    ppermute x10, waiting for transfers between devices, swap(): return [lax.ppermute(part, 'my', pairs) for part in parts]  10.9 us
    pallas_call x1, Pallas kernels, last_rows(): pl.pallas_call(functools.partial(last_kernel, mx_count, first), out_shape...  10.1 us
    unnamed x28, local copies, waits for them, and re-layouts  4.91 us
  transfers between devices with their start and end apart: 21, of which 9 were waited for; matrix products, arithmetic and copies ran while one was open for 1% of the time, Pallas kernels for 65%

profile of v6, /device:TPU:8, one launch (start us, length us, event | category | flops | bytes accessed | tf_op | source)
XLA Modules:
  0.0 203.3 jit_solution(3525991261597931312)
XLA Ops:
  0.0 2.0 %collective-permute-start.1 = (bf16[256,2048]{1,0:T(8,128)(2,1)}, bf16[256,2048]{1,0:T(8,128)(2,1)S(1)}, u32[]{:S(2)}, u32[]{:S(2)}) collective-permute-start(bf16[256,2048]{1,0:T(8,128)(2,1)} %refs_0_.5), channel_id=1, source_target_pairs={{4,0},{8,4},{12,8},{5,1},{9,5},{13,9},{6,2},{10,6},{14,10},{7,3},{... | collective-permute-start | bytes 3145736 | tf_op jit(solution)/shard_map/ppermute | solution.py:444
  2.1 3.9 %collective-permute-start = (bf16[256,2048]{1,0:T(8,128)(2,1)}, bf16[256,2048]{1,0:T(8,128)(2,1)S(1)}, u32[]{:S(2)}, u32[]{:S(2)}) collective-permute-start(bf16[256,2048]{1,0:T(8,128)(2,1)} %refs_0_.5), channel_id=1, source_target_pairs={{0,4},{4,8},{8,12},{1,5},{5,9},{9,13},{2,6},{6,10},{10,14},{3,7},{... | collective-permute-start | bytes 3145736 | tf_op jit(solution)/shard_map/ppermute | solution.py:444
  10.9 2.9 %collective-permute-done.5 = f32[8,2,1664]{2,0,1:T(8,128)S(1)} collective-permute-done((f32[8,2,1664]{2,0,1:T(8,128)S(1)}, f32[8,2,1664]{2,0,1:T(8,128)S(1)}, u32[]{:S(2)}, u32[]{:S(2)}) %collective-permute-start.5) | collective-permute-done | bytes 106528 | tf_op jit(solution)/shard_map/ppermute | solution.py:453
  13.9 13.2 %collective-permute-done.1.refs_2_ = bf16[256,2048]{1,0:T(8,128)(2,1)S(1)} collective-permute-done((bf16[256,2048]{1,0:T(8,128)(2,1)}, bf16[256,2048]{1,0:T(8,128)(2,1)S(1)}, u32[]{:S(2)}, u32[]{:S(2)}) %collective-permute-start.1) | collective-permute-done | bytes 1048608 | tf_op jit(solution)/shard_map/ppermute | solution.py:444
  27.1 2.2 %collective-permute-start.3 = (bf16[256,2048]{1,0:T(8,128)(2,1)S(1)}, bf16[256,2048]{1,0:T(8,128)(2,1)}, u32[]{:S(2)}, u32[]{:S(2)}) collective-permute-start(bf16[256,2048]{1,0:T(8,128)(2,1)S(1)} %collective-permute-done.1.refs_2_), channel_id=1, source_target_pairs={{4,0},{8,4},{5,1},{9,5},{6,2},{10,6},{7,3},{11,7},{20,16},{24,20},... | collective-permute-start | bytes 3145736 | tf_op jit(solution)/shard_map/ppermute | solution.py:444
  29.3 5.6 %collective-permute-start.2 = (bf16[256,2048]{1,0:T(8,128)(2,1)S(1)}, bf16[256,2048]{1,0:T(8,128)(2,1)}, u32[]{:S(2)}, u32[]{:S(2)}) collective-permute-start(bf16[256,2048]{1,0:T(8,128)(2,1)S(1)} %collective-permute-done.refs_1_), channel_id=1, source_target_pairs={{4,8},{8,12},{5,9},{9,13},{6,10},{10,14},{7,11},{11,15},{20,24},{2... | collective-permute-start | bytes 3145736 | tf_op jit(solution)/shard_map/ppermute | solution.py:444
  36.0 4.9 %pack_rows.3 = (bf16[256,2048]{1,0:T(8,128)(2,1)}, bf16[2,256,256]{2,1,0:T(8,128)(2,1)}, bf16[256,128]{1,0:T(8,128)(2,1)}) custom-call(s32[2]{0:T(128)} %pad_add_fusion.ids, s32[8]{0:T(128)} %rows.7, s32[8]{0:T(128)} %tenants.7, bf16[256,2048]{1,0:T(8,128)(2,1)} %refs_0_.5, bf16[256,2048]{1,0:T(8,128)(2,1)} %copy-done.4, bf16[256,2048]{1,0:T(8,128)(2,1)} %copy-done.3, ...), custom_call_target="tpu_custom_call" | custom-call | tf_op jit(solution)/shard_map/pack_rows/pallas_call | solution.py:118
  41.0 10.2 %dot_pair.9 = (bf16[256,1664]{1,0:T(8,128)(2,1)}, bf16[256,1664]{1,0:T(8,128)(2,1)}) custom-call(s32[2]{0:T(128)} %pad_add_fusion.ids, bf16[256,2048]{1,0:T(8,128)(2,1)} %get-tuple-element.26.refs_0_, bf16[2,256,256]{2,1,0:T(8,128)(2,1)} %get-tuple-element.27.refs_1_.refs_2_, bf16[2048,6656]{1,0:T(8,128)(2,1)} %refs_2_.15, bf16[2048,6656]{1,0:T(8,128)(2,1)} %refs_3_.15, ...), custom_call_target="tpu_custom_call" | custom-call | tf_op jit(solution)/shard_map/dot_pair/pallas_call | solution.py:304
  51.7 2.5 %collective-permute-done.6.refs_5_ = bf16[256,1664]{1,0:T(8,128)(2,1)S(1)} collective-permute-done((bf16[256,1664]{1,0:T(8,128)(2,1)}, bf16[256,1664]{1,0:T(8,128)(2,1)S(1)}, u32[]{:S(2)}, u32[]{:S(2)}) %collective-permute-start.6) | collective-permute-done | bytes 852000 | tf_op jit(solution)/shard_map/ppermute | solution.py:470
  55.2 10.7 %dot_pair.10.refs_6_ = bf16[2,256,1664]{2,1,0:T(8,128)(2,1)} custom-call(s32[2]{0:T(128)} %pad_add_fusion.ids, bf16[256,2048]{1,0:T(8,128)(2,1)} %get-tuple-element.26.refs_0_, bf16[2,256,256]{2,1,0:T(8,128)(2,1)} %get-tuple-element.27.refs_1_.refs_2_, bf16[2048,6656]{1,0:T(8,128)(2,1)} %refs_2_.15, bf16[2048,6656]{1,0:T(8,128)(2,1)} %refs_3_.15, ...), custom_call_target="tpu_custom_call" | custom-call | tf_op jit(solution)/shard_map/dot_pair/pallas_call | solution.py:304
  67.7 5.0 %pack_rows.4 = (bf16[256,2048]{1,0:T(8,128)(2,1)}, bf16[2,256,256]{2,1,0:T(8,128)(2,1)}, bf16[256,128]{1,0:T(8,128)(2,1)}, bf16[256,2048]{1,0:T(8,128)(2,1)}, bf16[256,2048]{1,0:T(8,128)(2,1)}) custom-call(s32[2]{0:T(128)} %pad_add_fusion.ids, s32[8]{0:T(128)} %rows.7, s32[8]{0:T(128)} %tenants.7, ...), custom_call_target="tpu_custom_call", output_to_operand_aliasing={{3}: (6, {}), {4}: (7, {})} | custom-call | flops 999999995904 | tf_op jit(solution)/shard_map/pack_rows/pallas_call | solution.py:118
  73.4 2.2 %collective-permute-start.9 = (bf16[256,2048]{1,0:T(8,128)(2,1)}, bf16[256,2048]{1,0:T(8,128)(2,1)}, u32[]{:S(2)}, u32[]{:S(2)}) collective-permute-start(bf16[256,2048]{1,0:T(8,128)(2,1)} %get-tuple-element.31.refs_4_), channel_id=1, source_target_pairs={{4,0},{5,1},{6,2},{7,3},{20,16},{21,17},{22,18},{23,19}} | collective-permute-start | bytes 3145736 | tf_op jit(solution)/shard_map/ppermute | solution.py:444
  75.7 10.2 %dot_pair.11 = (bf16[256,1664]{1,0:T(8,128)(2,1)}, bf16[256,1664]{1,0:T(8,128)(2,1)}) custom-call(s32[2]{0:T(128)} %pad_add_fusion.ids, bf16[256,2048]{1,0:T(8,128)(2,1)} %get-tuple-element.32.refs_0_.refs_1_, bf16[2,256,256]{2,1,0:T(8,128)(2,1)} %get-tuple-element.33.refs_1_.refs_3_, bf16[2048,6656]{1,0:T(8,128)(2,1)} %refs_2_.15, ...), custom_call_target="tpu_custom_call" | custom-call | tf_op jit(solution)/shard_map/dot_pair/pallas_call | solution.py:304
  86.5 2.1 %collective-permute-done.10.refs_5_ = bf16[256,1664]{1,0:T(8,128)(2,1)S(1)} collective-permute-done((bf16[256,1664]{1,0:T(8,128)(2,1)}, bf16[256,1664]{1,0:T(8,128)(2,1)S(1)}, u32[]{:S(2)}, u32[]{:S(2)}) %collective-permute-start.10) | collective-permute-done | bytes 852000 | tf_op jit(solution)/shard_map/ppermute | solution.py:470
  90.7 10.7 %dot_pair.12.refs_7_ = bf16[2,256,1664]{2,1,0:T(8,128)(2,1)} custom-call(s32[2]{0:T(128)} %pad_add_fusion.ids, bf16[256,2048]{1,0:T(8,128)(2,1)} %get-tuple-element.32.refs_0_.refs_1_, bf16[2,256,256]{2,1,0:T(8,128)(2,1)} %get-tuple-element.33.refs_1_.refs_3_, bf16[2048,6656]{1,0:T(8,128)(2,1)} %refs_2_.15, bf16[2048,6656]{1,0:T(8,128)(2,1)} %refs_3_.15, ...), custom_call_target="tpu_custom_call" | custom-call | tf_op jit(solution)/shard_map/dot_pair/pallas_call | solution.py:304
  101.9 14.4 %dot_pair.13 = (bf16[512,1664]{1,0:T(8,128)(2,1)}, bf16[512,1664]{1,0:T(8,128)(2,1)}) custom-call(s32[2]{0:T(128)} %pad_add_fusion.ids, bf16[256,2048]{1,0:T(8,128)(2,1)} %get-tuple-element.26.refs_0_, bf16[256,2048]{1,0:T(8,128)(2,1)} %get-tuple-element.32.refs_0_.refs_1_, bf16[2,256,256]{2,1,0:T(8,128)(2,1)} %get-tuple-element.27.refs_1_.refs_2_, ...), custom_call_target="tpu_custom_call" | custom-call | tf_op jit(solution)/shard_map/dot_pair/pallas_call | solution.py:304
  117.3 5.2 %pack_rows.5 = (bf16[256,2048]{1,0:T(8,128)(2,1)}, bf16[2,256,256]{2,1,0:T(8,128)(2,1)}, bf16[256,128]{1,0:T(8,128)(2,1)}) custom-call(s32[2]{0:T(128)} %pad_add_fusion.ids, s32[8]{0:T(128)} %rows.7, s32[8]{0:T(128)} %tenants.7, bf16[256,2048]{1,0:T(8,128)(2,1)} %refs_0_.5, bf16[256,2048]{1,0:T(8,128)(2,1)} %copy-done.4, bf16[256,2048]{1,0:T(8,128)(2,1)} %copy-done.3, ...), custom_call_target="tpu_custom_call" | custom-call | tf_op jit(solution)/shard_map/pack_rows/pallas_call | solution.py:118
  122.5 10.3 %dot_pair.14 = (bf16[256,1664]{1,0:T(8,128)(2,1)}, bf16[256,1664]{1,0:T(8,128)(2,1)}) custom-call(s32[2]{0:T(128)} %pad_add_fusion.ids, bf16[256,2048]{1,0:T(8,128)(2,1)} %get-tuple-element.37.refs_0_, bf16[2,256,256]{2,1,0:T(8,128)(2,1)} %get-tuple-element.38.refs_1_, bf16[2048,6656]{1,0:T(8,128)(2,1)} %refs_2_.15, bf16[2048,6656]{1,0:T(8,128)(2,1)} %refs_3_.15, ...), custom_call_target="tpu_custom_call" | custom-call | tf_op jit(solution)/shard_map/dot_pair/pallas_call | solution.py:304
  135.7 2.4 %collective-permute-done.14.refs_6_ = bf16[256,1664]{1,0:T(8,128)(2,1)} collective-permute-done((bf16[256,1664]{1,0:T(8,128)(2,1)}, bf16[256,1664]{1,0:T(8,128)(2,1)}, u32[]{:S(2)}, u32[]{:S(2)}) %collective-permute-start.14) | collective-permute-done | bytes 852000 | tf_op jit(solution)/shard_map/ppermute | solution.py:470
  138.1 10.7 %dot_pair.15.refs_5_ = bf16[2,256,1664]{2,1,0:T(8,128)(2,1)} custom-call(s32[2]{0:T(128)} %pad_add_fusion.ids, bf16[256,2048]{1,0:T(8,128)(2,1)} %get-tuple-element.37.refs_0_, bf16[2,256,256]{2,1,0:T(8,128)(2,1)} %get-tuple-element.38.refs_1_, bf16[2048,6656]{1,0:T(8,128)(2,1)} %refs_2_.15, bf16[2048,6656]{1,0:T(8,128)(2,1)} %refs_3_.15, ...), custom_call_target="tpu_custom_call" | custom-call | tf_op jit(solution)/shard_map/dot_pair/pallas_call | solution.py:304
  151.7 10.4 %dot_pair.16 = (bf16[256,1664]{1,0:T(8,128)(2,1)}, bf16[256,1664]{1,0:T(8,128)(2,1)}) custom-call(s32[2]{0:T(128)} %pad_add_fusion.ids, bf16[256,2048]{1,0:T(8,128)(2,1)} %get-tuple-element.37.refs_0_, bf16[2,256,256]{2,1,0:T(8,128)(2,1)} %get-tuple-element.38.refs_1_, bf16[2048,6656]{1,0:T(8,128)(2,1)} %refs_2_.15, bf16[2048,6656]{1,0:T(8,128)(2,1)} %refs_3_.15, ...), custom_call_target="tpu_custom_call" | custom-call | tf_op jit(solution)/shard_map/dot_pair/pallas_call | solution.py:304
  162.7 17.5 %finish_dots.1.refs_7_.earlier_ref = bf16[512,1664]{1,0:T(8,128)(2,1)} custom-call(s32[2]{0:T(128)} %pad_add_fusion.ids, bf16[256,2048]{1,0:T(8,128)(2,1)} %get-tuple-element.26.refs_0_, bf16[256,2048]{1,0:T(8,128)(2,1)} %get-tuple-element.32.refs_0_.refs_1_, bf16[2,256,256]{2,1,0:T(8,128)(2,1)} %get-tuple-element.27.refs_1_.refs_2_, ...), custom_call_target="tpu_custom_call" | custom-call | tf_op jit(solution)/shard_map/finish_dots/pallas_call | solution.py:304
  182.1 10.9 %dot_pair.17.sums_ref = f32[2,256,1664]{2,1,0:T(8,128)} custom-call(s32[2]{0:T(128)} %pad_add_fusion.ids, bf16[256,2048]{1,0:T(8,128)(2,1)} %get-tuple-element.37.refs_0_, bf16[2,256,256]{2,1,0:T(8,128)(2,1)} %get-tuple-element.38.refs_1_, bf16[2048,6656]{1,0:T(8,128)(2,1)} %refs_2_.15, bf16[2048,6656]{1,0:T(8,128)(2,1)} %refs_3_.15, ...), custom_call_target="tpu_custom_call" | custom-call | tf_op jit(solution)/shard_map/dot_pair/pallas_call | solution.py:304
  193.0 10.1 %last_rows.1 = bf16[1024,1664]{1,0:T(8,128)(2,1)} custom-call(s32[2]{0:T(128)} %pad_add_fusion.ids, s32[8]{0:T(128)} %rows.7, s32[8]{0:T(128)} %tenants.7, f32[2,256,1664]{2,1,0:T(8,128)} %dot_pair.17.sums_ref, bf16[2,256,1664]{2,1,0:T(8,128)(2,1)} %collective-permute-done.20.far_ref, bf16[256,128]{1,0:T(8,128)(2,1)} %get-tuple-element.46.pick, ...), custom_call_target="tpu_custom_call" | custom-call | tf_op jit(solution)/shard_map/last_rows/pallas_call | solution.py:395
  (71 shorter events, 22.1 us)
Async XLA Ops:
  0.0 27.1 %collective-permute-start.1 = (bf16[256,2048]{1,0:T(8,128)(2,1)}, bf16[256,2048]{1,0:T(8,128)(2,1)S(1)}, u32[]{:S(2)}, u32[]{:S(2)}) collective-permute-start(bf16[256,2048]{1,0:T(8,128)(2,1)} %refs_0_.5), channel_id=1, source_target_pairs={{4,0},{8,4},{12,8},{5,1},{9,5},{13,9},{6,2},{10,6},{14,10},{7,3},{... | collective-permute-start | bytes 3145736 | tf_op jit(solution)/shard_map/ppermute | solution.py:444
  2.1 27.3 %collective-permute-start = (bf16[256,2048]{1,0:T(8,128)(2,1)}, bf16[256,2048]{1,0:T(8,128)(2,1)S(1)}, u32[]{:S(2)}, u32[]{:S(2)}) collective-permute-start(bf16[256,2048]{1,0:T(8,128)(2,1)} %refs_0_.5), channel_id=1, source_target_pairs={{0,4},{4,8},{8,12},{1,5},{5,9},{9,13},{2,6},{6,10},{10,14},{3,7},{... | collective-permute-start | bytes 3145736 | tf_op jit(solution)/shard_map/ppermute | solution.py:444
  7.2 1.5 collective-permute-start.4
  8.8 5.1 %collective-permute-start.5 = (f32[8,2,1664]{2,0,1:T(8,128)S(1)}, f32[8,2,1664]{2,0,1:T(8,128)S(1)}, u32[]{:S(2)}, u32[]{:S(2)}) collective-permute-start(f32[8,2,1664]{2,0,1:T(8,128)S(1)} %slice_bitcast_fusion), channel_id=1, source_target_pairs={{0,2},{1,3},{2,0},{3,1},{4,6},{5,7},{6,4},{7,5},{8,10},{9,11},{10,... | collective-permute-start | bytes 319496 | tf_op jit(solution)/shard_map/ppermute | solution.py:453
  27.1 8.9 %copy-start.3 = (bf16[256,2048]{1,0:T(8,128)(2,1)}, bf16[256,2048]{1,0:T(8,128)(2,1)S(1)}, u32[]{:S(2)}) copy-start(bf16[256,2048]{1,0:T(8,128)(2,1)S(1)} %collective-permute-done.1.refs_2_) | copy-start | bytes 3145732
  27.1 40.5 %collective-permute-start.3 = (bf16[256,2048]{1,0:T(8,128)(2,1)S(1)}, bf16[256,2048]{1,0:T(8,128)(2,1)}, u32[]{:S(2)}, u32[]{:S(2)}) collective-permute-start(bf16[256,2048]{1,0:T(8,128)(2,1)S(1)} %collective-permute-done.1.refs_2_), channel_id=1, source_target_pairs={{4,0},{8,4},{5,1},{9,5},{6,2},{10,6},{7,3},{11,7},{20,16},{24,20},... | collective-permute-start | bytes 3145736 | tf_op jit(solution)/shard_map/ppermute | solution.py:444
  29.3 38.3 %collective-permute-start.2 = (bf16[256,2048]{1,0:T(8,128)(2,1)S(1)}, bf16[256,2048]{1,0:T(8,128)(2,1)}, u32[]{:S(2)}, u32[]{:S(2)}) collective-permute-start(bf16[256,2048]{1,0:T(8,128)(2,1)S(1)} %collective-permute-done.refs_1_), channel_id=1, source_target_pairs={{4,8},{8,12},{5,9},{9,13},{6,10},{10,14},{7,11},{11,15},{20,24},{2... | collective-permute-start | bytes 3145736 | tf_op jit(solution)/shard_map/ppermute | solution.py:444
  51.2 3.1 %collective-permute-start.6 = (bf16[256,1664]{1,0:T(8,128)(2,1)}, bf16[256,1664]{1,0:T(8,128)(2,1)S(1)}, u32[]{:S(2)}, u32[]{:S(2)}) collective-permute-start(bf16[256,1664]{1,0:T(8,128)(2,1)} %get-tuple-element.28), channel_id=1, source_target_pairs={{0,1},{1,0},{2,3},{3,2},{4,5},{5,4},{6,7},{7,6},{8,9},{9,8},{10,11... | collective-permute-start | bytes 2555912 | tf_op jit(solution)/shard_map/ppermute | solution.py:470
  51.2 3.9 %collective-permute-start.7 = (bf16[256,1664]{1,0:T(8,128)(2,1)}, bf16[256,1664]{1,0:T(8,128)(2,1)}, u32[]{:S(2)}, u32[]{:S(2)}) collective-permute-start(bf16[256,1664]{1,0:T(8,128)(2,1)} %get-tuple-element.29), channel_id=1, source_target_pairs={{0,1},{1,0},{2,3},{3,2},{4,5},{5,4},{6,7},{7,6},{8,9},{9,8},{10,11... | collective-permute-start | bytes 2555912 | tf_op jit(solution)/shard_map/ppermute | solution.py:470
  65.9 50.5 %collective-permute-start.12 = (bf16[2,256,1664]{2,1,0:T(8,128)(2,1)}, bf16[2,256,1664]{2,1,0:T(8,128)(2,1)}, u32[]{:S(2)}, u32[]{:S(2)}) collective-permute-start(bf16[2,256,1664]{2,1,0:T(8,128)(2,1)} %dot_pair.10.refs_6_), channel_id=1, source_target_pairs={{0,2},{1,3},{2,0},{3,1},{4,6},{5,7},{6,4},{7,5},{8,10},{9,11},{10,... | collective-permute-start | bytes 5111816 | tf_op jit(solution)/shard_map/ppermute | solution.py:477
  72.7 43.7 %collective-permute-start.8 = (bf16[256,2048]{1,0:T(8,128)(2,1)}, bf16[256,2048]{1,0:T(8,128)(2,1)S(1)}, u32[]{:S(2)}, u32[]{:S(2)}) collective-permute-start(bf16[256,2048]{1,0:T(8,128)(2,1)} %get-tuple-element.30.refs_3_), channel_id=1, source_target_pairs={{8,12},{9,13},{10,14},{11,15},{24,28},{25,29},{26,30},{27,31}} | collective-permute-start | bytes 3145736 | tf_op jit(solution)/shard_map/ppermute | solution.py:444
  73.4 42.9 %collective-permute-start.9 = (bf16[256,2048]{1,0:T(8,128)(2,1)}, bf16[256,2048]{1,0:T(8,128)(2,1)}, u32[]{:S(2)}, u32[]{:S(2)}) collective-permute-start(bf16[256,2048]{1,0:T(8,128)(2,1)} %get-tuple-element.31.refs_4_), channel_id=1, source_target_pairs={{4,0},{5,1},{6,2},{7,3},{20,16},{21,17},{22,18},{23,19}} | collective-permute-start | bytes 3145736 | tf_op jit(solution)/shard_map/ppermute | solution.py:444
  85.9 2.7 %collective-permute-start.10 = (bf16[256,1664]{1,0:T(8,128)(2,1)}, bf16[256,1664]{1,0:T(8,128)(2,1)S(1)}, u32[]{:S(2)}, u32[]{:S(2)}) collective-permute-start(bf16[256,1664]{1,0:T(8,128)(2,1)} %get-tuple-element.34), channel_id=1, source_target_pairs={{0,1},{1,0},{2,3},{3,2},{4,5},{5,4},{6,7},{7,6},{8,9},{9,8},{10,11... | collective-permute-start | bytes 2555912 | tf_op jit(solution)/shard_map/ppermute | solution.py:470
  86.0 3.8 %collective-permute-start.11 = (bf16[256,1664]{1,0:T(8,128)(2,1)}, bf16[256,1664]{1,0:T(8,128)(2,1)S(1)}, u32[]{:S(2)}, u32[]{:S(2)}) collective-permute-start(bf16[256,1664]{1,0:T(8,128)(2,1)} %get-tuple-element.35), channel_id=1, source_target_pairs={{0,1},{1,0},{2,3},{3,2},{4,5},{5,4},{6,7},{7,6},{8,9},{9,8},{10,11... | collective-permute-start | bytes 2555912 | tf_op jit(solution)/shard_map/ppermute | solution.py:470
  101.4 49.1 %collective-permute-start.15 = (bf16[2,256,1664]{2,1,0:T(8,128)(2,1)}, bf16[2,256,1664]{2,1,0:T(8,128)(2,1)S(1)}, u32[]{:S(2)}, u32[]{:S(2)}) collective-permute-start(bf16[2,256,1664]{2,1,0:T(8,128)(2,1)} %dot_pair.12.refs_7_), channel_id=1, source_target_pairs={{0,2},{1,3},{2,0},{3,1},{4,6},{5,7},{6,4},{7,5},{8,10},{9,11},{10,... | collective-permute-start | bytes 5111816 | tf_op jit(solution)/shard_map/ppermute | solution.py:477
  122.5 11.0 %copy-start.5 = (bf16[512,1664]{1,0:T(8,128)(2,1)S(1)}, bf16[512,1664]{1,0:T(8,128)(2,1)}, u32[]{:S(2)}) copy-start(bf16[512,1664]{1,0:T(8,128)(2,1)} %get-tuple-element.36.refs_8_) | copy-start | bytes 5111812
  132.9 2.8 %collective-permute-start.13 = (bf16[256,1664]{1,0:T(8,128)(2,1)}, bf16[256,1664]{1,0:T(8,128)(2,1)}, u32[]{:S(2)}, u32[]{:S(2)}) collective-permute-start(bf16[256,1664]{1,0:T(8,128)(2,1)} %get-tuple-element.39), channel_id=1, source_target_pairs={{0,1},{1,0},{2,3},{3,2},{4,5},{5,4},{6,7},{7,6},{8,9},{9,8},{10,11... | collective-permute-start | bytes 2555912 | tf_op jit(solution)/shard_map/ppermute | solution.py:470
  133.0 5.1 %collective-permute-start.14 = (bf16[256,1664]{1,0:T(8,128)(2,1)}, bf16[256,1664]{1,0:T(8,128)(2,1)}, u32[]{:S(2)}, u32[]{:S(2)}) collective-permute-start(bf16[256,1664]{1,0:T(8,128)(2,1)} %get-tuple-element.40), channel_id=1, source_target_pairs={{0,1},{1,0},{2,3},{3,2},{4,5},{5,4},{6,7},{7,6},{8,9},{9,8},{10,11... | collective-permute-start | bytes 2555912 | tf_op jit(solution)/shard_map/ppermute | solution.py:470
  133.5 29.2 %collective-permute-start.19 = (bf16[512,1664]{1,0:T(8,128)(2,1)}, bf16[512,1664]{1,0:T(8,128)(2,1)}, u32[]{:S(2)}, u32[]{:S(2)}) collective-permute-start(bf16[512,1664]{1,0:T(8,128)(2,1)} %get-tuple-element.43), channel_id=1, source_target_pairs={{0,1},{1,0},{2,3},{3,2},{4,5},{5,4},{6,7},{7,6},{8,9},{9,8},{10,11... | collective-permute-start | bytes 5111816 | tf_op jit(solution)/shard_map/ppermute | solution.py:470
  133.5 29.2 %collective-permute-start.18 = (bf16[512,1664]{1,0:T(8,128)(2,1)S(1)}, bf16[512,1664]{1,0:T(8,128)(2,1)}, u32[]{:S(2)}, u32[]{:S(2)}) collective-permute-start(bf16[512,1664]{1,0:T(8,128)(2,1)S(1)} %copy-done.5), channel_id=1, source_target_pairs={{0,1},{1,0},{2,3},{3,2},{4,5},{5,4},{6,7},{7,6},{8,9},{9,8},{10,11... | collective-permute-start | bytes 5111816 | tf_op jit(solution)/shard_map/ppermute | solution.py:470
  148.8 44.2 %collective-permute-start.20 = (bf16[2,256,1664]{2,1,0:T(8,128)(2,1)}, bf16[2,256,1664]{2,1,0:T(8,128)(2,1)}, u32[]{:S(2)}, u32[]{:S(2)}) collective-permute-start(bf16[2,256,1664]{2,1,0:T(8,128)(2,1)} %dot_pair.15.refs_5_), channel_id=1, source_target_pairs={{0,2},{1,3},{2,0},{3,1},{4,6},{5,7},{6,4},{7,5},{8,10},{9,11},{10,... | collective-permute-start | bytes 5111816 | tf_op jit(solution)/shard_map/ppermute | solution.py:477
  162.1 18.1 %collective-permute-start.17 = (bf16[256,1664]{1,0:T(8,128)(2,1)}, bf16[256,1664]{1,0:T(8,128)(2,1)S(1)}, u32[]{:S(2)}, u32[]{:S(2)}) collective-permute-start(bf16[256,1664]{1,0:T(8,128)(2,1)} %get-tuple-element.42), channel_id=1, source_target_pairs={{0,1},{1,0},{2,3},{3,2},{4,5},{5,4},{6,7},{7,6},{8,9},{9,8},{10,11... | collective-permute-start | bytes 2555912 | tf_op jit(solution)/shard_map/ppermute | solution.py:470
  162.2 18.1 %collective-permute-start.16 = (bf16[256,1664]{1,0:T(8,128)(2,1)}, bf16[256,1664]{1,0:T(8,128)(2,1)S(1)}, u32[]{:S(2)}, u32[]{:S(2)}) collective-permute-start(bf16[256,1664]{1,0:T(8,128)(2,1)} %get-tuple-element.41.refs_14_), channel_id=1, source_target_pairs={{0,1},{1,0},{2,3},{3,2},{4,5},{5,4},{6,7},{7,6},{8,9},{9,8},{10,11... | collective-permute-start | bytes 2555912 | tf_op jit(solution)/shard_map/ppermute | solution.py:470
  193.0 10.2 %copy-start.1 = (f32[8,2,6656]{2,1,0:T(2,128)S(1)}, f32[8,2,6656]{2,1,0:T(2,128)}, u32[]{:S(2)}) copy-start(f32[8,2,6656]{2,1,0:T(2,128)} %param.14) | copy-start | bytes 1277956
  (9 other events, 21.1 us)
